TPU v7x, 32 devices: a whole 2x2x4 slice. The times are simulated.
32 devices in a mesh: dp: 8 (over y, x, core), ctx: 4 (over z).
Axes of the slice: x: 2, y: 2, z: 4, core: 2. Of those that a mesh axis runs over, the one named last changes fastest.
Arguments:
- inputs: bfloat16 [16, 1024, 1088], P('dp', 'ctx'), may hold values from -6 to 6
- cotangent: bfloat16 [16, 1024, 1088], P('dp', 'ctx'), may hold values from -6 to 6
- w_qkv: bfloat16 [1088, 3264], P('dp', 'ctx'), may hold values from -0.1875 to 0.1875
- w_out: bfloat16 [1088, 1088], P('dp', 'ctx'), may hold values from -0.5 to 0.5
- w_up: bfloat16 [1088, 4352], P('dp', 'ctx'), may hold values from -0.1875 to 0.1875
- w_down: bfloat16 [4352, 1088], P('dp', 'ctx'), may hold values from -0.09375 to 0.09375
- vectors: bfloat16 [8, 1088], P(None, 'ctx'), may hold values from 0.099609375 to 1.8984375
- bias_up: bfloat16 [4352], P('ctx'), may hold values from -3 to 3
- segment_ids: int32 [16, 1024], P('dp'), may hold values from 0 to 7, never falling along the last dimension, each value on 1 to 512 neighbouring positions
- padding: int32 [16, 1024], P('dp'), may hold values 0 or 1
- stretch_order: int32 [8], replicated, may hold values from 0 to 7, each once
Outputs:
- output: bfloat16 [16, 1024, 1088], P('dp', 'ctx')
- input_grad: float32 [16, 1024, 1088], P('dp', 'ctx')
- grad_qkv: float32 [1088, 3264], P('dp', 'ctx')
- grad_out: float32 [1088, 1088], P('dp', 'ctx')
- grad_up: float32 [1088, 4352], P('dp', 'ctx')
- grad_down: float32 [4352, 1088], P('dp', 'ctx')
- grad_vectors: float32 [8, 1088], P(None, 'ctx')
- grad_bias_up: float32 [4352], P('ctx')
- clipped_qkv: bfloat16 [1088, 3264], P('dp', 'ctx')
- clipped_query_bias: bfloat16 [1088], P('ctx')
- head_max: float32 [17], replicated
Inputs may be any that keep to these rules, and one draw needn't show every extreme that they name: A permutation; the device at index c of ctx holds, in this order, the position blocks stretch_order[2 c] and stretch_order[2 c + 1], each 128 positions long, of each of its sequences. `segment_ids`: never falls along positions; a document spans 1 to 512 positions.
All inputs are finite; a program needn't handle non-finite values. No bound on the sum of `padding` on one device may be relied on, other than what follows from the above.
Results may differ from a plain program's by a relative error of at most 0.038.
Values may be sent and summed in bfloat16 or wider, within the bound.
A program may use at most 320 MiB of HBM per device.

v0:
```python
from functools import partial

import jax
import jax.numpy as jnp
from jax import lax
from jax.sharding import PartitionSpec as P

D = 1088
HEADS = 17
HD = 64
LEN = 1024
MB = 2


eps_norm = 1e-05
clip_limit = 5.0
masked_fill = -1e30


def layer_norm(values_in, gain_row, shift_row):
    average = jnp.mean(values_in, axis=-1, keepdims=True)
    centred = values_in - average
    variance = jnp.mean(centred * centred, axis=-1, keepdims=True)
    return centred * lax.rsqrt(variance + eps_norm) * gain_row + shift_row


def to_low(values_in):
    return values_in.astype(jnp.bfloat16)


def product(left, right):
    return jnp.dot(left, right, preferred_element_type=jnp.float32)


def contract_rows(left, right):
    return lax.dot_general(
        left, right, (((0,), (0,)), ((), ())), preferred_element_type=jnp.float32
    )


def contract_cols(left, right):
    return lax.dot_general(
        left, right, (((1,), (1,)), ((), ())), preferred_element_type=jnp.float32
    )


def column_sum(values_in):
    return jnp.sum(values_in.astype(jnp.float32), axis=0)


def gather_weights(w_qkv, w_out, w_up, w_down, vectors, bias_up):
    by_columns = (
        lax.all_gather(w_qkv, "ctx", axis=1, tiled=True),
        lax.all_gather(w_out, "ctx", axis=1, tiled=True),
        lax.all_gather(w_up, "ctx", axis=1, tiled=True),
        lax.all_gather(w_down, "ctx", axis=1, tiled=True),
        lax.all_gather(vectors, "ctx", axis=1, tiled=True),
        lax.all_gather(bias_up, "ctx", axis=0, tiled=True),
    )
    complete = (
        lax.all_gather(by_columns[0], "dp", axis=0, tiled=True),
        lax.all_gather(by_columns[1], "dp", axis=0, tiled=True),
        lax.all_gather(by_columns[2], "dp", axis=0, tiled=True),
        lax.all_gather(by_columns[3], "dp", axis=0, tiled=True),
    )
    return (
        complete[0],
        complete[1],
        complete[2],
        complete[3],
        by_columns[4].astype(jnp.float32),
        by_columns[5].astype(jnp.float32),
    )


def reduce_grads(grad_qkv, grad_out, grad_up, grad_down, grad_vectors, grad_bias):
    by_rows = (
        lax.psum_scatter(
            grad_qkv.astype(jnp.bfloat16), "dp", scatter_dimension=0, tiled=True
        ).astype(jnp.float32),
        lax.psum_scatter(
            grad_out.astype(jnp.bfloat16), "dp", scatter_dimension=0, tiled=True
        ).astype(jnp.float32),
        lax.psum_scatter(
            grad_up.astype(jnp.bfloat16), "dp", scatter_dimension=0, tiled=True
        ).astype(jnp.float32),
        lax.psum_scatter(
            grad_down.astype(jnp.bfloat16), "dp", scatter_dimension=0, tiled=True
        ).astype(jnp.float32),
    )
    by_columns = (
        lax.psum_scatter(
            by_rows[0].astype(jnp.bfloat16), "ctx", scatter_dimension=1, tiled=True
        ).astype(jnp.float32),
        lax.psum_scatter(
            by_rows[1].astype(jnp.bfloat16), "ctx", scatter_dimension=1, tiled=True
        ).astype(jnp.float32),
        lax.psum_scatter(
            by_rows[2].astype(jnp.bfloat16), "ctx", scatter_dimension=1, tiled=True
        ).astype(jnp.float32),
        lax.psum_scatter(
            by_rows[3].astype(jnp.bfloat16), "ctx", scatter_dimension=1, tiled=True
        ).astype(jnp.float32),
        lax.psum_scatter(
            grad_vectors.astype(jnp.bfloat16), "ctx", scatter_dimension=1, tiled=True
        ).astype(jnp.float32),
        lax.psum_scatter(
            grad_bias.astype(jnp.bfloat16), "ctx", scatter_dimension=0, tiled=True
        ).astype(jnp.float32),
    )
    small_sums = lax.psum((by_columns[4], by_columns[5]), "dp")
    return (
        by_columns[0],
        by_columns[1],
        by_columns[2],
        by_columns[3],
        small_sums[0],
        small_sums[1],
    )


def split_heads(values_in):
    return values_in.reshape(values_in.shape[0], HEADS, HD)


def head_scores(queries, key_rows, allowed):
    score_scale = HD ** (-0.5)
    scores = (
        jnp.einsum(
            "qhd,khd->hqk",
            split_heads(queries),
            split_heads(key_rows),
            preferred_element_type=jnp.float32,
        )
        * score_scale
    )
    return jnp.where(allowed[None], scores, masked_fill)


def attend_forward(pieces):
    queries, key_rows, value_rows, allowed = pieces
    masked = head_scores(queries, key_rows, allowed)
    row_top = jnp.max(masked, axis=-1, keepdims=True)
    log_total = row_top + jnp.log(jnp.sum(jnp.exp(masked - row_top), axis=-1, keepdims=True))
    attn_probs = to_low(jnp.exp(masked - log_total))
    attended = jnp.einsum(
        "hqk,khd->qhd", attn_probs, split_heads(value_rows), preferred_element_type=jnp.float32
    )
    return (attended.reshape(queries.shape[0], -1), log_total, jnp.max(masked, axis=(1, 2)))


def score_grads(queries, key_rows, value_rows, allowed, log_total, grad_attended):
    masked = head_scores(queries, key_rows, allowed)
    attn_probs = jnp.exp(masked - log_total)
    grad_probs = jnp.einsum(
        "qhd,khd->hqk",
        split_heads(grad_attended),
        split_heads(value_rows),
        preferred_element_type=jnp.float32,
    )
    return (attn_probs, grad_probs)


def attend_backward(pieces):
    queries, key_rows, value_rows, allowed, log_total, grad_attended = pieces
    score_scale = HD ** (-0.5)
    attn_probs, grad_probs = score_grads(
        queries, key_rows, value_rows, allowed, log_total, grad_attended
    )
    delta_row = jnp.sum(attn_probs * grad_probs, axis=-1, keepdims=True)
    grad_scores = to_low(attn_probs * (grad_probs - delta_row))
    grad_queries = (
        jnp.einsum(
            "hqk,khd->qhd", grad_scores, split_heads(key_rows), preferred_element_type=jnp.float32
        )
        * score_scale
    )
    grad_keys = (
        jnp.einsum(
            "hqk,qhd->khd", grad_scores, split_heads(queries), preferred_element_type=jnp.float32
        )
        * score_scale
    )
    grad_values = jnp.einsum(
        "hqk,qhd->khd",
        to_low(attn_probs),
        split_heads(grad_attended),
        preferred_element_type=jnp.float32,
    )
    return (
        grad_queries.reshape(queries.shape[0], -1),
        grad_keys.reshape(key_rows.shape[0], -1),
        grad_values.reshape(value_rows.shape[0], -1),
    )


def forward_micro(weights, block_in, allowed):
    wide_qkv, wide_out, wide_up, wide_down, vec_rows, bias_row = weights
    block_seqs, query_len = (block_in.shape[0], block_in.shape[1])
    flat_in = block_in.reshape(-1, D).astype(jnp.float32)
    normed = to_low(layer_norm(flat_in, vec_rows[0], vec_rows[1]))
    projected = product(normed, wide_qkv) + jnp.concatenate(
        [vec_rows[2], jnp.zeros((D,), jnp.float32), vec_rows[3]]
    )
    queries = to_low(projected[:, :D]).reshape(block_seqs, query_len, D)
    key_local = to_low(projected[:, D : 2 * D]).reshape(block_seqs, query_len, D)
    value_local = to_low(projected[:, 2 * D :]).reshape(block_seqs, query_len, D)
    key_full, value_full = (
        lax.all_gather(key_local, "ctx", axis=1, tiled=True),
        lax.all_gather(value_local, "ctx", axis=1, tiled=True),
    )
    attended_raw, log_total, head_tops = lax.map(
        attend_forward, (queries, key_full, value_full, allowed)
    )
    attended = to_low(attended_raw.reshape(-1, D))
    residual = flat_in + product(attended, wide_out) + vec_rows[4]
    normed_two = to_low(layer_norm(residual, vec_rows[5], vec_rows[6]))
    up_pre = product(normed_two, wide_up) + bias_row
    hidden = to_low(jax.nn.gelu(up_pre, approximate=True))
    output = residual + product(hidden, wide_down) + vec_rows[7]
    saved = (
        flat_in,
        normed,
        queries,
        key_full,
        value_full,
        key_local,
        value_local,
        allowed,
        log_total,
        attended,
        residual,
        normed_two,
        up_pre,
        hidden,
    )
    return (saved, to_low(output).reshape(block_in.shape), jnp.max(head_tops, axis=0))


def backward_micro(weights, saved, block_cot):
    wide_qkv, wide_out, wide_up, wide_down, vec_rows, bias_row = weights
    (
        flat_in,
        normed,
        queries,
        key_full,
        value_full,
        key_local,
        value_local,
        allowed,
        log_total,
        attended,
        residual,
        normed_two,
        up_pre,
        hidden,
    ) = saved
    grad_mlp = block_cot.reshape(-1, D)
    grad_output = grad_mlp.astype(jnp.float32)
    grad_down = contract_rows(hidden, grad_mlp)
    grad_bias_two = column_sum(grad_mlp)
    grad_hidden = contract_cols(grad_mlp, wide_down)
    unused, gelu_back = jax.vjp(partial(jax.nn.gelu, approximate=True), up_pre)
    grad_pre = to_low(gelu_back(grad_hidden)[0])
    grad_up = contract_rows(normed_two, grad_pre)
    grad_bias_up = column_sum(grad_pre)
    unused, norm_back_two = jax.vjp(layer_norm, residual, vec_rows[5], vec_rows[6])
    back_two = norm_back_two(contract_cols(grad_pre, wide_up))
    grad_residual = grad_output + back_two[0]
    grad_branch = to_low(grad_residual)
    grad_out = contract_rows(attended, grad_branch)
    grad_attended = to_low(contract_cols(grad_branch, wide_out)).reshape(queries.shape)
    grad_queries, key_part, value_part = lax.map(
        attend_backward, (queries, key_full, value_full, allowed, log_total, grad_attended)
    )
    grad_keys, grad_values = (
        lax.psum_scatter(
            key_part.astype(jnp.bfloat16), "ctx", scatter_dimension=1, tiled=True
        ).astype(jnp.float32),
        lax.psum_scatter(
            value_part.astype(jnp.bfloat16), "ctx", scatter_dimension=1, tiled=True
        ).astype(jnp.float32),
    )
    grad_proj = jnp.concatenate(
        [
            to_low(grad_queries).reshape(-1, D),
            to_low(grad_keys).reshape(-1, D),
            to_low(grad_values).reshape(-1, D),
        ],
        axis=1,
    )
    grad_qkv = contract_rows(normed, grad_proj)
    unused, norm_back_one = jax.vjp(layer_norm, flat_in, vec_rows[0], vec_rows[1])
    back_one = norm_back_one(contract_cols(grad_proj, wide_qkv))
    grad_input = grad_residual + back_one[0]
    grad_vectors = jnp.stack(
        [
            back_one[1],
            back_one[2],
            column_sum(grad_proj[:, :D]),
            column_sum(grad_proj[:, 2 * D :]),
            column_sum(grad_branch),
            back_two[1],
            back_two[2],
            grad_bias_two,
        ]
    )
    return (
        (grad_qkv, grad_out, grad_up, grad_down, grad_vectors, grad_bias_up),
        grad_input.reshape(queries.shape),
    )


def shards(
    inputs,
    cotangent,
    w_qkv,
    w_out,
    w_up,
    w_down,
    vectors,
    bias_up,
    segment_ids,
    padding,
    stretch_order,
):
    local_seqs, query_len = (inputs.shape[0], inputs.shape[1])
    seqs_micro = local_seqs // MB
    stretch_len = LEN // stretch_order.shape[0]
    stored = jnp.arange(LEN, dtype=jnp.int32)
    positions = stretch_order[stored // stretch_len] * stretch_len + stored % stretch_len
    query_first = lax.axis_index("ctx") * query_len
    query_pos = lax.dynamic_slice_in_dim(positions, query_first, query_len)
    causal = positions[None, :] <= query_pos[:, None]
    diagonal = positions[None, :] == query_pos[:, None]
    seg_stored = jnp.take(segment_ids, positions, axis=1)
    pad_stored = jnp.take(padding, positions, axis=1)
    seg_query = lax.dynamic_slice_in_dim(seg_stored, query_first, query_len, 1)
    allowed_all = (
        (seg_query[:, :, None] == seg_stored[:, None, :])
        & causal[None]
        & ((pad_stored[:, None, :] == 1) | diagonal[None])
    )
    running = jnp.full((HEADS,), masked_fill, jnp.float32)
    output_blocks = []
    grad_blocks = []
    summed = None
    for micro in range(MB):
        picked = slice(micro * seqs_micro, (micro + 1) * seqs_micro)
        weights = gather_weights(w_qkv, w_out, w_up, w_down, vectors, bias_up)
        saved, out_block, block_top = forward_micro(weights, inputs[picked], allowed_all[picked])
        running = jnp.maximum(running, block_top)
        output_blocks.append(out_block)
        weights = gather_weights(w_qkv, w_out, w_up, w_down, vectors, bias_up)
        fresh, grad_block = backward_micro(weights, saved, cotangent[picked])
        grad_blocks.append(grad_block)
        summed = (
            fresh
            if summed is None
            else tuple((older + newer for older, newer in zip(summed, fresh)))
        )
    summed = reduce_grads(summed[0], summed[1], summed[2], summed[3], summed[4], summed[5])
    global_top = lax.pmax(running, ("dp", "ctx"))
    factor = clip_limit / jnp.maximum(global_top, clip_limit)
    per_column = jnp.repeat(jnp.sqrt(factor), HD)
    column_scale = jnp.concatenate([per_column, per_column, jnp.ones((D,), jnp.float32)])
    cols_here = w_qkv.shape[1]
    local_scale = lax.dynamic_slice_in_dim(
        column_scale, lax.axis_index("ctx") * cols_here, cols_here
    )
    clipped_qkv = (w_qkv.astype(jnp.float32) * local_scale[None, :]).astype(jnp.bfloat16)
    bias_here = vectors.shape[1]
    bias_scale = lax.dynamic_slice_in_dim(per_column, lax.axis_index("ctx") * bias_here, bias_here)
    clipped_bias = (vectors[2].astype(jnp.float32) * bias_scale).astype(jnp.bfloat16)
    return (
        jnp.concatenate(output_blocks, axis=0),
        jnp.concatenate(grad_blocks, axis=0),
        summed[0],
        summed[1],
        summed[2],
        summed[3],
        summed[4],
        summed[5],
        clipped_qkv,
        clipped_bias,
        global_top,
    )


def solution(mesh):
    return jax.shard_map(
        shards,
        mesh=mesh,
        in_specs=(
            P("dp", "ctx", None),
            P("dp", "ctx", None),
            P("dp", "ctx"),
            P("dp", "ctx"),
            P("dp", "ctx"),
            P("dp", "ctx"),
            P(None, "ctx"),
            P("ctx"),
            P("dp", None),
            P("dp", None),
            P(),
        ),
        out_specs=(
            P("dp", "ctx", None),
            P("dp", "ctx", None),
            P("dp", "ctx"),
            P("dp", "ctx"),
            P("dp", "ctx"),
            P("dp", "ctx"),
            P(None, "ctx"),
            P("ctx"),
            P("dp", "ctx"),
            P("ctx"),
            P(),
        ),
        check_vma=False,
    )
```

profile of v0, /device:TPU:0, one launch (start us, length us, event | category | flops | bytes accessed | tf_op | source)
XLA Modules:
  0.0 1199.9 jit_solution(2660815829268363257)
XLA Ops:
  7.2 23.6 %all-gather.5 = bf16[4,816,136]{1,2,0:T(8,128)(2,1)S(1)} all-gather(bf16[1,816,136]{1,2,0:T(8,128)(2,1)} %bitcast.288), channel_id=1, replica_groups=mesh['dp'=8,'ctx'=4] {'ctx'}, dimensions={0}, use_global_device_ids=true | all-gather | bytes 1109760 | tf_op jit(solution)/shard_map/all_gather | solution.py:53
  34.4 13.1 %all-gather.4 = bf16[4,272,8]{1,2,0:T(8,128)(2,1)S(1)} all-gather(bf16[1,272,8]{1,2,0:T(8,128)(2,1)S(1)} %bitcast.302), channel_id=1, replica_groups=mesh['dp'=8,'ctx'=4] {'ctx'}, dimensions={0}, use_global_device_ids=true | all-gather | bytes 21760 | tf_op jit(solution)/shard_map/all_gather | solution.py:57
  48.9 33.4 %all-gather.19.cloned.1.call-done = bf16[1088,3264]{1,0:T(8,128)(2,1)} async-done(((bf16[136,3264]{1,0:T(8,128)(2,1)}), bf16[1088,3264]{1,0:T(8,128)(2,1)}) %all-gather.19.cloned.1.call-update) | async-done | bytes 7102480 | tf_op jit(solution)/shard_map/all_gather | solution.py:61
  82.4 6.8 fusion.7
  91.0 20.2 %all-gather.6 = bf16[4,272,136]{1,2,0:T(8,128)(2,1)S(1)} all-gather(bf16[1,272,136]{1,2,0:T(8,128)(2,1)S(1)} %bitcast.299), channel_id=1, replica_groups=mesh['dp'=8,'ctx'=4] {'ctx'}, dimensions={0}, use_global_device_ids=true | all-gather | bytes 369920 | tf_op jit(solution)/shard_map/all_gather | solution.py:54
  112.5 6.8 fusion.6
  125.6 31.5 %all-gather.25.cloned.1.call-done = bf16[544,1088]{0,1:T(8,128)(2,1)} async-done(((bf16[544,272]{0,1:T(8,128)(2,1)}), bf16[544,1088]{0,1:T(8,128)(2,1)}) %all-gather.25.cloned.1.call-update) | async-done | bytes 1183760 | tf_op jit(solution)/shard_map/all_gather | solution.py:56
  160.7 4.5 compare_select_fusion.1
  165.9 2.8 gather_fusion
  174.1 17.9 %all-reduce = bf16[4352]{0:T(1024)(128)(2,1)S(1)} all-reduce(bf16[4352]{0:T(1024)(128)(2,1)S(1)} %dynamic-update-slice), channel_id=1, replica_groups=mesh['dp'=8,'ctx'=4] {'ctx'}, use_global_device_ids=true, to_apply=%add | all-reduce | flops 4352 | bytes 17408
  193.1 13.9 %all-gather.35.cloned.1.call-done = bf16[1024,1088]{0,1:T(8,128)(2,1)} async-done(((bf16[256,1088]{0,1:T(8,128)(2,1)}), bf16[1024,1088]{0,1:T(8,128)(2,1)}) %all-gather.35.cloned.1.call-update) | async-done | bytes 2228240 | tf_op jit(solution)/shard_map/all_gather | solution.py:209
  207.0 9.7 fusion.127
  216.7 9.0 exponential_reduce_fusion
  225.7 29.9 %all-gather.33.cloned.1.call-done = bf16[1024,1088]{0,1:T(8,128)(2,1)} async-done(((bf16[256,1088]{0,1:T(8,128)(2,1)}), bf16[1024,1088]{0,1:T(8,128)(2,1)}) %all-gather.33.cloned.1.call-update) | async-done | bytes 2228240 | tf_op jit(solution)/shard_map/all_gather | solution.py:210
  255.6 9.2 fusion.57
  264.8 21.0 %all-gather.21.cloned.1.call-done = bf16[1088,1088]{1,0:T(8,128)(2,1)} async-done(((bf16[136,1088]{1,0:T(8,128)(2,1)}), bf16[1088,1088]{1,0:T(8,128)(2,1)}) %all-gather.21.cloned.1.call-update) | async-done | bytes 2367504 | tf_op jit(solution)/shard_map/all_gather | solution.py:62
  285.8 3.2 fusion.128
  289.1 47.2 %all-gather.31.cloned.1.call-done = bf16[1024,1088]{0,1:T(8,128)(2,1)} async-done(((bf16[256,1088]{0,1:T(8,128)(2,1)}), bf16[1024,1088]{0,1:T(8,128)(2,1)}) %all-gather.31.cloned.1.call-update) | async-done | bytes 2228240 | tf_op jit(solution)/shard_map/all_gather | solution.py:209
  336.3 21.0 %fusion.129 = (f32[17,256]{1,0:T(8,128)S(1)}, f32[17,256,1024]{2,1,0:T(8,128)}) fusion(bf16[256,17,64]{0,2,1:T(8,128)(2,1)S(1)} %bitcast.263, bf16[1024,17,64]{0,2,1:T(8,128)(2,1)} %bitcast.257, pred[256,1024]{1,0:T(8,128)(4,1)S(1)} %get-tuple-element.233), kind=kOutput, calls=%fused_computation.235 | convolution fusion | flops 583790336 | bytes 20890624 | tf_op jit(solution)/shard_map/while/body/eval_jaxpr/qhd,khd->hqk/dot_general | solution.py:129
  357.4 9.0 exponential_reduce_fusion.1
  366.4 18.2 %all-gather.29.cloned.1.call-done = bf16[1024,1088]{0,1:T(8,128)(2,1)} async-done(((bf16[256,1088]{0,1:T(8,128)(2,1)}), bf16[1024,1088]{0,1:T(8,128)(2,1)}) %all-gather.29.cloned.1.call-update) | async-done | bytes 2228240 | tf_op jit(solution)/shard_map/all_gather | solution.py:210
  384.6 8.8 fusion.54
  395.9 47.8 %all-gather.23.cloned.1.call-done = bf16[1088,4352]{1,0:T(8,128)(2,1)} async-done(((bf16[136,4352]{1,0:T(8,128)(2,1)}), bf16[1088,4352]{1,0:T(8,128)(2,1)}) %all-gather.23.cloned.1.call-update) | async-done | bytes 9469968 | tf_op jit(solution)/shard_map/all_gather | solution.py:63
  443.7 9.2 convolution_add_fusion.4
  452.8 4.9 convolution_add_fusion.5
  457.8 49.5 %all-gather.27.cloned.1.call-done = bf16[4352,1088]{1,0:T(8,128)(2,1)} async-done(((bf16[544,1088]{1,0:T(8,128)(2,1)}), bf16[4352,1088]{1,0:T(8,128)(2,1)}) %all-gather.27.cloned.1.call-update) | async-done | bytes 9469968 | tf_op jit(solution)/shard_map/all_gather | solution.py:64
  507.3 8.0 convert_reduce_fusion
  515.3 8.2 fusion.131
  524.4 6.3 convert_reduce_fusion.1
  530.7 8.5 multiply_reduce_fusion.3
  544.6 5.5 fusion.38
  551.2 13.8 %fusion.116 = (f32[17]{0:T(128)}, f32[17,256]{1,0:T(8,128)S(1)}, f32[17,256,1024]{2,1,0:T(8,128)}) fusion(f32[17,256,1024]{2,1,0:T(8,128)} %get-tuple-element.257, f32[17,256]{1,0:T(8,128)S(1)} %log_add_fusion.1, bf16[256,17,64]{0,2,1:T(8,128)(2,1)S(1)} %bitcast.274, bf16[1024,17,64]{0,2,1:T(8,128)(2,1)} %bitcast.253), kind=kOutput, calls=%fused_computation.225 | convolution fusion | flops 588246784 | bytes 38471748 | tf_op jit(solution)/shard_map/while/body/eval_jaxpr/qhd,khd->hqk/dot_general | solution.py:155
  564.9 12.7 %multiply_convert_fusion.1 = bf16[17,256,1024]{2,1,0:T(8,128)(2,1)S(1)} fusion(f32[17,256,1024]{2,1,0:T(8,128)} %get-tuple-element.261, f32[17,256,1024]{2,1,0:T(8,128)} %get-tuple-element.257, f32[17,256]{1,0:T(8,128)S(1)} %get-tuple-element.176, f32[17,256]{1,0:T(8,128)S(1)} %log_add_fusion.1), kind=kLoop, calls=%fused_computation.9 | loop fusion | flops 17825792 | bytes 44599296 | tf_op jit(solution)/shard_map/while/body/eval_jaxpr/convert_element_type | solution.py:28
  577.7 3.5 multiply_convert_fusion.3
  585.5 9.6 fusion.41
  595.1 12.9 %fusion.117 = (f32[17]{0:T(128)S(1)}, f32[17,256]{1,0:T(8,128)S(1)}, f32[17,256,1024]{2,1,0:T(8,128)}) fusion(f32[17,256,1024]{2,1,0:T(8,128)} %get-tuple-element.253, f32[17,256]{1,0:T(8,128)S(1)} %log_add_fusion, bf16[256,17,64]{0,2,1:T(8,128)(2,1)S(1)} %bitcast.272, bf16[1024,17,64]{0,2,1:T(8,128)(2,1)} %bitcast.251), kind=kOutput, calls=%fused_computation.226 | convolution fusion | flops 588246784 | bytes 38471748 | tf_op jit(solution)/shard_map/while/body/eval_jaxpr/qhd,khd->hqk/dot_general | solution.py:155
  608.1 12.6 %multiply_convert_fusion = bf16[17,256,1024]{2,1,0:T(8,128)(2,1)S(1)} fusion(f32[17,256,1024]{2,1,0:T(8,128)} %get-tuple-element.262, f32[17,256,1024]{2,1,0:T(8,128)} %get-tuple-element.253, f32[17,256]{1,0:T(8,128)S(1)} %get-tuple-element.178, f32[17,256]{1,0:T(8,128)S(1)} %log_add_fusion), kind=kLoop, calls=%fused_computation.7 | loop fusion | flops 17825792 | bytes 44599296 | tf_op jit(solution)/shard_map/while/body/eval_jaxpr/convert_element_type | solution.py:28
  620.7 3.5 multiply_convert_fusion.2
  631.5 9.9 fusion.115
  641.4 11.0 fusion.1
  653.6 13.0 %fusion.86 = f32[4352,1088]{1,0:T(8,128)} fusion(bf16[2,256,1088]{1,2,0:T(8,128)(2,1)S(1)} %copy-done.17, f32[256,4352]{1,0:T(8,128)} %convolution_add_fusion.5), kind=kOutput, calls=%fused_computation.145 | convolution fusion | flops 2434334720 | bytes 23953408 | tf_op jit(solution)/shard_map/dot_general | solution.py:36
  666.6 13.6 %fusion = bf16[4352,1088]{1,0:T(8,128)(2,1)} fusion(f32[4352,1088]{1,0:T(8,128)} %fusion.86, bf16[2,256,1088]{1,2,0:T(8,128)(2,1)S(1)} %copy-done.17, f32[256,4352]{1,0:T(8,128)} %convolution_add_fusion.4), kind=kOutput, calls=%fused_computation.5 | convolution fusion | flops 2443804672 | bytes 33423360 | tf_op jit(solution)/shard_map/dot_general | solution.py:36
  680.5 8.0 convert_reduce_fusion.8
  688.6 6.6 convert_reduce_fusion.11
  695.3 8.6 fusion.79
  703.9 35.4 %reduce-scatter.30.cloned.1.call-done = bf16[1,256,1088]{1,2,0:T(8,128)(2,1)} async-done(((bf16[1,1024,1088]{1,2,0:T(8,128)(2,1)}), bf16[1,256,1088]{1,2,0:T(8,128)(2,1)}) %reduce-scatter.30.cloned.1.call-update) | async-done | bytes 557072 | tf_op jit(solution)/shard_map/reduce_scatter | solution.py:277
  739.3 8.8 fusion.2
  749.0 36.1 %reduce-scatter.50.cloned.1.call-done = bf16[136,1088]{1,0:T(8,128)(2,1)} async-done(((bf16[1088,1088]{1,0:T(8,128)(2,1)}), bf16[136,1088]{1,0:T(8,128)(2,1)}) %reduce-scatter.50.cloned.1.call-update) | async-done | bytes 295952
  787.6 5.6 fusion.78
  793.3 5.9 fusion.73
  802.1 67.2 %reduce-scatter.36.cloned.1.call-done = bf16[136,4352]{1,0:T(8,128)(2,1)} async-done(((bf16[1088,4352]{1,0:T(8,128)(2,1)}), bf16[136,4352]{1,0:T(8,128)(2,1)}) %reduce-scatter.36.cloned.1.call-update) | async-done | bytes 1183760 | tf_op jit(solution)/shard_map/reduce_scatter | solution.py:84
  869.2 3.6 copy.75
  874.3 39.6 %pmax.7 = f32[17]{0:T(128)S(1)} all-reduce(f32[17]{0:T(128)S(1)} %maximum_maximum_fusion), channel_id=1, replica_groups=mesh['dp'=8,'ctx'=4] {'dp','ctx'}, use_global_device_ids=true, to_apply=%region_58.60 | all-reduce | flops 17 | bytes 136 | tf_op jit(solution)/shard_map/pmax | solution.py:363
  915.0 37.5 %reduce-scatter.38.cloned.1.call-done = bf16[544,1088]{1,0:T(8,128)(2,1)} async-done(((bf16[4352,1088]{1,0:T(8,128)(2,1)}), bf16[544,1088]{1,0:T(8,128)(2,1)}) %reduce-scatter.38.cloned.1.call-update) | async-done | bytes 1183760 | tf_op jit(solution)/shard_map/reduce_scatter | solution.py:87
  955.3 9.5 fusion.29
  964.9 10.8 fusion.28
  976.8 49.6 %reduce-scatter.34.cloned.1.call-done = bf16[136,3264]{1,0:T(8,128)(2,1)} async-done(((bf16[1088,3264]{1,0:T(8,128)(2,1)}), bf16[136,3264]{1,0:T(8,128)(2,1)}) %reduce-scatter.34.cloned.1.call-update) | async-done | bytes 887824 | tf_op jit(solution)/shard_map/reduce_scatter | solution.py:78
  1029.6 18.7 %all-reduce.2 = bf16[4352]{0:T(1024)(128)(2,1)S(1)} all-reduce(bf16[4352]{0:T(1024)(128)(2,1)S(1)} %add_convert_fusion.3), channel_id=19, replica_groups=mesh['dp'=8,'ctx'=4] {'ctx'}, use_global_device_ids=true, to_apply=%region_54.56.clone | all-reduce | flops 4352 | bytes 17408
  1052.8 2.8 add_bitcast_fusion.1
  1057.1 15.1 %reduce-scatter.48.cloned.1.call-done = bf16[272,8]{1,0:T(8,128)(2,1)} async-done(((bf16[1088,8]{1,0:T(8,128)(2,1)}), bf16[272,8]{1,0:T(8,128)(2,1)}) %reduce-scatter.48.cloned.1.call-update) | async-done | bytes 4368
  1073.2 23.8 %all-reduce.3 = (f32[8,272]{1,0:T(8,128)}, f32[1088]{0:T(1024)}) all-reduce(bf16[8,272]{1,0:T(8,128)(2,1)S(1)} %copy.80, f32[1088]{0:T(1024)S(1)} %dynamic-slice_convert_fusion), channel_id=1, replica_groups=mesh['dp'=8,'ctx'=4] {'dp'}, use_global_device_ids=true, to_apply=%region_51.53 | all-reduce | flops 3264 | bytes 21760 | tf_op jit(solution)/shard_map/psum | solution.py:111
  1096.9 21.8 %reduce-scatter.44.cloned.1.call-done = bf16[1088,136]{1,0:T(8,128)(2,1)} async-done(((bf16[4352,136]{1,0:T(8,128)(2,1)}), bf16[1088,136]{1,0:T(8,128)(2,1)}) %reduce-scatter.44.cloned.1.call-update) | async-done | bytes 295952
  1120.9 32.3 %reduce-scatter.46.cloned.1.call-done = bf16[272,544]{1,0:T(8,128)(2,1)} async-done(((bf16[1088,544]{1,0:T(8,128)(2,1)}), bf16[272,544]{1,0:T(8,128)(2,1)}) %reduce-scatter.46.cloned.1.call-update) | async-done | bytes 295952
  1155.4 35.8 %reduce-scatter.40.cloned.1.call-done = bf16[816,136]{1,0:T(8,128)(2,1)} async-done(((bf16[3264,136]{1,0:T(8,128)(2,1)}), bf16[816,136]{1,0:T(8,128)(2,1)}) %reduce-scatter.40.cloned.1.call-update) | async-done | bytes 221968
  (334 shorter events, 75.4 us)
Async XLA Ops:
  7.2 75.2 %all-gather.19.cloned.1.call-start = ((), (), s32[]{:S(2)}) async-start(), calls=%async_computation.13 | async-start | bytes 8146944 | tf_op jit(solution)/shard_map/all_gather | solution.py:61
  31.2 17.1 %copy-start.3 = (bf16[2,256,1088]{1,2,0:T(8,128)(2,1)S(1)}, bf16[2,256,1088]{1,2,0:T(8,128)(2,1)}, u32[]{:S(2)}) copy-start(bf16[2,256,1088]{1,2,0:T(8,128)(2,1)} %param.13) | copy-start | bytes 3342340
  32.9 88.9 %all-gather.37.cloned.1.call-start = ((), (), s32[]{:S(2)}) async-start(), calls=%async_computation.29 | async-start | bytes 1566720 | tf_op jit(solution)/shard_map/all_gather | solution.py:55
  33.6 123.5 %all-gather.25.cloned.1.call-start = ((), (), s32[]{:S(2)}) async-start(), calls=%async_computation.16 | async-start | bytes 1740800 | tf_op jit(solution)/shard_map/all_gather | solution.py:56
  34.4 172.6 %all-gather.35.cloned.1.call-start = ((), (), s32[]{:S(2)}) async-start(), calls=%async_computation.28 | async-start | bytes 2785280 | tf_op jit(solution)/shard_map/all_gather | solution.py:209
  48.3 64.2 %copy-start.37 = (f32[1088]{0:T(1024)}, f32[1088]{0:T(1024)S(1)}, u32[]{:S(2)}) copy-start(f32[1088]{0:T(1024)S(1)} %get-tuple-element.208) | copy-start | bytes 13060
  48.3 64.2 %copy-start.39 = (f32[1088]{0:T(1024)}, f32[1088]{0:T(1024)S(1)}, u32[]{:S(2)}) copy-start(f32[1088]{0:T(1024)S(1)} %get-tuple-element.207) | copy-start | bytes 13060
  48.6 40.6 %copy-start.46 = (f32[256]{0:T(256)}, f32[256]{0:T(256)S(1)}, u32[]{:S(2)}) copy-start(f32[256]{0:T(256)S(1)} %get-tuple-element.272) | copy-start | bytes 3076
  48.6 63.9 %copy-start.42 = (f32[256]{0:T(256)}, f32[256]{0:T(256)S(1)}, u32[]{:S(2)}) copy-start(f32[256]{0:T(256)S(1)} %get-tuple-element.273) | copy-start | bytes 3076
  48.9 40.3 %copy-start.58 = (f32[256]{0:T(256)}, f32[256]{0:T(256)S(1)}, u32[]{:S(2)}) copy-start(f32[256]{0:T(256)S(1)} %get-tuple-element.198) | copy-start | bytes 3076
  48.9 63.5 %copy-start.60 = (f32[256]{0:T(256)}, f32[256]{0:T(256)S(1)}, u32[]{:S(2)}) copy-start(f32[256]{0:T(256)S(1)} %get-tuple-element.197) | copy-start | bytes 3076
  48.9 40.3 %copy-start.53 = (f32[256]{0:T(256)}, f32[256]{0:T(256)S(1)}, u32[]{:S(2)}) copy-start(f32[256]{0:T(256)S(1)} %fusion.105) | copy-start | bytes 3076
  90.3 116.7 %copy-start.19 = (bf16[256,1088]{0,1:T(8,128)(2,1)}, bf16[256,1088]{0,1:T(8,128)(2,1)S(1)}, u32[]{:S(2)}) copy-start(bf16[256,1088]{0,1:T(8,128)(2,1)S(1)} %get-tuple-element.227) | copy-start | bytes 1671172
  90.3 165.2 %all-gather.33.cloned.1.call-start = ((), (), s32[]{:S(2)}) async-start(), calls=%async_computation.27 | async-start | bytes 2785280 | tf_op jit(solution)/shard_map/all_gather | solution.py:210
  90.9 194.8 %all-gather.21.cloned.1.call-start = ((), (), s32[]{:S(2)}) async-start(), calls=%async_computation.14 | async-start | bytes 2820096 | tf_op jit(solution)/shard_map/all_gather | solution.py:62
  112.4 224.0 %all-gather.31.cloned.1.call-start = ((), (), s32[]{:S(2)}) async-start(), calls=%async_computation.26 | async-start | bytes 2785280 | tf_op jit(solution)/shard_map/all_gather | solution.py:209
  120.6 264.0 %all-gather.29.cloned.1.call-start = ((), (), s32[]{:S(2)}) async-start(), calls=%async_computation.25 | async-start | bytes 2785280 | tf_op jit(solution)/shard_map/all_gather | solution.py:210
  121.3 322.3 %all-gather.23.cloned.1.call-start = ((), (), s32[]{:S(2)}) async-start(), calls=%async_computation.15 | async-start | bytes 10653696 | tf_op jit(solution)/shard_map/all_gather | solution.py:63
  125.6 34.2 %copy-start.66 = (s32[2,1024]{1,0:T(2,128)S(1)}, s32[2,1024]{1,0:T(2,128)}, u32[]{:S(2)}) copy-start(s32[2,1024]{1,0:T(2,128)} %param.21) | copy-start | bytes 24580
  125.6 34.5 %copy-start.52 = (s32[8]{0:T(128)S(1)}, s32[8]{0:T(128)}, u32[]{:S(2)}) copy-start(s32[8]{0:T(128)} %param.23) | copy-start | bytes 100
  125.6 381.7 %all-gather.27.cloned.1.call-start = ((), (), s32[]{:S(2)}) async-start(), calls=%async_computation.17 | async-start | bytes 11280384 | tf_op jit(solution)/shard_map/all_gather | solution.py:64
  159.7 9.6 copy-start.67
  159.7 12.9 %copy-start.74 = (u32[32]{0:T(128)S(1)}, u32[32]{0:T(128)}, u32[]{:S(2)}) copy-start(u32[32]{0:T(128)} %constant.218) | copy-start | bytes 388
  159.7 14.1 %copy-start.73 = (bf16[1088]{0:T(1024)(128)(2,1)S(1)}, bf16[1088]{0:T(1024)(128)(2,1)}, u32[]{:S(2)}) copy-start(bf16[1088]{0:T(1024)(128)(2,1)} %param.20) | copy-start | bytes 6532
  159.7 535.4 %reduce-scatter.28.cloned.1.call-start = ((), (), s32[]{:S(2)}) async-start(), calls=%async_computation.19 | async-start | bytes 2785280 | tf_op jit(solution)/shard_map/reduce_scatter | solution.py:280
  285.8 50.6 %copy-start.21 = (bf16[256,1088]{0,1:T(8,128)(2,1)S(1)}, bf16[256,1088]{0,1:T(8,128)(2,1)}, u32[]{:S(2)}) copy-start(bf16[256,1088]{0,1:T(8,128)(2,1)} %get-tuple-element.224) | copy-start | bytes 1671172
  384.6 8.8 copy-start.77
  443.7 9.2 copy-start.2
  443.7 9.2 copy-start.6
  452.8 54.5 %copy-start.15 = (bf16[2,256,1088]{1,2,0:T(8,128)(2,1)S(1)}, bf16[2,256,1088]{1,2,0:T(8,128)(2,1)}, u32[]{:S(2)}) copy-start(bf16[2,256,1088]{1,2,0:T(8,128)(2,1)} %param.14) | copy-start | bytes 3342340
  515.3 8.2 copy-start.10
  515.3 9.1 copy-start.76
  530.7 8.5 copy-start.34
  530.7 13.9 %slice-start = ((s8[17825792]{0:T(1024)(128)(4,1)}), s8[4194304]{0:T(1024)(128)(4,1)S(1)}, s32[]{:S(2)}) async-start(s8[17825792]{0:T(1024)(128)(4,1)} %bitcast.246), calls=%async_computation.36 | async-start | bytes 8388608
  530.7 13.9 %slice-start.1 = ((s8[17825792]{0:T(1024)(128)(4,1)}), s8[4194304]{0:T(1024)(128)(4,1)S(1)}, s32[]{:S(2)}) async-start(s8[17825792]{0:T(1024)(128)(4,1)} %bitcast.246), calls=%async_computation.37 | async-start | bytes 8388608
  530.7 13.9 %slice-start.2 = ((s8[17825792]{0:T(1024)(128)(4,1)}), s8[4194304]{0:T(1024)(128)(4,1)S(1)}, s32[]{:S(2)}) async-start(s8[17825792]{0:T(1024)(128)(4,1)} %bitcast.246), calls=%async_computation.38 | async-start | bytes 8388608
  530.7 13.9 %slice-start.3 = ((s8[17825792]{0:T(1024)(128)(4,1)}), s8[4194304]{0:T(1024)(128)(4,1)S(1)}, s32[]{:S(2)}) async-start(s8[17825792]{0:T(1024)(128)(4,1)} %bitcast.246), calls=%async_computation.39 | async-start | bytes 8388608
  550.1 145.1 %reduce-scatter.26.cloned.1.call-start = ((), (), s32[]{:S(2)}) async-start(), calls=%async_computation.18 | async-start | bytes 2785280 | tf_op jit(solution)/shard_map/reduce_scatter | solution.py:277
  564.9 12.7 %copy-start.22 = (bf16[256,1088]{0,1:T(8,128)(2,1)S(1)}, bf16[256,1088]{0,1:T(8,128)(2,1)}, u32[]{:S(2)}) copy-start(bf16[256,1088]{0,1:T(8,128)(2,1)} %get-tuple-element.224) | copy-start | bytes 1671172
  581.8 122.0 %reduce-scatter.32.cloned.1.call-start = ((), (), s32[]{:S(2)}) async-start(), calls=%async_computation.21 | async-start | bytes 2785280 | tf_op jit(solution)/shard_map/reduce_scatter | solution.py:280
  595.1 144.2 %reduce-scatter.30.cloned.1.call-start = ((), (), s32[]{:S(2)}) async-start(), calls=%async_computation.20 | async-start | bytes 2785280 | tf_op jit(solution)/shard_map/reduce_scatter | solution.py:277
  608.1 12.7 %copy-start.20 = (bf16[256,1088]{0,1:T(8,128)(2,1)S(1)}, bf16[256,1088]{0,1:T(8,128)(2,1)}, u32[]{:S(2)}) copy-start(bf16[256,1088]{0,1:T(8,128)(2,1)} %copy-done.19) | copy-start | bytes 1671172
  624.8 160.2 %reduce-scatter.50.cloned.1.call-start = ((), (), s32[]{:S(2)}) async-start(), calls=%async_computation.35 | async-start | bytes 2820096
  630.3 238.9 %reduce-scatter.36.cloned.1.call-start = ((), (), s32[]{:S(2)}) async-start(), calls=%async_computation.23 | async-start | bytes 10653696 | tf_op jit(solution)/shard_map/reduce_scatter | solution.py:84
  652.4 300.1 %reduce-scatter.38.cloned.1.call-start = ((), (), s32[]{:S(2)}) async-start(), calls=%async_computation.24 | async-start | bytes 11280384 | tf_op jit(solution)/shard_map/reduce_scatter | solution.py:87
  680.2 346.2 %reduce-scatter.34.cloned.1.call-start = ((), (), s32[]{:S(2)}) async-start(), calls=%async_computation.22 | async-start | bytes 8146944 | tf_op jit(solution)/shard_map/reduce_scatter | solution.py:78
  695.2 44.0 %copy-start.47 = (f32[256]{0:T(256)S(1)}, f32[256]{0:T(256)}, u32[]{:S(2)}) copy-start(f32[256]{0:T(256)} %copy-done.46) | copy-start | bytes 3076
  695.2 44.0 %copy-start.54 = (f32[256]{0:T(256)S(1)}, f32[256]{0:T(256)}, u32[]{:S(2)}) copy-start(f32[256]{0:T(256)} %copy-done.53) | copy-start | bytes 3076
  748.1 302.8 %reduce-scatter.42.cloned.1.call-start = ((), (), s32[]{:S(2)}) async-start(), calls=%async_computation.31 | async-start | bytes 696320
  787.1 285.1 %reduce-scatter.48.cloned.1.call-start = ((), (), s32[]{:S(2)}) async-start(), calls=%async_computation.34 | async-start | bytes 348160
  802.0 72.3 %copy-start.75 = (f32[17]{0:T(128)S(1)}, f32[17]{0:T(128)}, u32[]{:S(2)}) copy-start(f32[17]{0:T(128)} %get-tuple-element.175) | copy-start | bytes 208
  802.0 112.3 %copy-start.55 = (f32[4352]{0:T(1024)S(1)}, f32[4352]{0:T(1024)}, u32[]{:S(2)}) copy-start(f32[4352]{0:T(1024)} %get-tuple-element.270) | copy-start | bytes 52228
  802.0 112.2 %copy-start.56 = (f32[4352]{0:T(1024)S(1)}, f32[4352]{0:T(1024)}, u32[]{:S(2)}) copy-start(f32[4352]{0:T(1024)} %get-tuple-element.268) | copy-start | bytes 52228
  802.0 112.3 %copy-start.35 = (bf16[136,816]{1,0:T(8,128)(2,1)S(1)}, bf16[136,816]{1,0:T(8,128)(2,1)}, u32[]{:S(2)}) copy-start(bf16[136,816]{1,0:T(8,128)(2,1)} %param.15) | copy-start | bytes 665860
  802.0 316.7 %reduce-scatter.44.cloned.1.call-start = ((), (), s32[]{:S(2)}) async-start(), calls=%async_computation.32 | async-start | bytes 2785280
  872.9 280.3 %reduce-scatter.46.cloned.1.call-start = ((), (), s32[]{:S(2)}) async-start(), calls=%async_computation.33 | async-start | bytes 1740800
  913.9 41.1 %copy-start.79 = (f32[17]{0:T(128)}, f32[17]{0:T(128)S(1)}, u32[]{:S(2)}) copy-start(f32[17]{0:T(128)S(1)} %pmax.7) | copy-start | bytes 208
  914.3 41.0 %copy-start.68 = (f32[1088]{0:T(1024)S(1)}, f32[1088]{0:T(1024)}, u32[]{:S(2)}) copy-start(f32[1088]{0:T(1024)} %get-tuple-element.202) | copy-start | bytes 13060
  955.1 236.1 %reduce-scatter.40.cloned.1.call-start = ((), (), s32[]{:S(2)}) async-start(), calls=%async_computation.30 | async-start | bytes 2088960
  955.3 9.6 copy-start.9
  976.8 76.0 %copy-start.12 = (f32[256,1088]{0,1:T(8,128)S(1)}, f32[256,1088]{0,1:T(8,128)}, u32[]{:S(2)}) copy-start(f32[256,1088]{0,1:T(8,128)} %copy-done.11) | copy-start | bytes 3342340
  976.8 76.0 %copy-start.14 = (f32[256,1088]{0,1:T(8,128)S(1)}, f32[256,1088]{0,1:T(8,128)}, u32[]{:S(2)}) copy-start(f32[256,1088]{0,1:T(8,128)} %copy-done.13) | copy-start | bytes 3342340
  976.8 76.0 %copy-start.63 = (f32[256]{0:T(256)S(1)}, f32[256]{0:T(256)}, u32[]{:S(2)}) copy-start(f32[256]{0:T(256)} %copy-done.62) | copy-start | bytes 3076
  976.8 76.0 %copy-start.65 = (f32[256]{0:T(256)S(1)}, f32[256]{0:T(256)}, u32[]{:S(2)}) copy-start(f32[256]{0:T(256)} %copy-done.64) | copy-start | bytes 3076
  (44 other events, 146.8 us)
Sparse Core Ops, SparseCore 0:
  33.0 49.3 all-gather.18
  83.9 37.8 all-gather.36
  123.4 33.7 all-gather.24
  159.1 47.8 all-gather.34
  209.0 46.5 all-gather.32
  257.9 27.8 all-gather.20
  287.9 48.3 all-gather.30
  337.9 46.6 all-gather.28
  386.5 57.1 all-gather.22
  446.0 61.3 all-gather.26
  550.3 45.9 reduce-scatter.27
  598.5 45.3 reduce-scatter.25
  646.2 45.4 reduce-scatter.31
  693.8 45.4 reduce-scatter.29
  742.5 42.4 reduce-scatter.49
  788.4 80.7 reduce-scatter.35
  872.7 79.7 reduce-scatter.37
  956.3 69.9 reduce-scatter.33
  1029.3 21.6 reduce-scatter.41
  1053.7 18.4 reduce-scatter.47
  1074.5 44.1 reduce-scatter.43
  1121.1 32.0 reduce-scatter.45
  1155.5 35.6 reduce-scatter.39
where the time goes:
time: 1210 us; the launch traced here: 1200 us
  waiting for transfers between devices  629 us (52%)
  matrix products  281 us (23%)
  blocking collectives  157 us (13%)
  other arithmetic  65 us (5%)
  local copies, waits for them, and re-layouts  49.3 us (4%)
  between operations  16.8 us (1%)
    unnamed x29, waiting for transfers between devices  147 us
    dot_general x8, matrix products, contract_rows(): lax.dot_general(left, right, (((0,), (0,)), ((), ())), preferred_element_...  69.2 us
    reduce_scatter x1, waiting for transfers between devices, reduce_grads(): lax.psum_scatter(grad_up.astype(jnp.bfloat16), 'dp', scatter_dimension=0,...  67.2 us
    all_gather x2, waiting for transfers between devices, forward_micro(): lax.all_gather(key_local, 'ctx', axis=1, tiled=True)  61.1 us
    dot_general x8, matrix products, product(): return jnp.dot(left, right, preferred_element_type=jnp.float32)  52.5 us
    reduce_scatter x1, waiting for transfers between devices, reduce_grads(): lax.psum_scatter(grad_qkv.astype(jnp.bfloat16), 'dp', scatter_dimension=0...  49.6 us
    all_gather x1, waiting for transfers between devices, gather_weights(): lax.all_gather(by_columns[3], 'dp', axis=0, tiled=True)  49.5 us
    all_gather x2, waiting for transfers between devices, forward_micro(): lax.all_gather(value_local, 'ctx', axis=1, tiled=True)  48 us
  transfers between devices with their start and end apart: 23, of which 20 were waited for; matrix products, arithmetic and copies ran while one was open for 28% of the time, Pallas kernels for 0%

commit v1 on v0

v1 whole, which is shorter than its diff:
```python
from functools import partial

import jax
import jax.numpy as jnp
from jax import lax
from jax.experimental import pallas as pl
from jax.experimental.pallas import tpu as pltpu
from jax.sharding import PartitionSpec as P

HD = 64
LANES = 128
AXES = ("dp", "ctx")

eps_norm = 1e-05
clip_limit = 5.0
masked_fill = -1e30
f32 = jnp.float32
bf16 = jnp.bfloat16


def layer_norm(values_in, gain_row, shift_row):
    average = jnp.mean(values_in, axis=-1, keepdims=True)
    centred = values_in - average
    variance = jnp.mean(centred * centred, axis=-1, keepdims=True)
    return centred * lax.rsqrt(variance + eps_norm) * gain_row + shift_row


def to_low(values_in):
    return values_in.astype(bf16)


def product(left, right):
    return jnp.dot(left, right, preferred_element_type=f32)


def contract_rows(left, right):
    return lax.dot_general(left, right, (((0,), (0,)), ((), ())), preferred_element_type=f32)


def contract_cols(left, right):
    return lax.dot_general(left, right, (((1,), (1,)), ((), ())), preferred_element_type=f32)


def column_sum(values_in):
    return jnp.sum(values_in.astype(f32), axis=0)


class Moves:
    def __init__(self, dp, ctx, local_seqs):
        self.dp, self.ctx, self.seqs = dp, ctx, local_seqs
        self.d = lax.axis_index("dp")
        self.z = lax.axis_index("ctx")
        self.core = self.d % 2
        self.cube = dp == 8 and ctx == 4
        self.x = (self.d // 2) % 2
        self.y = self.d // 4

    def permute(self, values, target):
        pairs = []
        for d in range(self.dp):
            for z in range(self.ctx):
                there = target(d, z)
                if there is not None:
                    pairs.append((d * self.ctx + z, there[0] * self.ctx + there[1]))
        return lax.ppermute(values, AXES, pairs)

    def swap_core(self, values):
        return self.permute(values, lambda d, z: (d ^ 1, z))

    def swap_x(self, values):
        return self.permute(values, lambda d, z: (d ^ 2, z))

    def swap_y(self, values):
        return self.permute(values, lambda d, z: (d ^ 4, z))

    def up(self, values):
        return self.permute(values, lambda d, z: (d, z + 1) if z + 1 < self.ctx else None)

    def down(self, values):
        return self.permute(values, lambda d, z: (d, z - 1) if z > 0 else None)

    def sequence_target(self, step):
        n = self.seqs

        def target(d, z):
            return (d - d % 2 + z // n, n * (d % 2) + (z + step) % n)

        return target

    def to_sequences(self, values):
        n = self.seqs
        came = []
        for step in range(n):
            block = lax.dynamic_index_in_dim(values, (self.z + step) % n, 0, keepdims=False)
            came.append(self.permute(block, self.sequence_target(step)))
        return jnp.concatenate([self.choose(came, (self.z - t) % n) for t in range(n)], axis=0)

    def from_sequences(self, values):
        n = self.seqs
        parts = values.reshape(n, values.shape[0] // n, values.shape[1])
        came = []
        for step in range(n):
            forward = self.sequence_target(step)
            block = lax.dynamic_index_in_dim(parts, (self.z - step) % n, 0, keepdims=False)
            back = {}
            for d in range(self.dp):
                for z in range(self.ctx):
                    back[forward(d, z)] = (d, z)
            came.append(self.permute(block, lambda d, z: back[(d, z)]))
        return jnp.stack([self.choose(came, (j - self.z) % n) for j in range(n)], axis=0)

    @staticmethod
    def choose(items, index):
        picked = items[0]
        for i in range(1, len(items)):
            picked = jnp.where(index == i, items[i], picked)
        return picked

    def gather_ctx(self, block):
        if not self.cube:
            return lax.all_gather(block, "ctx", axis=0, tiled=False)
        rising, falling = [block], [block]
        for _ in range(self.ctx - 1):
            rising.append(self.up(rising[-1]))
            falling.append(self.down(falling[-1]))
        line = jnp.stack(rising[:0:-1] + falling, axis=0)
        return lax.dynamic_slice_in_dim(line, self.ctx - 1 - self.z, self.ctx, 0)

    def gather_dp(self, block):
        if not self.cube:
            return lax.all_gather(block, "dp", axis=0, tiled=True)
        rows, cols = block.shape
        half = (cols // 2 + LANES - 1) // LANES * LANES
        from_x, from_y = self.swap_x(block), self.swap_y(block)
        far = jnp.concatenate(
            [self.swap_y(from_x[:, :half]), self.swap_x(from_y[:, half:])], axis=1
        )
        mine = jnp.zeros((4, rows, cols), block.dtype)
        here = 2 * self.y + self.x
        for step, part in enumerate((block, from_x, from_y, far)):
            mine = lax.dynamic_update_slice(mine, part[None], (here ^ step, 0, 0))
        other = self.swap_core(mine)
        first = jnp.where(self.core == 0, mine, other)
        second = jnp.where(self.core == 0, other, mine)
        return jnp.stack([first, second], axis=1).reshape(8 * rows, cols)

    def scatter_ctx(self, blocks):
        if not self.cube:
            return lax.psum_scatter(blocks, "ctx", scatter_dimension=0, tiled=False).astype(f32)

        def part(index):
            return lax.dynamic_index_in_dim(blocks, jnp.clip(index, 0, self.ctx - 1), 0, False)

        falling = rising = None
        for step in range(self.ctx - 1, 0, -1):
            low, high = part(self.z - step), part(self.z + step)
            if falling is not None:
                low = to_low(low.astype(f32) + falling.astype(f32))
                high = to_low(high.astype(f32) + rising.astype(f32))
            n = self.ctx
            falling = self.permute(
                low, lambda d, z: (d, z - 1) if z - step >= 0 else None
            )
            rising = self.permute(
                high, lambda d, z: (d, z + 1) if z + step < n else None
            )
        return part(self.z).astype(f32) + falling.astype(f32) + rising.astype(f32)

    def weight_terms(self, left, right):
        if not self.cube:
            return to_low(contract_rows(left, right))
        tokens, width = left.shape
        rows = width // self.dp
        parts = left.reshape(tokens, self.dp // 2, 2, rows)
        even = parts[:, :, 0].reshape(tokens, -1)
        odd = parts[:, :, 1].reshape(tokens, -1)
        own = jnp.where(self.core == 0, even, odd)
        sibling = jnp.where(self.core == 0, odd, even)
        came = self.swap_core(to_low(contract_rows(sibling, right)))
        return to_low(contract_rows(own, right) + came.astype(f32))

    def scatter_dp(self, terms):
        if not self.cube:
            return lax.psum_scatter(terms, "dp", scatter_dimension=0, tiled=True)
        rows, cols = terms.shape[0] // 4, terms.shape[1]
        half = (cols // 2 + LANES - 1) // LANES * LANES
        grid = terms.reshape(2, 2, rows, cols)

        def pick(values, index, axis):
            return lax.dynamic_index_in_dim(values, index, axis, False)

        def added(one, two):
            return to_low(one.astype(f32) + two.astype(f32))

        left, right = grid[..., :half], grid[..., half:]
        left_x = self.swap_x(pick(left, 1 - self.x, 1))
        right_y = self.swap_y(pick(right, 1 - self.y, 0))
        left = added(pick(left, self.x, 1), left_x)
        right = added(pick(right, self.y, 0), right_y)
        left_y = self.swap_y(pick(left, 1 - self.y, 0))
        right_x = self.swap_x(pick(right, 1 - self.x, 0))
        left = added(pick(left, self.y, 0), left_y)
        right = added(pick(right, self.x, 0), right_x)
        return jnp.concatenate([left, right], axis=1)


def nt(left, right):
    return lax.dot_general(left, right, (((1,), (1,)), ((), ())), preferred_element_type=f32)


def tn(left, right):
    return lax.dot_general(left, right, (((0,), (0,)), ((), ())), preferred_element_type=f32)


def fill_bias(kinfo_ref, qinfo_ref, bias_ref):
    diff = qinfo_ref[0:1, :] - kinfo_ref[:, 0:1]
    fine = (diff >= 0) & (diff <= kinfo_ref[:, 1:2])
    bias_ref[...] = jnp.where(fine, 0.0, masked_fill)


def attend_forward_kernel(
    heads, kinfo_ref, qinfo_ref, q_ref, own_ref, sib_ref, out_ref, lse_ref, top_ref, bias_ref
):
    step = pl.program_id(0)

    @pl.when(step == 0)
    def _():
        fill_bias(kinfo_ref, qinfo_ref, bias_ref)

    keys = jnp.concatenate([own_ref[0], sib_ref[0]], axis=0)
    values = jnp.concatenate([own_ref[1], sib_ref[1]], axis=0)
    queries = q_ref[...]
    lane = lax.broadcasted_iota(jnp.int32, queries.shape, 1)
    outs = []
    for side in range(2):
        mine = (lane >= HD) if side else (lane < HD)
        picked = jnp.where(mine, queries, jnp.zeros_like(queries)) * bf16(HD**-0.5)
        scores = nt(keys, picked) + bias_ref[...]
        top = jnp.max(scores, axis=0, keepdims=True)
        weights = jnp.exp(scores - top)
        total = jnp.sum(weights, axis=0, keepdims=True)
        mixed = tn(values[:, side * HD : (side + 1) * HD], weights.astype(bf16))
        outs.append(mixed * (1.0 / total))
        lse_ref[0, side : side + 1, :] = top + jnp.log(total)
        top_ref[0, side : side + 1, :] = top
    out_ref[...] = jnp.concatenate(outs, axis=0).T.astype(bf16)


def attend_backward_kernel(
    heads,
    kinfo_ref,
    qinfo_ref,
    q_ref,
    own_ref,
    sib_ref,
    grad_ref,
    lse_ref,
    dq_ref,
    down_ref,
    dsib_ref,
    bias_ref,
):
    step = pl.program_id(0)

    @pl.when(step == 0)
    def _():
        fill_bias(kinfo_ref, qinfo_ref, bias_ref)

    keys = jnp.concatenate([own_ref[0], sib_ref[0]], axis=0)
    values = jnp.concatenate([own_ref[1], sib_ref[1]], axis=0)
    queries, grads = q_ref[...], grad_ref[...]
    half = queries.shape[0]
    lane = lax.broadcasted_iota(jnp.int32, queries.shape, 1)
    dqs, dk, dv = [], 0.0, 0.0
    for side in range(2):
        mine = (lane >= HD) if side else (lane < HD)
        picked = jnp.where(mine, queries, jnp.zeros_like(queries)) * bf16(HD**-0.5)
        grad = jnp.where(mine, grads, jnp.zeros_like(grads))
        scores = nt(keys, picked) + bias_ref[...]
        weights = jnp.exp(scores - lse_ref[0, side : side + 1, :])
        dp = nt(values, grad)
        delta = jnp.sum(weights * dp, axis=0, keepdims=True)
        ds = (weights * (dp - delta)).astype(bf16)
        dqs.append(tn(keys[:, side * HD : (side + 1) * HD], ds) * (HD**-0.5))
        dk = dk + product(ds, picked)
        dv = dv + product(weights.astype(bf16), grad)
    dq_ref[...] = jnp.concatenate(dqs, axis=0).T.astype(bf16)
    dk, dv = dk.astype(bf16), dv.astype(bf16)
    down_ref[0] = dk[:half]
    dsib_ref[0] = dk[half:]
    down_ref[1] = dv[:half]
    dsib_ref[1] = dv[half:]


def pair_specs(rows):
    flat = pl.BlockSpec((rows, LANES), lambda i: (0, i))
    double = pl.BlockSpec((2, rows, LANES), lambda i: (0, 0, i))
    per_head = pl.BlockSpec((1, 2, rows), lambda i: (i, 0, 0))
    return flat, double, per_head


def attend_forward(heads, kinfo, qinfo, queries, own, sib):
    rows, width = queries.shape
    pairs = width // LANES
    flat, double, per_head = pair_specs(rows)
    small = jax.ShapeDtypeStruct((pairs, 2, rows), f32)
    return pl.pallas_call(
        partial(attend_forward_kernel, heads),
        grid=(pairs,),
        in_specs=[
            pl.BlockSpec(kinfo.shape, lambda i: (0, 0)),
            pl.BlockSpec(qinfo.shape, lambda i: (0, 0)),
            flat,
            double,
            double,
        ],
        out_specs=[flat, per_head, per_head],
        out_shape=[jax.ShapeDtypeStruct((rows, width), bf16), small, small],
        scratch_shapes=[pltpu.VMEM((2 * rows, rows), f32)],
        compiler_params=pltpu.CompilerParams(vmem_limit_bytes=48 * 2**20),
        cost_estimate=pl.CostEstimate(
            flops=pairs * 16 * rows * rows * LANES,
            bytes_accessed=rows * width * 12,
            transcendentals=pairs * 4 * rows * rows,
        ),
        name="attend_forward",
    )(kinfo, qinfo, queries, own, sib)


def attend_backward(heads, kinfo, qinfo, queries, own, sib, grad, lse):
    rows, width = queries.shape
    pairs = width // LANES
    flat, double, per_head = pair_specs(rows)
    both = jax.ShapeDtypeStruct((2, rows, width), bf16)
    return pl.pallas_call(
        partial(attend_backward_kernel, heads),
        grid=(pairs,),
        in_specs=[
            pl.BlockSpec(kinfo.shape, lambda i: (0, 0)),
            pl.BlockSpec(qinfo.shape, lambda i: (0, 0)),
            flat,
            double,
            double,
            flat,
            per_head,
        ],
        out_specs=[flat, double, double],
        out_shape=[jax.ShapeDtypeStruct((rows, width), bf16), both, both],
        scratch_shapes=[pltpu.VMEM((2 * rows, rows), f32)],
        compiler_params=pltpu.CompilerParams(vmem_limit_bytes=48 * 2**20),
        cost_estimate=pl.CostEstimate(
            flops=pairs * 40 * rows * rows * LANES,
            bytes_accessed=rows * width * 22,
            transcendentals=pairs * 4 * rows * rows,
        ),
        name="attend_backward",
    )(kinfo, qinfo, queries, own, sib, grad, lse)


def shards(
    dp,
    ctx,
    inputs,
    cotangent,
    w_qkv,
    w_out,
    w_up,
    w_down,
    vectors,
    bias_up,
    segment_ids,
    padding,
    stretch_order,
):
    local_seqs, query_len, width = inputs.shape
    length = segment_ids.shape[1]
    half = length // 2
    heads = width // HD
    wide = (width + LANES - 1) // LANES * LANES
    rows_d = w_qkv.shape[0]
    cols_d = w_out.shape[1]
    cols_f = w_up.shape[1]
    ratio = w_down.shape[0] // rows_d
    hidden_width = cols_f * ctx
    moves = Moves(dp, ctx, local_seqs)
    core, place = moves.core, moves.z

    extra = jnp.concatenate([vectors.reshape(-1, cols_f), bias_up[None]], axis=0)
    first = jnp.concatenate([jnp.concatenate([w_qkv, w_out], axis=1), extra], axis=0)
    first = moves.gather_ctx(first)
    x_flat = moves.to_sequences(inputs).astype(f32)
    down_packed = jnp.swapaxes(w_down.reshape(ratio, rows_d, cols_d), 0, 1).reshape(rows_d, -1)
    second = moves.gather_ctx(jnp.concatenate([w_up, down_packed], axis=0))
    cot = moves.to_sequences(cotangent)

    def columns(blocks):
        return jnp.swapaxes(blocks, 0, 1).reshape(blocks.shape[1], -1)

    cols_q = w_qkv.shape[1]
    part_qkv = columns(first[:, :rows_d, :cols_q])
    part_out = columns(first[:, :rows_d, cols_q:])
    small = first[:, rows_d:]
    vec_rows = columns(small[:, :-1].reshape(ctx, 8, cols_d)).astype(f32)
    bias_row = small[:, -1].reshape(-1).astype(f32)
    part_up = columns(second[:, :rows_d])
    part_down = second[:, rows_d:].reshape(ctx, rows_d, ratio, cols_d)
    part_down = jnp.transpose(part_down, (2, 1, 0, 3)).reshape(ratio * rows_d, width)

    wide_qkv = moves.gather_dp(part_qkv)
    wide_out = moves.gather_dp(part_out)
    wide_up = moves.gather_dp(part_up)
    wide_down = moves.gather_dp(part_down)

    info = jnp.stack([segment_ids, padding], axis=0)
    info_there = moves.swap_core(info)
    info = jnp.where(place // local_seqs == core, info, info_there)
    info = lax.dynamic_index_in_dim(info, place % local_seqs, 1, False)
    stretches = stretch_order.shape[0]
    stretch_len = length // stretches
    info = jnp.take(info.reshape(2, stretches, stretch_len), stretch_order, axis=1)
    positions = stretch_order[:, None] * stretch_len + jnp.arange(stretch_len, dtype=jnp.int32)
    code = (info[0] * (2 * length) + positions).reshape(2, half)
    reach = (info[1] * (length - 1)).reshape(2, half)
    code_own = lax.dynamic_index_in_dim(code, core, 0, False)
    code_sib = lax.dynamic_index_in_dim(code, 1 - core, 0, False)
    reach_own = lax.dynamic_index_in_dim(reach, core, 0, False)
    reach_sib = lax.dynamic_index_in_dim(reach, 1 - core, 0, False)
    kinfo = jnp.stack(
        [jnp.concatenate([code_own, code_sib]), jnp.concatenate([reach_own, reach_sib])], axis=1
    )
    qinfo = code_own[None]

    normed = to_low(layer_norm(x_flat, vec_rows[0], vec_rows[1]))
    projected = product(normed, wide_qkv)

    def padded(values):
        return jnp.pad(to_low(values), ((0, 0), (0, wide - width)))

    queries = padded(projected[:, :width] + vec_rows[2])
    own = jnp.stack(
        [
            padded(projected[:, width : 2 * width]),
            padded(projected[:, 2 * width :] + vec_rows[3]),
        ]
    )
    sib = moves.swap_core(own)
    attended, lse, tops = attend_forward(heads, kinfo, qinfo, queries, own, sib)
    attended = attended[:, :width]
    block_top = jnp.max(tops, axis=2).reshape(-1)[:heads]
    global_top = lax.pmax(block_top, AXES)
    residual = x_flat + product(attended, wide_out) + vec_rows[4]
    normed_two = to_low(layer_norm(residual, vec_rows[5], vec_rows[6]))
    up_pre = product(normed_two, wide_up) + bias_row
    hidden = to_low(jax.nn.gelu(up_pre, approximate=True))
    output = to_low(residual + product(hidden, wide_down) + vec_rows[7])
    output = moves.from_sequences(output)

    grad_output = cot.astype(f32)
    grad_bias_two = column_sum(cot)
    sum_down = moves.weight_terms(hidden, cot)
    sum_down = moves.scatter_dp(sum_down)
    grad_hidden = contract_cols(cot, wide_down)
    unused, gelu_back = jax.vjp(partial(jax.nn.gelu, approximate=True), up_pre)
    grad_pre = to_low(gelu_back(grad_hidden)[0])
    grad_bias_up = column_sum(grad_pre)
    sum_up = moves.weight_terms(normed_two, grad_pre)
    sum_up = moves.scatter_dp(sum_up)
    unused, norm_back_two = jax.vjp(layer_norm, residual, vec_rows[5], vec_rows[6])
    back_two = norm_back_two(contract_cols(grad_pre, wide_up))
    grad_residual = grad_output + back_two[0]
    grad_branch = to_low(grad_residual)
    sum_out = moves.weight_terms(attended, grad_branch)
    sum_out = moves.scatter_dp(sum_out)
    grad_attended = padded(contract_cols(grad_branch, wide_out))
    dq, d_own, d_sib = attend_backward(
        heads, kinfo, qinfo, queries, own, sib, grad_attended, lse
    )
    d_came = moves.swap_core(d_sib)
    d_own = to_low(d_own.astype(f32) + d_came.astype(f32))
    grad_proj = jnp.concatenate([dq[:, :width], d_own[0, :, :width], d_own[1, :, :width]], axis=1)
    sum_qkv = moves.weight_terms(normed, grad_proj)
    sum_qkv = moves.scatter_dp(sum_qkv)
    unused, norm_back_one = jax.vjp(layer_norm, x_flat, vec_rows[0], vec_rows[1])
    back_one = norm_back_one(contract_cols(grad_proj, wide_qkv))
    grad_input = to_low(grad_residual + back_one[0])
    grad_input = moves.from_sequences(grad_input).astype(f32)
    grad_vectors = jnp.stack(
        [
            back_one[1],
            back_one[2],
            column_sum(dq[:, :width]),
            column_sum(d_own[1, :, :width]),
            column_sum(grad_branch),
            back_two[1],
            back_two[2],
            grad_bias_two,
        ]
    )

    def by_place(values):
        return jnp.swapaxes(values.reshape(values.shape[0], ctx, -1), 0, 1)

    blocks_down = sum_down.reshape(ratio, rows_d, ctx, cols_d)
    blocks_down = jnp.transpose(blocks_down, (2, 1, 0, 3)).reshape(ctx, rows_d, -1)
    later = jnp.concatenate([by_place(sum_up), blocks_down, by_place(sum_out)], axis=2)
    later = moves.scatter_ctx(later)
    grad_up = later[:, :cols_f]
    grad_down = later[:, cols_f : 2 * cols_f].reshape(rows_d, ratio, cols_d)
    grad_down = jnp.swapaxes(grad_down, 0, 1).reshape(ratio * rows_d, cols_d)
    grad_out = later[:, 2 * cols_f :]
    grad_qkv = moves.scatter_ctx(by_place(sum_qkv))

    tiny = jnp.concatenate([grad_vectors, grad_bias_up.reshape(-1, width)], axis=0)
    tiny = lax.psum(tiny, AXES)
    grad_vectors = lax.dynamic_slice_in_dim(tiny[:8], place * cols_d, cols_d, 1)
    grad_bias = lax.dynamic_slice_in_dim(tiny[8:].reshape(-1), place * cols_f, cols_f)

    factor = clip_limit / jnp.maximum(global_top, clip_limit)
    per_column = jnp.repeat(jnp.sqrt(factor), HD)
    column_scale = jnp.concatenate([per_column, per_column, jnp.ones((width,), f32)])
    local_scale = lax.dynamic_slice_in_dim(column_scale, place * cols_q, cols_q)
    clipped_qkv = to_low(w_qkv.astype(f32) * local_scale[None, :])
    bias_scale = lax.dynamic_slice_in_dim(per_column, place * cols_d, cols_d)
    clipped_bias = to_low(vectors[2].astype(f32) * bias_scale)
    return (
        output,
        grad_input,
        grad_qkv,
        grad_out,
        grad_up,
        grad_down,
        grad_vectors,
        grad_bias,
        clipped_qkv,
        clipped_bias,
        global_top,
    )


def solution(mesh):
    return jax.shard_map(
        partial(shards, mesh.shape["dp"], mesh.shape["ctx"]),
        mesh=mesh,
        in_specs=(
            P("dp", "ctx", None),
            P("dp", "ctx", None),
            P("dp", "ctx"),
            P("dp", "ctx"),
            P("dp", "ctx"),
            P("dp", "ctx"),
            P(None, "ctx"),
            P("ctx"),
            P("dp", None),
            P("dp", None),
            P(),
        ),
        out_specs=(
            P("dp", "ctx", None),
            P("dp", "ctx", None),
            P("dp", "ctx"),
            P("dp", "ctx"),
            P("dp", "ctx"),
            P("dp", "ctx"),
            P(None, "ctx"),
            P("ctx"),
            P("dp", "ctx"),
            P("ctx"),
            P(),
        ),
        check_vma=False,
    )
```

time: 1210 us -> 882 us (0.73)
  waiting for transfers between devices: 629 us -> 176 us
  matrix products: 281 us -> 110 us
  starting transfers between devices: 2.47 us -> 160 us
  local copies, waits for them, and re-layouts: 49.3 us -> 169 us
  blocking collectives: 157 us -> 87.3 us
  Pallas kernels: 0 us -> 54.8 us
  other arithmetic: 65 us -> 107 us
  between operations: 16.8 us -> 3.31 us
    all_gather x10 -> x0, waiting for transfers between devices: 293 us -> none  [the longest x2 61.1 us: forward_micro(): lax.all_gather(key_local, 'ctx', axis=1, tiled=True)]
    reduce_scatter x7 -> x0, waiting for transfers between devices: 190 us -> none  [the longest x1 67.2 us: reduce_grads(): lax.psum_scatter(grad_up.astype(jnp.bfloat16), 'dp', scatter_dimension=0,...]
    ppermute x0 -> x75, waiting for transfers between devices: none -> 176 us  [permute(): return lax.ppermute(values, AXES, pairs)]
    ppermute x0 -> x75, starting transfers between devices: none -> 160 us  [permute(): return lax.ppermute(values, AXES, pairs)]
    unnamed x29 -> x0, waiting for transfers between devices: 147 us -> none
    dot_general x20 -> x4, matrix products: 165 us -> 39.3 us  [product(): return jnp.dot(left, right, preferred_element_type=f32)]
    all_gather x3 -> x0, blocking collectives: 56.9 us -> none  [the longest x1 23.6 us: gather_weights(): lax.all_gather(w_qkv, 'ctx', axis=1, tiled=True)]
    pallas_call x0 -> x2, Pallas kernels: none -> 54.8 us  [the longest x1 34.4 us: attend_backward(): pl.pallas_call(partial(attend_backward_kernel, heads), grid=(pairs,), in_...]
  transfers between devices with their start and end apart: 23 -> 75, of which waited for: 20 -> 23; matrix products, arithmetic and copies ran while one was open for 28% -> 43% of each run, Pallas kernels for 0% -> 6%
where the time goes in v1:
time: 882 us; the launch traced here: 868 us
  waiting for transfers between devices  176 us (20%)
  local copies, waits for them, and re-layouts  169 us (19%)
  starting transfers between devices  160 us (18%)
  matrix products  110 us (12%)
  other arithmetic  107 us (12%)
  blocking collectives  87.3 us (10%)
  Pallas kernels  54.8 us (6%)
    ppermute x75, waiting for transfers between devices, permute(): return lax.ppermute(values, AXES, pairs)  176 us
    ppermute x75, starting transfers between devices, permute(): return lax.ppermute(values, AXES, pairs)  160 us
    psum x1, blocking collectives, shards(): tiny = lax.psum(tiny, AXES)  48.6 us
    another operation x8, other arithmetic, gather_dp(): return jnp.stack([first, second], axis=1).reshape(8 * rows, cols)  43.6 us
    dot_general x4, matrix products, product(): return jnp.dot(left, right, preferred_element_type=f32)  39.3 us
    pmax x1, blocking collectives, shards(): global_top = lax.pmax(block_top, AXES)  38.6 us
    dot_general x4, matrix products, contract_cols(): lax.dot_general(left, right, (((1,), (1,)), ((), ())), preferred_element_...  35.9 us
    dot_general x8, matrix products, contract_rows(): lax.dot_general(left, right, (((0,), (0,)), ((), ())), preferred_element_...  34.8 us
  transfers between devices with their start and end apart: 75, of which 23 were waited for; matrix products, arithmetic and copies ran while one was open for 43% of the time, Pallas kernels for 6%

profile of v1, /device:TPU:0, one launch (start us, length us, event | category | flops | bytes accessed | tf_op | source)
XLA Modules:
  0.0 868.2 jit_solution(6321930268903506383)
XLA Ops:
  4.1 5.7 collective-permute-start.3
  13.0 5.9 collective-permute-start.1
  30.7 5.9 collective-permute-start.20
  39.2 14.3 %collective-permute-done.6 = bf16[139,1088]{1,0:T(8,128)(2,1)S(1)} collective-permute-done((bf16[139,1088]{1,0:T(8,128)(2,1)}, bf16[139,1088]{1,0:T(8,128)(2,1)S(1)}, u32[]{:S(2)}, u32[]{:S(2)}) %collective-permute-start.6) | collective-permute-done | bytes 302496 | tf_op jit(solution)/shard_map/ppermute | solution.py:65
  53.5 29.9 %collective-permute-start.4 = (bf16[139,1088]{1,0:T(8,128)(2,1)}, bf16[139,1088]{1,0:T(8,128)(2,1)S(1)}, u32[]{:S(2)}, u32[]{:S(2)}) collective-permute-start(bf16[139,1088]{1,0:T(8,128)(2,1)} %collective-permute-done.3), channel_id=1, source_target_pairs={{0,1},{1,2},{2,3},{4,5},{5,6},{6,7},{8,9},{9,10},{10,11},{12,13},{... | collective-permute-start | bytes 907400 | tf_op jit(solution)/shard_map/ppermute | solution.py:65
  87.1 4.5 collective-permute-done.4
  91.7 4.3 collective-permute-start.5
  96.4 2.8 collective-permute-start.21
  103.3 11.8 %collective-permute-done.8 = bf16[139,1088]{1,0:T(8,128)(2,1)S(1)} collective-permute-done((bf16[139,1088]{1,0:T(8,128)(2,1)S(1)}, bf16[139,1088]{1,0:T(8,128)(2,1)S(1)}, u32[]{:S(2)}, u32[]{:S(2)}) %collective-permute-start.8) | collective-permute-done | bytes 302496 | tf_op jit(solution)/shard_map/ppermute | solution.py:65
  161.0 5.5 collective-permute-done.25
  167.9 2.9 reshape.357
  195.8 18.6 %collective-permute-done.12 = bf16[136,1600]{1,0:T(8,128)(2,1)S(1)} collective-permute-done((bf16[136,1600]{1,0:T(8,128)(2,1)S(1)}, bf16[136,1600]{1,0:T(8,128)(2,1)S(1)}, u32[]{:S(2)}, u32[]{:S(2)}) %collective-permute-start.12) | collective-permute-done | bytes 435232 | tf_op jit(solution)/shard_map/ppermute | solution.py:65
  231.0 9.8 %collective-permute-done.26 = bf16[136,4352]{1,0:T(8,128)(2,1)S(1)} collective-permute-done((bf16[136,4352]{1,0:T(8,128)(2,1)S(1)}, bf16[136,4352]{1,0:T(8,128)(2,1)S(1)}, u32[]{:S(2)}, u32[]{:S(2)}) %collective-permute-start.26) | collective-permute-done | bytes 1183776 | tf_op jit(solution)/shard_map/ppermute | solution.py:65
  251.1 3.7 pad_maximum_fusion.2
  254.8 7.5 fusion.39
  270.5 3.3 bitcast_dynamic-update-slice_fusion.1
  281.5 3.1 copy.224
  286.6 20.3 %attend_forward.1 = (bf16[512,1152]{1,0:T(8,128)(2,1)S(1)}, f32[9,2,512]{2,1,0:T(2,128)S(1)}, f32[9,2,512]{2,1,0:T(2,128)S(1)}) custom-call(s32[1024,2]{1,0:T(8,128)S(1)} %copy-done.3, s32[1,512]{1,0:T(1,128)S(1)} %get-tuple-element.146.qinfo_ref, bf16[512,1152]{1,0:T(8,128)(2,1)S(1)} %pad.13.q_ref, bf16[2,512,1152]{2,1,0:T(8,128)(2,1)S(1)} %pad_maximum_fusion.4.own_ref, ...), custom_call_target="tpu_custom_call" | custom-call | flops 4831838208 | bytes 7077888 | tf_op jit(solution)/shard_map/attend_forward/pallas_call | solution.py:307
  309.2 38.6 %pmax.7 = f32[17]{0:T(128)S(1)} all-reduce(f32[17]{0:T(128)S(1)} %bitcast.438), channel_id=1, replica_groups=mesh['dp'=8,'ctx'=4] {'dp','ctx'}, use_global_device_ids=true, to_apply=%region_19.20 | all-reduce | flops 17 | bytes 136 | tf_op jit(solution)/shard_map/pmax | solution.py:450
  348.8 3.5 fusion.80
  356.9 8.0 select_bitcast_fusion.3
  364.9 8.2 pad_maximum_fusion.1
  373.1 15.1 %multiply_convert_fusion = (bf16[512,4352]{1,0:T(8,128)(2,1)}, f32[512,4352]{1,0:T(8,128)}) fusion(f32[4352]{0:T(1024)S(1)} %copy-done.76, bf16[512,1088]{0,1:T(8,128)(2,1)S(1)} %add_convert_fusion.8, bf16[1088,4352]{1,0:T(8,128)(2,1)} %bitcast.395), kind=kOutput, calls=%fused_computation.17 | convolution fusion | flops 4870897664 | bytes 23970816 | tf_op jit(solution)/shard_map/dot_general | solution.py:33
  388.2 6.5 copy.205
  394.7 4.1 broadcast_select_fusion
  398.8 4.8 convolution_convert_fusion
  403.7 8.7 select_bitcast_fusion.1
  412.4 8.9 %pad_maximum_fusion = bf16[4,2,544,1088]{3,2,1,0:T(8,128)(2,1)} fusion(bf16[4,1,544,1088]{3,2,1,0:T(8,128)(2,1)} %get-tuple-element.81, bf16[4,1,544,1088]{3,2,1,0:T(8,128)(2,1)} %get-tuple-element.80), kind=kLoop, calls=%fused_computation.6 | loop fusion | flops 4734976 | bytes 18939904 | tf_op jit(solution)/shard_map/stack | solution.py:145
  421.3 14.1 %convert_reduce_fusion = (f32[4352]{0:T(1024)S(1)}, bf16[512,4352]{1,0:T(8,128)(2,1)S(1)}) fusion(f32[512,4352]{1,0:T(8,128)} %get-tuple-element.155, f32[4352]{0:T(1024)S(1)} %copy-done.76, bf16[4352,1088]{1,0:T(8,128)(2,1)} %bitcast.393, bf16[256,1088]{0,1:T(8,128)(2,1)S(1)} %copy-done.31, bf16[256,1088]{0,1:T(8,128)(2,1)S(1)} %copy-done.30), kind=kOutput, calls=%fused_computation.16 | convolution fusion | flops 4902088704 | bytes 23988224 | tf_op jit(solution)/shard_map/dot_general | solution.py:41
  435.4 10.8 %multiply_reduce_fusion = (f32[1088]{0:T(1024)S(1)}, f32[512]{0:T(512)S(1)}, f32[1088]{0:T(1024)S(1)}, f32[512,1088]{0,1:T(8,128)S(1)}) fusion(f32[512,1088]{0,1:T(8,128)S(1)} %copy-done.17, f32[512]{0:T(512)S(1)} %fusion.70, f32[512]{0:T(512)S(1)} %broadcast_multiply_fusion, f32[1088]{0:T(1024)S(1)} %copy-done.64, ...), kind=kOutput, calls=%fused_computation.69 | convolution fusion | flops 4853069312 | bytes 18402048 | tf_op jit(solution)/shard_map/dot_general | solution.py:41
  454.3 34.4 %attend_backward.1 = (bf16[512,1152]{1,0:T(8,128)(2,1)S(1)}, bf16[2,512,1152]{2,1,0:T(8,128)(2,1)}, bf16[2,512,1152]{2,1,0:T(8,128)(2,1)}) custom-call(s32[1024,2]{1,0:T(8,128)S(1)} %copy-done.4, s32[1,512]{1,0:T(1,128)S(1)} %get-tuple-element.146.qinfo_ref, bf16[512,1152]{1,0:T(8,128)(2,1)S(1)} %copy-done.2, bf16[2,512,1152]{2,1,0:T(8,128)(2,1)} %copy-done, ...), custom_call_target="tpu_custom_call" | custom-call | flops 12079595520 | bytes 12976128 | tf_op jit(solution)/shard_map/attend_backward/pallas_call | solution.py:335
  491.5 13.3 %fusion.14 = bf16[512,1088]{0,1:T(8,128)(2,1)} fusion(f32[512,1088]{0,1:T(8,128)S(1)} %copy-done.18, bf16[512,4352]{1,0:T(8,128)(2,1)} %get-tuple-element.154, bf16[4352,1088]{1,0:T(8,128)(2,1)} %bitcast.394, f32[1088]{0:T(1024)S(1)} %copy-done.79), kind=kOutput, calls=%fused_computation.43 | convolution fusion | flops 4850286592 | bytes 17273088 | tf_op jit(solution)/shard_map/dot_general | solution.py:33
  504.8 2.8 reshape.360
  507.6 3.3 constant_dynamic-slice_fusion.18
  514.4 7.0 convolution_convert_fusion.1
  521.4 5.2 collective-permute-done.36
  534.6 2.8 collective-permute-done.67
  542.9 5.1 collective-permute-done.66
  549.3 2.9 add_convert_fusion.2
  554.4 6.8 concatenate.75
  561.2 8.4 fusion.73
  573.9 48.6 %psum.7 = f32[12,1088]{1,0:T(8,128)S(1)} all-reduce(f32[12,1088]{1,0:T(8,128)S(1)} %concatenate.84), channel_id=1, replica_groups=mesh['dp'=8,'ctx'=4] {'dp','ctx'}, use_global_device_ids=true, to_apply=%region_17.18 | all-reduce | flops 13056 | bytes 104448 | tf_op jit(solution)/shard_map/psum | solution.py:514
  628.2 3.8 convolution_convert_fusion.2
  635.6 5.0 collective-permute-done.41
  641.6 6.3 fusion
  647.9 8.3 copy.206
  660.4 2.8 collective-permute-start.60
  663.4 4.5 add_convert_fusion
  670.6 9.1 %collective-permute-done.62 = bf16[2,544,448]{2,1,0:T(8,128)(2,1)S(1)} collective-permute-done((bf16[2,544,448]{2,1,0:T(8,128)(2,1)S(1)}, bf16[2,544,448]{2,1,0:T(8,128)(2,1)S(1)}, u32[]{:S(2)}, u32[]{:S(2)}) %collective-permute-start.62) | collective-permute-done | bytes 974880 | tf_op jit(solution)/shard_map/ppermute | solution.py:65
  680.2 4.1 add_convert_fusion.1
  689.0 19.3 %collective-permute-done.55 = bf16[2,136,2176]{2,1,0:T(8,128)(2,1)S(1)} collective-permute-done((bf16[2,136,2176]{2,1,0:T(8,128)(2,1)S(1)}, bf16[2,136,2176]{2,1,0:T(8,128)(2,1)S(1)}, u32[]{:S(2)}, u32[]{:S(2)}) %collective-permute-start.55) | collective-permute-done | bytes 1183776 | tf_op jit(solution)/shard_map/ppermute | solution.py:65
  714.9 5.4 collective-permute-done.63
  722.7 9.5 %collective-permute-done.56 = bf16[136,2176]{1,0:T(8,128)(2,1)S(1)} collective-permute-done((bf16[136,2176]{1,0:T(8,128)(2,1)S(1)}, bf16[136,2176]{1,0:T(8,128)(2,1)S(1)}, u32[]{:S(2)}, u32[]{:S(2)}) %collective-permute-start.56) | collective-permute-done | bytes 591904 | tf_op jit(solution)/shard_map/ppermute | solution.py:65
  732.3 20.0 %collective-permute-done.58 = bf16[136,2176]{1,0:T(8,128)(2,1)S(1)} collective-permute-done((bf16[136,2176]{1,0:T(8,128)(2,1)S(1)}, bf16[136,2176]{1,0:T(8,128)(2,1)S(1)}, u32[]{:S(2)}, u32[]{:S(2)}) %collective-permute-start.58) | collective-permute-done | bytes 591904 | tf_op jit(solution)/shard_map/ppermute | solution.py:65
  761.9 8.4 concatenate.83
  770.3 11.3 %constant_dynamic-slice_fusion.9 = (bf16[1,136,2448]{2,0,1:T(2,128)(2,1)}, bf16[1,136,2448]{2,0,1:T(2,128)(2,1)}, bf16[1,136,2448]{2,0,1:T(2,128)(2,1)}, bf16[1,...) fusion(bf16[4,136,2448]{2,0,1:T(4,128)(2,1)S(1)} %concatenate.8, ...), kind=kLoop, calls=%fused_computation.250 | loop fusion | flops 332928 | bytes 9987868 | tf_op jit(solution)/shard_map/jit(dynamic_index_in_dim)/dynamic_slice | solution.py:152
  784.2 5.8 collective-permute-start.72
  795.9 4.3 collective-permute-done.47
  800.4 3.5 collective-permute-done.45
  804.8 3.5 constant_dynamic-slice_fusion.15
  814.4 9.7 %collective-permute-start.52 = (bf16[136,816]{1,0:T(8,128)(2,1)S(1)}, bf16[136,816]{1,0:T(8,128)(2,1)S(1)}, u32[]{:S(2)}, u32[]{:S(2)}) collective-permute-start(bf16[136,816]{1,0:T(8,128)(2,1)S(1)} %fusion.51), channel_id=1, source_target_pairs={{0,1},{1,2},{4,5},{5,6},{8,9},{9,10},{12,13},{13,14},{16,17},{17,1... | collective-permute-start | bytes 665864 | tf_op jit(solution)/shard_map/ppermute | solution.py:65
  827.2 16.6 %collective-permute-start.74 = (bf16[136,2448]{1,0:T(8,128)(2,1)S(1)}, bf16[136,2448]{1,0:T(8,128)(2,1)S(1)}, u32[]{:S(2)}, u32[]{:S(2)}) collective-permute-start(bf16[136,2448]{1,0:T(8,128)(2,1)S(1)} %fusion.30), channel_id=1, source_target_pairs={{0,1},{1,2},{2,3},{4,5},{5,6},{6,7},{8,9},{9,10},{10,11},{12,13},{... | collective-permute-start | bytes 1997576 | tf_op jit(solution)/shard_map/ppermute | solution.py:65
  843.8 3.9 collective-permute-start.53
  849.3 14.2 %collective-permute-done.53 = bf16[136,816]{1,0:T(8,128)(2,1)S(1)} collective-permute-done((bf16[136,816]{1,0:T(8,128)(2,1)S(1)}, bf16[136,816]{1,0:T(8,128)(2,1)S(1)}, u32[]{:S(2)}, u32[]{:S(2)}) %collective-permute-start.53) | collective-permute-done | bytes 221984 | tf_op jit(solution)/shard_map/ppermute | solution.py:65
  (550 shorter events, 254.3 us)
Async XLA Ops:
  4.1 33.9 %collective-permute-start.3 = (bf16[139,1088]{1,0:T(8,128)(2,1)}, bf16[139,1088]{1,0:T(8,128)(2,1)}, u32[]{:S(2)}, u32[]{:S(2)}) collective-permute-start(bf16[139,1088]{1,0:T(8,128)(2,1)} %fusion.59), channel_id=1, source_target_pairs={{0,1},{1,2},{2,3},{4,5},{5,6},{6,7},{8,9},{9,10},{10,11},{12,13},{... | collective-permute-start | bytes 907400 | tf_op jit(solution)/shard_map/ppermute | solution.py:65
  12.1 17.4 %collective-permute-start = (bf16[256,1088]{0,1:T(8,128)(2,1)}, bf16[256,1088]{0,1:T(8,128)(2,1)}, u32[]{:S(2)}, u32[]{:S(2)}) collective-permute-start(bf16[256,1088]{0,1:T(8,128)(2,1)} %get-tuple-element.130), channel_id=1, source_target_pairs={{0,1},{1,0},{2,5},{3,4},{4,3},{5,2},{6,7},{7,6},{8,9},{9,8},{10,13... | collective-permute-start | bytes 1671176 | tf_op jit(solution)/shard_map/ppermute | solution.py:65
  13.0 17.8 %collective-permute-start.1 = (bf16[256,1088]{0,1:T(8,128)(2,1)}, bf16[256,1088]{0,1:T(8,128)(2,1)}, u32[]{:S(2)}, u32[]{:S(2)}) collective-permute-start(bf16[256,1088]{0,1:T(8,128)(2,1)} %get-tuple-element.129), channel_id=1, source_target_pairs={{0,0},{1,1},{2,4},{3,5},{4,2},{5,3},{6,6},{7,7},{8,8},{9,9},{10,12... | collective-permute-start | bytes 1671176 | tf_op jit(solution)/shard_map/ppermute | solution.py:65
  19.0 64.4 %collective-permute-start.38 = (bf16[256,1088]{0,1:T(8,128)(2,1)S(1)}, bf16[256,1088]{0,1:T(8,128)(2,1)S(1)}, u32[]{:S(2)}, u32[]{:S(2)}) collective-permute-start(bf16[256,1088]{0,1:T(8,128)(2,1)S(1)} %get-tuple-element.122), channel_id=1, source_target_pairs={{0,1},{1,0},{2,5},{3,4},{4,3},{5,2},{6,7},{7,6},{8,9},{9,8},{10,13... | collective-permute-start | bytes 1671176 | tf_op jit(solution)/shard_map/ppermute | solution.py:65
  23.6 61.1 %collective-permute-start.39 = (bf16[256,1088]{0,1:T(8,128)(2,1)S(1)}, bf16[256,1088]{0,1:T(8,128)(2,1)}, u32[]{:S(2)}, u32[]{:S(2)}) collective-permute-start(bf16[256,1088]{0,1:T(8,128)(2,1)S(1)} %get-tuple-element.121), channel_id=1, source_target_pairs={{0,0},{1,1},{2,4},{3,5},{4,2},{5,3},{6,6},{7,7},{8,8},{9,9},{10,12... | collective-permute-start | bytes 1671176 | tf_op jit(solution)/shard_map/ppermute | solution.py:65
  29.4 24.1 %collective-permute-start.6 = (bf16[139,1088]{1,0:T(8,128)(2,1)}, bf16[139,1088]{1,0:T(8,128)(2,1)S(1)}, u32[]{:S(2)}, u32[]{:S(2)}) collective-permute-start(bf16[139,1088]{1,0:T(8,128)(2,1)} %fusion.59), channel_id=1, source_target_pairs={{1,0},{2,1},{3,2},{5,4},{6,5},{7,6},{9,8},{10,9},{11,10},{13,12},{... | collective-permute-start | bytes 907400 | tf_op jit(solution)/shard_map/ppermute | solution.py:65
  30.7 65.6 %collective-permute-start.20 = (bf16[272,1088]{1,0:T(8,128)(2,1)S(1)}, bf16[272,1088]{1,0:T(8,128)(2,1)}, u32[]{:S(2)}, u32[]{:S(2)}) collective-permute-start(bf16[272,1088]{1,0:T(8,128)(2,1)S(1)} %constant_dynamic-update-slice_fusion), channel_id=1, source_target_pairs={{0,1},{1,2},{2,3},{4,5},{5,6},{6,7},{8,9},{9,10},{10,11},{12,13},{... | collective-permute-start | bytes 1775624 | tf_op jit(solution)/shard_map/ppermute | solution.py:65
  37.9 61.3 %collective-permute-start.23 = (bf16[272,1088]{1,0:T(8,128)(2,1)S(1)}, bf16[272,1088]{1,0:T(8,128)(2,1)}, u32[]{:S(2)}, u32[]{:S(2)}) collective-permute-start(bf16[272,1088]{1,0:T(8,128)(2,1)S(1)} %constant_dynamic-update-slice_fusion), channel_id=1, source_target_pairs={{1,0},{2,1},{3,2},{5,4},{6,5},{7,6},{9,8},{10,9},{11,10},{13,12},{... | collective-permute-start | bytes 1775624 | tf_op jit(solution)/shard_map/ppermute | solution.py:65
  53.5 38.2 %collective-permute-start.4 = (bf16[139,1088]{1,0:T(8,128)(2,1)}, bf16[139,1088]{1,0:T(8,128)(2,1)S(1)}, u32[]{:S(2)}, u32[]{:S(2)}) collective-permute-start(bf16[139,1088]{1,0:T(8,128)(2,1)} %collective-permute-done.3), channel_id=1, source_target_pairs={{0,1},{1,2},{2,3},{4,5},{5,6},{6,7},{8,9},{9,10},{10,11},{12,13},{... | collective-permute-start | bytes 907400 | tf_op jit(solution)/shard_map/ppermute | solution.py:65
  83.4 17.1 %collective-permute-start.7 = (bf16[139,1088]{1,0:T(8,128)(2,1)S(1)}, bf16[139,1088]{1,0:T(8,128)(2,1)S(1)}, u32[]{:S(2)}, u32[]{:S(2)}) collective-permute-start(bf16[139,1088]{1,0:T(8,128)(2,1)S(1)} %collective-permute-done.6), channel_id=1, source_target_pairs={{1,0},{2,1},{3,2},{5,4},{6,5},{7,6},{9,8},{10,9},{11,10},{13,12},{... | collective-permute-start | bytes 907400 | tf_op jit(solution)/shard_map/ppermute | solution.py:65
  91.7 10.3 %collective-permute-start.5 = (bf16[139,1088]{1,0:T(8,128)(2,1)S(1)}, bf16[139,1088]{1,0:T(8,128)(2,1)S(1)}, u32[]{:S(2)}, u32[]{:S(2)}) collective-permute-start(bf16[139,1088]{1,0:T(8,128)(2,1)S(1)} %collective-permute-done.4), channel_id=1, source_target_pairs={{0,1},{1,2},{2,3},{4,5},{5,6},{6,7},{8,9},{9,10},{10,11},{12,13},{... | collective-permute-start | bytes 907400 | tf_op jit(solution)/shard_map/ppermute | solution.py:65
  96.4 47.3 %collective-permute-start.21 = (bf16[272,1088]{1,0:T(8,128)(2,1)}, bf16[272,1088]{1,0:T(8,128)(2,1)}, u32[]{:S(2)}, u32[]{:S(2)}) collective-permute-start(bf16[272,1088]{1,0:T(8,128)(2,1)} %collective-permute-done.20), channel_id=1, source_target_pairs={{0,1},{1,2},{2,3},{4,5},{5,6},{6,7},{8,9},{9,10},{10,11},{12,13},{... | collective-permute-start | bytes 1775624 | tf_op jit(solution)/shard_map/ppermute | solution.py:65
  99.2 53.4 %collective-permute-start.24 = (bf16[272,1088]{1,0:T(8,128)(2,1)}, bf16[272,1088]{1,0:T(8,128)(2,1)}, u32[]{:S(2)}, u32[]{:S(2)}) collective-permute-start(bf16[272,1088]{1,0:T(8,128)(2,1)} %collective-permute-done.23), channel_id=1, source_target_pairs={{1,0},{2,1},{3,2},{5,4},{6,5},{7,6},{9,8},{10,9},{11,10},{13,12},{... | collective-permute-start | bytes 1775624 | tf_op jit(solution)/shard_map/ppermute | solution.py:65
  100.5 14.6 %collective-permute-start.8 = (bf16[139,1088]{1,0:T(8,128)(2,1)S(1)}, bf16[139,1088]{1,0:T(8,128)(2,1)S(1)}, u32[]{:S(2)}, u32[]{:S(2)}) collective-permute-start(bf16[139,1088]{1,0:T(8,128)(2,1)S(1)} %collective-permute-done.7), channel_id=1, source_target_pairs={{1,0},{2,1},{3,2},{5,4},{6,5},{7,6},{9,8},{10,9},{11,10},{13,12},{... | collective-permute-start | bytes 907400 | tf_op jit(solution)/shard_map/ppermute | solution.py:65
  117.9 27.2 %collective-permute-start.15 = (bf16[136,1088]{1,0:T(8,128)(2,1)}, bf16[136,1088]{1,0:T(8,128)(2,1)}, u32[]{:S(2)}, u32[]{:S(2)}) collective-permute-start(bf16[136,1088]{1,0:T(8,128)(2,1)} %reshape.351), channel_id=1, source_target_pairs={{0,8},{1,9},{2,10},{3,11},{4,12},{5,13},{6,14},{7,15},{8,0},{9,1},... | collective-permute-start | bytes 887816 | tf_op jit(solution)/shard_map/ppermute | solution.py:65
  119.4 27.3 %collective-permute-start.16 = (bf16[136,1088]{1,0:T(8,128)(2,1)}, bf16[136,1088]{1,0:T(8,128)(2,1)}, u32[]{:S(2)}, u32[]{:S(2)}) collective-permute-start(bf16[136,1088]{1,0:T(8,128)(2,1)} %reshape.351), channel_id=1, source_target_pairs={{0,16},{1,17},{2,18},{3,19},{4,20},{5,21},{6,22},{7,23},{8,24},{9,... | collective-permute-start | bytes 887816 | tf_op jit(solution)/shard_map/ppermute | solution.py:65
  133.6 53.1 %collective-permute-start.9 = (bf16[136,3264]{1,0:T(8,128)(2,1)}, bf16[136,3264]{1,0:T(8,128)(2,1)}, u32[]{:S(2)}, u32[]{:S(2)}) collective-permute-start(bf16[136,3264]{1,0:T(8,128)(2,1)} %reshape.349), channel_id=1, source_target_pairs={{0,8},{1,9},{2,10},{3,11},{4,12},{5,13},{6,14},{7,15},{8,0},{9,1},... | collective-permute-start | bytes 2663432 | tf_op jit(solution)/shard_map/ppermute | solution.py:65
  143.7 12.6 %collective-permute-start.22 = (bf16[272,1088]{1,0:T(8,128)(2,1)}, bf16[272,1088]{1,0:T(8,128)(2,1)S(1)}, u32[]{:S(2)}, u32[]{:S(2)}) collective-permute-start(bf16[272,1088]{1,0:T(8,128)(2,1)} %collective-permute-done.21), channel_id=1, source_target_pairs={{0,1},{1,2},{2,3},{4,5},{5,6},{6,7},{8,9},{9,10},{10,11},{12,13},{... | collective-permute-start | bytes 1775624 | tf_op jit(solution)/shard_map/ppermute | solution.py:65
  152.6 36.2 %collective-permute-start.10 = (bf16[136,3264]{1,0:T(8,128)(2,1)}, bf16[136,3264]{1,0:T(8,128)(2,1)}, u32[]{:S(2)}, u32[]{:S(2)}) collective-permute-start(bf16[136,3264]{1,0:T(8,128)(2,1)} %reshape.349), channel_id=1, source_target_pairs={{0,16},{1,17},{2,18},{3,19},{4,20},{5,21},{6,22},{7,23},{8,24},{9,... | collective-permute-start | bytes 2663432 | tf_op jit(solution)/shard_map/ppermute | solution.py:65
  154.2 12.4 %collective-permute-start.25 = (bf16[272,1088]{1,0:T(8,128)(2,1)}, bf16[272,1088]{1,0:T(8,128)(2,1)S(1)}, u32[]{:S(2)}, u32[]{:S(2)}) collective-permute-start(bf16[272,1088]{1,0:T(8,128)(2,1)} %collective-permute-done.24), channel_id=1, source_target_pairs={{1,0},{2,1},{3,2},{5,4},{6,5},{7,6},{9,8},{10,9},{11,10},{13,12},{... | collective-permute-start | bytes 1775624 | tf_op jit(solution)/shard_map/ppermute | solution.py:65
  156.3 60.8 %collective-permute-start.19 = (bf16[4,136,1088]{2,1,0:T(8,128)(2,1)}, bf16[4,136,1088]{2,1,0:T(8,128)(2,1)}, u32[]{:S(2)}, u32[]{:S(2)}) collective-permute-start(bf16[4,136,1088]{2,1,0:T(8,128)(2,1)} %fusion.60), channel_id=1, source_target_pairs={{0,4},{1,5},{2,6},{3,7},{4,0},{5,1},{6,2},{7,3},{8,12},{9,13},{10,... | collective-permute-start | bytes 3551240 | tf_op jit(solution)/shard_map/ppermute | solution.py:65
  176.9 47.6 %collective-permute-start.31 = (bf16[544,1088]{1,0:T(8,128)(2,1)}, bf16[544,1088]{1,0:T(8,128)(2,1)}, u32[]{:S(2)}, u32[]{:S(2)}) collective-permute-start(bf16[544,1088]{1,0:T(8,128)(2,1)} %reshape.358), channel_id=1, source_target_pairs={{0,8},{1,9},{2,10},{3,11},{4,12},{5,13},{6,14},{7,15},{8,0},{9,1},... | collective-permute-start | bytes 3551240 | tf_op jit(solution)/shard_map/ppermute | solution.py:65
  177.4 50.1 %collective-permute-start.32 = (bf16[544,1088]{1,0:T(8,128)(2,1)}, bf16[544,1088]{1,0:T(8,128)(2,1)}, u32[]{:S(2)}, u32[]{:S(2)}) collective-permute-start(bf16[544,1088]{1,0:T(8,128)(2,1)} %reshape.358), channel_id=1, source_target_pairs={{0,16},{1,17},{2,18},{3,19},{4,20},{5,21},{6,22},{7,23},{8,24},{9,... | collective-permute-start | bytes 3551240 | tf_op jit(solution)/shard_map/ppermute | solution.py:65
  187.8 27.2 %collective-permute-start.11 = (bf16[136,1664]{1,0:T(8,128)(2,1)S(1)}, bf16[136,1664]{1,0:T(8,128)(2,1)S(1)}, u32[]{:S(2)}, u32[]{:S(2)}) collective-permute-start(bf16[136,1664]{1,0:T(8,128)(2,1)S(1)} %slice.238), channel_id=1, source_target_pairs={{0,16},{1,17},{2,18},{3,19},{4,20},{5,21},{6,22},{7,23},{8,24},{9,... | collective-permute-start | bytes 1357832 | tf_op jit(solution)/shard_map/ppermute | solution.py:65
  189.9 24.5 %collective-permute-start.12 = (bf16[136,1600]{1,0:T(8,128)(2,1)S(1)}, bf16[136,1600]{1,0:T(8,128)(2,1)S(1)}, u32[]{:S(2)}, u32[]{:S(2)}) collective-permute-start(bf16[136,1600]{1,0:T(8,128)(2,1)S(1)} %slice.239), channel_id=1, source_target_pairs={{0,8},{1,9},{2,10},{3,11},{4,12},{5,13},{6,14},{7,15},{8,0},{9,1},... | collective-permute-start | bytes 1305608 | tf_op jit(solution)/shard_map/ppermute | solution.py:65
  214.4 26.3 %collective-permute-start.26 = (bf16[136,4352]{1,0:T(8,128)(2,1)S(1)}, bf16[136,4352]{1,0:T(8,128)(2,1)S(1)}, u32[]{:S(2)}, u32[]{:S(2)}) collective-permute-start(bf16[136,4352]{1,0:T(8,128)(2,1)S(1)} %copy-done.48), channel_id=1, source_target_pairs={{0,8},{1,9},{2,10},{3,11},{4,12},{5,13},{6,14},{7,15},{8,0},{9,1},... | collective-permute-start | bytes 3551240 | tf_op jit(solution)/shard_map/ppermute | solution.py:65
  215.0 28.9 %collective-permute-start.27 = (bf16[136,4352]{1,0:T(8,128)(2,1)S(1)}, bf16[136,4352]{1,0:T(8,128)(2,1)S(1)}, u32[]{:S(2)}, u32[]{:S(2)}) collective-permute-start(bf16[136,4352]{1,0:T(8,128)(2,1)S(1)} %copy-done.48), channel_id=1, source_target_pairs={{0,16},{1,17},{2,18},{3,19},{4,20},{5,21},{6,22},{7,23},{8,24},{9,... | collective-permute-start | bytes 3551240 | tf_op jit(solution)/shard_map/ppermute | solution.py:65
  217.0 31.5 %collective-permute-start.13 = (bf16[4,136,3264]{2,1,0:T(8,128)(2,1)}, bf16[4,136,3264]{2,1,0:T(8,128)(2,1)S(1)}, u32[]{:S(2)}, u32[]{:S(2)}) collective-permute-start(bf16[4,136,3264]{2,1,0:T(8,128)(2,1)} %fusion.46), channel_id=1, source_target_pairs={{0,4},{1,5},{2,6},{3,7},{4,0},{5,1},{6,2},{7,3},{8,12},{9,13},{10,... | collective-permute-start | bytes 10653704 | tf_op jit(solution)/shard_map/ppermute | solution.py:65
  226.5 52.0 %collective-permute-start.33 = (bf16[544,640]{1,0:T(8,128)(2,1)}, bf16[544,640]{1,0:T(8,128)(2,1)}, u32[]{:S(2)}, u32[]{:S(2)}) collective-permute-start(bf16[544,640]{1,0:T(8,128)(2,1)} %slice.252), channel_id=1, source_target_pairs={{0,16},{1,17},{2,18},{3,19},{4,20},{5,21},{6,22},{7,23},{8,24},{9,... | collective-permute-start | bytes 2088968 | tf_op jit(solution)/shard_map/ppermute | solution.py:65
  229.5 49.1 %collective-permute-start.34 = (bf16[544,448]{1,0:T(8,128)(2,1)}, bf16[544,448]{1,0:T(8,128)(2,1)}, u32[]{:S(2)}, u32[]{:S(2)}) collective-permute-start(bf16[544,448]{1,0:T(8,128)(2,1)} %slice.253), channel_id=1, source_target_pairs={{0,8},{1,9},{2,10},{3,11},{4,12},{5,13},{6,14},{7,15},{8,0},{9,1},... | collective-permute-start | bytes 1462280 | tf_op jit(solution)/shard_map/ppermute | solution.py:65
  241.6 32.2 %collective-permute-start.28 = (bf16[136,2176]{1,0:T(8,128)(2,1)}, bf16[136,2176]{1,0:T(8,128)(2,1)}, u32[]{:S(2)}, u32[]{:S(2)}) collective-permute-start(bf16[136,2176]{1,0:T(8,128)(2,1)} %slice.250), channel_id=1, source_target_pairs={{0,16},{1,17},{2,18},{3,19},{4,20},{5,21},{6,22},{7,23},{8,24},{9,... | collective-permute-start | bytes 1775624 | tf_op jit(solution)/shard_map/ppermute | solution.py:65
  244.7 29.0 %collective-permute-start.29 = (bf16[136,2176]{1,0:T(8,128)(2,1)}, bf16[136,2176]{1,0:T(8,128)(2,1)}, u32[]{:S(2)}, u32[]{:S(2)}) collective-permute-start(bf16[136,2176]{1,0:T(8,128)(2,1)} %slice.251), channel_id=1, source_target_pairs={{0,8},{1,9},{2,10},{3,11},{4,12},{5,13},{6,14},{7,15},{8,0},{9,1},... | collective-permute-start | bytes 1775624 | tf_op jit(solution)/shard_map/ppermute | solution.py:65
  270.4 16.2 %collective-permute-start.14 = (bf16[2,512,1152]{2,1,0:T(8,128)(2,1)S(1)}, bf16[2,512,1152]{2,1,0:T(8,128)(2,1)}, u32[]{:S(2)}, u32[]{:S(2)}) collective-permute-start(bf16[2,512,1152]{2,1,0:T(8,128)(2,1)S(1)} %pad_maximum_fusion.4.own_ref), channel_id=1, source_target_pairs={{0,4},{1,5},{2,6},{3,7},{4,0},{5,1},{6,2},{7,3},{8,12},{9,13},{10,... | collective-permute-start | bytes 7077896 | tf_op jit(solution)/shard_map/ppermute | solution.py:65
  276.1 80.8 %collective-permute-start.30 = (bf16[4,136,4352]{2,1,0:T(8,128)(2,1)}, bf16[4,136,4352]{2,1,0:T(8,128)(2,1)}, u32[]{:S(2)}, u32[]{:S(2)}) collective-permute-start(bf16[4,136,4352]{2,1,0:T(8,128)(2,1)} %fusion.36), channel_id=1, source_target_pairs={{0,4},{1,5},{2,6},{3,7},{4,0},{5,1},{6,2},{7,3},{8,12},{9,13},{10,... | collective-permute-start | bytes 14204936 | tf_op jit(solution)/shard_map/ppermute | solution.py:65
  281.0 122.7 %collective-permute-start.35 = (bf16[4,544,1088]{2,1,0:T(8,128)(2,1)}, bf16[4,544,1088]{2,1,0:T(8,128)(2,1)}, u32[]{:S(2)}, u32[]{:S(2)}) collective-permute-start(bf16[4,544,1088]{2,1,0:T(8,128)(2,1)} %fusion.35), channel_id=1, source_target_pairs={{0,4},{1,5},{2,6},{3,7},{4,0},{5,1},{6,2},{7,3},{8,12},{9,13},{10,... | collective-permute-start | bytes 14204936 | tf_op jit(solution)/shard_map/ppermute | solution.py:65
  403.6 238.0 %collective-permute-start.59 = (bf16[2176,1088]{0,1:T(8,128)(2,1)}, bf16[2176,1088]{0,1:T(8,128)(2,1)}, u32[]{:S(2)}, u32[]{:S(2)}) collective-permute-start(bf16[2176,1088]{0,1:T(8,128)(2,1)} %convolution_convert_fusion), channel_id=1, source_target_pairs={{0,4},{1,5},{2,6},{3,7},{4,0},{5,1},{6,2},{7,3},{8,12},{9,13},{10,... | collective-permute-start | bytes 14204936 | tf_op jit(solution)/shard_map/ppermute | solution.py:65
  488.8 60.5 %collective-permute-start.40 = (bf16[2,512,1152]{2,1,0:T(8,128)(2,1)}, bf16[2,512,1152]{2,1,0:T(8,128)(2,1)}, u32[]{:S(2)}, u32[]{:S(2)}) collective-permute-start(bf16[2,512,1152]{2,1,0:T(8,128)(2,1)} %get-tuple-element.21), channel_id=1, source_target_pairs={{0,4},{1,5},{2,6},{3,7},{4,0},{5,1},{6,2},{7,3},{8,12},{9,13},{10,... | collective-permute-start | bytes 7077896 | tf_op jit(solution)/shard_map/ppermute | solution.py:65
  491.5 36.6 %collective-permute-start.64 = (bf16[544,1088]{1,0:T(8,128)(2,1)}, bf16[544,1088]{1,0:T(8,128)(2,1)}, u32[]{:S(2)}, u32[]{:S(2)}) collective-permute-start(bf16[544,1088]{1,0:T(8,128)(2,1)} %convolution_convert_fusion.3), channel_id=1, source_target_pairs={{0,4},{1,5},{2,6},{3,7},{4,0},{5,1},{6,2},{7,3},{8,12},{9,13},{10,... | collective-permute-start | bytes 3551240 | tf_op jit(solution)/shard_map/ppermute | solution.py:65
  512.5 14.1 %collective-permute-start.36 = (bf16[256,1088]{0,1:T(8,128)(2,1)S(1)}, bf16[256,1088]{0,1:T(8,128)(2,1)S(1)}, u32[]{:S(2)}, u32[]{:S(2)}) collective-permute-start(bf16[256,1088]{0,1:T(8,128)(2,1)S(1)} %bitcast.424), channel_id=1, source_target_pairs={{0,1},{1,0},{2,5},{3,4},{4,3},{5,2},{6,7},{7,6},{8,9},{9,8},{10,13... | collective-permute-start | bytes 1671176 | tf_op jit(solution)/shard_map/ppermute | solution.py:65
  513.7 14.4 %collective-permute-start.37 = (bf16[256,1088]{0,1:T(8,128)(2,1)S(1)}, bf16[256,1088]{0,1:T(8,128)(2,1)S(1)}, u32[]{:S(2)}, u32[]{:S(2)}) collective-permute-start(bf16[256,1088]{0,1:T(8,128)(2,1)S(1)} %bitcast.423), channel_id=1, source_target_pairs={{0,0},{1,1},{2,4},{3,5},{4,2},{5,3},{6,6},{7,7},{8,8},{9,9},{10,12... | collective-permute-start | bytes 1671176 | tf_op jit(solution)/shard_map/ppermute | solution.py:65
  526.6 136.8 %collective-permute-start.54 = (bf16[544,4352]{1,0:T(8,128)(2,1)}, bf16[544,4352]{1,0:T(8,128)(2,1)}, u32[]{:S(2)}, u32[]{:S(2)}) collective-permute-start(bf16[544,4352]{1,0:T(8,128)(2,1)} %convolution_convert_fusion.1), channel_id=1, source_target_pairs={{0,4},{1,5},{2,6},{3,7},{4,0},{5,1},{6,2},{7,3},{8,12},{9,13},{10,... | collective-permute-start | bytes 14204936 | tf_op jit(solution)/shard_map/ppermute | solution.py:65
  625.4 15.1 %collective-permute-start.41 = (bf16[256,1088]{0,1:T(8,128)(2,1)S(1)}, bf16[256,1088]{0,1:T(8,128)(2,1)S(1)}, u32[]{:S(2)}, u32[]{:S(2)}) collective-permute-start(bf16[256,1088]{0,1:T(8,128)(2,1)S(1)} %bitcast.421), channel_id=1, source_target_pairs={{0,1},{1,0},{2,5},{3,4},{4,3},{5,2},{6,7},{7,6},{8,9},{9,8},{10,13... | collective-permute-start | bytes 1671176 | tf_op jit(solution)/shard_map/ppermute | solution.py:65
  627.5 13.0 %collective-permute-start.42 = (bf16[256,1088]{0,1:T(8,128)(2,1)S(1)}, bf16[256,1088]{0,1:T(8,128)(2,1)S(1)}, u32[]{:S(2)}, u32[]{:S(2)}) collective-permute-start(bf16[256,1088]{0,1:T(8,128)(2,1)S(1)} %bitcast.422), channel_id=1, source_target_pairs={{0,0},{1,1},{2,4},{3,5},{4,2},{5,3},{6,6},{7,7},{8,8},{9,9},{10,12... | collective-permute-start | bytes 1671176 | tf_op jit(solution)/shard_map/ppermute | solution.py:65
  632.1 48.1 %collective-permute-start.43 = (bf16[544,3264]{1,0:T(8,128)(2,1)}, bf16[544,3264]{1,0:T(8,128)(2,1)}, u32[]{:S(2)}, u32[]{:S(2)}) collective-permute-start(bf16[544,3264]{1,0:T(8,128)(2,1)} %convolution_convert_fusion.2), channel_id=1, source_target_pairs={{0,4},{1,5},{2,6},{3,7},{4,0},{5,1},{6,2},{7,3},{8,12},{9,13},{10,... | collective-permute-start | bytes 10653704 | tf_op jit(solution)/shard_map/ppermute | solution.py:65
  660.4 51.1 %collective-permute-start.60 = (bf16[2,544,640]{2,1,0:T(8,128)(2,1)S(1)}, bf16[2,544,640]{2,1,0:T(8,128)(2,1)S(1)}, u32[]{:S(2)}, u32[]{:S(2)}) collective-permute-start(bf16[2,544,640]{2,1,0:T(8,128)(2,1)S(1)} %dynamic-slice_bitcast_fusion), channel_id=1, source_target_pairs={{0,8},{1,9},{2,10},{3,11},{4,12},{5,13},{6,14},{7,15},{8,0},{9,1},... | collective-permute-start | bytes 4177928 | tf_op jit(solution)/shard_map/ppermute | solution.py:65
  663.3 16.4 %collective-permute-start.62 = (bf16[2,544,448]{2,1,0:T(8,128)(2,1)S(1)}, bf16[2,544,448]{2,1,0:T(8,128)(2,1)S(1)}, u32[]{:S(2)}, u32[]{:S(2)}) collective-permute-start(bf16[2,544,448]{2,1,0:T(8,128)(2,1)S(1)} %dynamic-slice_bitcast_fusion.4), channel_id=1, source_target_pairs={{0,16},{1,17},{2,18},{3,19},{4,20},{5,21},{6,22},{7,23},{8,24},{9,... | collective-permute-start | bytes 2924552 | tf_op jit(solution)/shard_map/ppermute | solution.py:65
  668.3 40.0 %collective-permute-start.55 = (bf16[2,136,2176]{2,1,0:T(8,128)(2,1)S(1)}, bf16[2,136,2176]{2,1,0:T(8,128)(2,1)S(1)}, u32[]{:S(2)}, u32[]{:S(2)}) collective-permute-start(bf16[2,136,2176]{2,1,0:T(8,128)(2,1)S(1)} %dynamic-slice_bitcast_fusion.3), channel_id=1, source_target_pairs={{0,8},{1,9},{2,10},{3,11},{4,12},{5,13},{6,14},{7,15},{8,0},{9,1},... | collective-permute-start | bytes 3551240 | tf_op jit(solution)/shard_map/ppermute | solution.py:65
  670.5 40.5 %collective-permute-start.57 = (bf16[2,136,2176]{2,1,0:T(8,128)(2,1)S(1)}, bf16[2,136,2176]{2,1,0:T(8,128)(2,1)S(1)}, u32[]{:S(2)}, u32[]{:S(2)}) collective-permute-start(bf16[2,136,2176]{2,1,0:T(8,128)(2,1)S(1)} %dynamic-slice_bitcast_fusion.2), channel_id=1, source_target_pairs={{0,16},{1,17},{2,18},{3,19},{4,20},{5,21},{6,22},{7,23},{8,24},{9,... | collective-permute-start | bytes 3551240 | tf_op jit(solution)/shard_map/ppermute | solution.py:65
  680.1 40.2 %collective-permute-start.63 = (bf16[544,448]{1,0:T(8,128)(2,1)S(1)}, bf16[544,448]{1,0:T(8,128)(2,1)S(1)}, u32[]{:S(2)}, u32[]{:S(2)}) collective-permute-start(bf16[544,448]{1,0:T(8,128)(2,1)S(1)} %dynamic-slice_bitcast_fusion.11), channel_id=1, source_target_pairs={{0,8},{1,9},{2,10},{3,11},{4,12},{5,13},{6,14},{7,15},{8,0},{9,1},... | collective-permute-start | bytes 1462280 | tf_op jit(solution)/shard_map/ppermute | solution.py:65
  686.0 107.9 %collective-permute-start.44 = (bf16[2,136,1664]{2,1,0:T(8,128)(2,1)}, bf16[2,136,1664]{2,1,0:T(8,128)(2,1)}, u32[]{:S(2)}, u32[]{:S(2)}) collective-permute-start(bf16[2,136,1664]{2,1,0:T(8,128)(2,1)} %dynamic-slice_bitcast_fusion.7), channel_id=1, source_target_pairs={{0,8},{1,9},{2,10},{3,11},{4,12},{5,13},{6,14},{7,15},{8,0},{9,1},... | collective-permute-start | bytes 2715656 | tf_op jit(solution)/shard_map/ppermute | solution.py:65
  708.3 81.7 %collective-permute-start.46 = (bf16[2,136,1600]{2,1,0:T(8,128)(2,1)}, bf16[2,136,1600]{2,1,0:T(8,128)(2,1)}, u32[]{:S(2)}, u32[]{:S(2)}) collective-permute-start(bf16[2,136,1600]{2,1,0:T(8,128)(2,1)} %dynamic-slice_bitcast_fusion.6), channel_id=1, source_target_pairs={{0,16},{1,17},{2,18},{3,19},{4,20},{5,21},{6,22},{7,23},{8,24},{9,... | collective-permute-start | bytes 2611208 | tf_op jit(solution)/shard_map/ppermute | solution.py:65
  711.0 21.2 %collective-permute-start.56 = (bf16[136,2176]{1,0:T(8,128)(2,1)S(1)}, bf16[136,2176]{1,0:T(8,128)(2,1)S(1)}, u32[]{:S(2)}, u32[]{:S(2)}) collective-permute-start(bf16[136,2176]{1,0:T(8,128)(2,1)S(1)} %dynamic-slice_bitcast_fusion.10), channel_id=1, source_target_pairs={{0,16},{1,17},{2,18},{3,19},{4,20},{5,21},{6,22},{7,23},{8,24},{9,... | collective-permute-start | bytes 1775624 | tf_op jit(solution)/shard_map/ppermute | solution.py:65
  711.5 40.9 %collective-permute-start.58 = (bf16[136,2176]{1,0:T(8,128)(2,1)S(1)}, bf16[136,2176]{1,0:T(8,128)(2,1)S(1)}, u32[]{:S(2)}, u32[]{:S(2)}) collective-permute-start(bf16[136,2176]{1,0:T(8,128)(2,1)S(1)} %dynamic-slice_bitcast_fusion.9), channel_id=1, source_target_pairs={{0,8},{1,9},{2,10},{3,11},{4,12},{5,13},{6,14},{7,15},{8,0},{9,1},... | collective-permute-start | bytes 1775624 | tf_op jit(solution)/shard_map/ppermute | solution.py:65
  720.3 34.8 %collective-permute-start.61 = (bf16[544,640]{1,0:T(8,128)(2,1)}, bf16[544,640]{1,0:T(8,128)(2,1)}, u32[]{:S(2)}, u32[]{:S(2)}) collective-permute-start(bf16[544,640]{1,0:T(8,128)(2,1)} %dynamic-slice_bitcast_fusion.8), channel_id=1, source_target_pairs={{0,16},{1,17},{2,18},{3,19},{4,20},{5,21},{6,22},{7,23},{8,24},{9,... | collective-permute-start | bytes 2088968 | tf_op jit(solution)/shard_map/ppermute | solution.py:65
  782.5 28.0 %collective-permute-start.69 = (bf16[136,2448]{1,0:T(8,128)(2,1)}, bf16[136,2448]{1,0:T(8,128)(2,1)S(1)}, u32[]{:S(2)}, u32[]{:S(2)}) collective-permute-start(bf16[136,2448]{1,0:T(8,128)(2,1)} %bitcast.372), channel_id=1, source_target_pairs={{3,2},{7,6},{11,10},{15,14},{19,18},{23,22},{27,26},{31,30}} | collective-permute-start | bytes 1997576 | tf_op jit(solution)/shard_map/ppermute | solution.py:65
  784.2 27.2 %collective-permute-start.72 = (bf16[136,2448]{1,0:T(8,128)(2,1)}, bf16[136,2448]{1,0:T(8,128)(2,1)S(1)}, u32[]{:S(2)}, u32[]{:S(2)}) collective-permute-start(bf16[136,2448]{1,0:T(8,128)(2,1)} %bitcast.371), channel_id=1, source_target_pairs={{0,1},{4,5},{8,9},{12,13},{16,17},{20,21},{24,25},{28,29}} | collective-permute-start | bytes 1997576 | tf_op jit(solution)/shard_map/ppermute | solution.py:65
  810.7 14.8 %collective-permute-start.70 = (bf16[136,2448]{1,0:T(8,128)(2,1)S(1)}, bf16[136,2448]{1,0:T(8,128)(2,1)S(1)}, u32[]{:S(2)}, u32[]{:S(2)}) collective-permute-start(bf16[136,2448]{1,0:T(8,128)(2,1)S(1)} %fusion.31), channel_id=1, source_target_pairs={{2,1},{3,2},{6,5},{7,6},{10,9},{11,10},{14,13},{15,14},{18,17},{19... | collective-permute-start | bytes 1997576 | tf_op jit(solution)/shard_map/ppermute | solution.py:65
  811.6 15.5 %collective-permute-start.73 = (bf16[136,2448]{1,0:T(8,128)(2,1)S(1)}, bf16[136,2448]{1,0:T(8,128)(2,1)S(1)}, u32[]{:S(2)}, u32[]{:S(2)}) collective-permute-start(bf16[136,2448]{1,0:T(8,128)(2,1)S(1)} %fusion.29), channel_id=1, source_target_pairs={{0,1},{1,2},{4,5},{5,6},{8,9},{9,10},{12,13},{13,14},{16,17},{17,1... | collective-permute-start | bytes 1997576 | tf_op jit(solution)/shard_map/ppermute | solution.py:65
  813.6 10.4 %collective-permute-start.49 = (bf16[136,816]{1,0:T(8,128)(2,1)S(1)}, bf16[136,816]{1,0:T(8,128)(2,1)S(1)}, u32[]{:S(2)}, u32[]{:S(2)}) collective-permute-start(bf16[136,816]{1,0:T(8,128)(2,1)S(1)} %fusion.53), channel_id=1, source_target_pairs={{2,1},{3,2},{6,5},{7,6},{10,9},{11,10},{14,13},{15,14},{18,17},{19... | collective-permute-start | bytes 665864 | tf_op jit(solution)/shard_map/ppermute | solution.py:65
  814.4 29.4 %collective-permute-start.52 = (bf16[136,816]{1,0:T(8,128)(2,1)S(1)}, bf16[136,816]{1,0:T(8,128)(2,1)S(1)}, u32[]{:S(2)}, u32[]{:S(2)}) collective-permute-start(bf16[136,816]{1,0:T(8,128)(2,1)S(1)} %fusion.51), channel_id=1, source_target_pairs={{0,1},{1,2},{4,5},{5,6},{8,9},{9,10},{12,13},{13,14},{16,17},{17,1... | collective-permute-start | bytes 665864 | tf_op jit(solution)/shard_map/ppermute | solution.py:65
  824.1 25.2 %collective-permute-start.50 = (bf16[136,816]{1,0:T(8,128)(2,1)S(1)}, bf16[136,816]{1,0:T(8,128)(2,1)S(1)}, u32[]{:S(2)}, u32[]{:S(2)}) collective-permute-start(bf16[136,816]{1,0:T(8,128)(2,1)S(1)} %fusion.54), channel_id=1, source_target_pairs={{1,0},{2,1},{3,2},{5,4},{6,5},{7,6},{9,8},{10,9},{11,10},{13,12},{... | collective-permute-start | bytes 665864 | tf_op jit(solution)/shard_map/ppermute | solution.py:65
  825.6 38.7 %collective-permute-start.71 = (bf16[136,2448]{1,0:T(8,128)(2,1)S(1)}, bf16[136,2448]{1,0:T(8,128)(2,1)S(1)}, u32[]{:S(2)}, u32[]{:S(2)}) collective-permute-start(bf16[136,2448]{1,0:T(8,128)(2,1)S(1)} %fusion.32), channel_id=1, source_target_pairs={{1,0},{2,1},{3,2},{5,4},{6,5},{7,6},{9,8},{10,9},{11,10},{13,12},{... | collective-permute-start | bytes 1997576 | tf_op jit(solution)/shard_map/ppermute | solution.py:65
  827.2 37.1 %collective-permute-start.74 = (bf16[136,2448]{1,0:T(8,128)(2,1)S(1)}, bf16[136,2448]{1,0:T(8,128)(2,1)S(1)}, u32[]{:S(2)}, u32[]{:S(2)}) collective-permute-start(bf16[136,2448]{1,0:T(8,128)(2,1)S(1)} %fusion.30), channel_id=1, source_target_pairs={{0,1},{1,2},{2,3},{4,5},{5,6},{6,7},{8,9},{9,10},{10,11},{12,13},{... | collective-permute-start | bytes 1997576 | tf_op jit(solution)/shard_map/ppermute | solution.py:65
  843.8 19.6 %collective-permute-start.53 = (bf16[136,816]{1,0:T(8,128)(2,1)S(1)}, bf16[136,816]{1,0:T(8,128)(2,1)S(1)}, u32[]{:S(2)}, u32[]{:S(2)}) collective-permute-start(bf16[136,816]{1,0:T(8,128)(2,1)S(1)} %fusion.52), channel_id=1, source_target_pairs={{0,1},{1,2},{2,3},{4,5},{5,6},{6,7},{8,9},{9,10},{10,11},{12,13},{... | collective-permute-start | bytes 665864 | tf_op jit(solution)/shard_map/ppermute | solution.py:65
  (100 other events, 1454.8 us)

commit v2 on v1

--- a/solution.py
+++ b/solution.py
@@ -1,3 +1,4 @@
+import math
 from functools import partial
 
 import jax
@@ -357,6 +358,818 @@
     )(kinfo, qinfo, queries, own, sib, grad, lse)
 
 
+MESH = pl.DeviceIdType.MESH
+
+
+class Sizes:
+    def __init__(self, width, hidden, ctx, dp, length):
+        self.width = width
+        self.wide = -(-width // LANES) * LANES
+        self.ctx = ctx
+        self.rows = 2 * width // dp
+        self.qkv = 3 * width // ctx
+        self.out = width // ctx
+        self.cols = -(-(self.qkv + self.out) // LANES) * LANES
+        self.up = hidden // ctx
+        self.half = length // 2
+        self.pairs = self.wide // LANES
+        self.out_tile = self.qkv // LANES * LANES
+        self.qkv_cols = 1024
+
+    def qkv_runs(self, z):
+        runs, at = [], z * self.qkv
+        end = at + self.qkv
+        while at < end:
+            kind = at // self.width
+            stop = min(end, (kind + 1) * self.width)
+            runs.append((at - z * self.qkv, kind * self.wide + at - kind * self.width, stop - at))
+            at = stop
+        return runs
+
+
+class Net:
+    def __init__(self):
+        self.d = lax.axis_index("dp")
+        self.z = lax.axis_index("ctx")
+        self.c = self.d % 2
+        self.p = self.d // 2
+        y, x = self.p // 2, self.p % 2
+        self.px, self.py, self.pd = 2 * y + 1 - x, 2 * (1 - y) + x, 2 * (1 - y) + 1 - x
+        self.x_to = (2 * self.px + self.c, self.z)
+        self.y_to = (2 * self.py + self.c, self.z)
+        self.sib = (2 * self.p + 1 - self.c, self.z)
+        self.near = self.c + 2 * (self.z // 2)
+        self.far = self.c + 2 * (1 - self.z // 2)
+
+
+def enter(net):
+    gate = pltpu.get_barrier_semaphore()
+    for c in range(2):
+        for z in range(4):
+
+            @pl.when((c != net.c) | (z != net.z))
+            def _():
+                pl.semaphore_signal(gate, inc=1, device_id=(2 * net.p + c, z), device_id_type=MESH)
+
+    for to in (net.x_to, net.y_to):
+        pl.semaphore_signal(gate, inc=1, device_id=to, device_id_type=MESH)
+    pl.semaphore_wait(gate, 9)
+
+
+class Gather:
+    def __init__(self, net, sizes, w, own, swapped, sems):
+        self.n, self.s, self.w, self.own, self.swapped = net, sizes, w, own, swapped
+        self.zs, self.zr, self.hs, self.hr, self.cs, self.cr, self.loc = sems
+
+    def at(self, p, z):
+        r, c = (z, p) if self.swapped else (p, z)
+        s = self.s
+        return self.w.at[
+            pl.ds(pl.multiple_of(r * s.rows, 16), s.rows),
+            pl.ds(pl.multiple_of(c * s.cols, LANES), s.cols),
+        ]
+
+    def copy(self, p, z, send, recv, to):
+        block = self.at(p, z)
+        return pltpu.make_async_remote_copy(
+            block, block, send, recv, device_id=to, device_id_type=MESH
+        )
+
+    def zcopy(self, z, up):
+        n = self.n
+        to = (n.d, n.z + 1 if up else n.z - 1)
+        return self.copy(n.p, z, self.zs.at[z // 2, int(up)], self.zr.at[z // 2], to)
+
+    def hop(self, p, z, to, k):
+        return self.copy(p, z, self.hs.at[z // 2, k], self.hr.at[z // 2, k], to)
+
+    def across(self, p, z):
+        return self.copy(p, z, self.cs.at[p, z // 2], self.cr.at[p, z // 2], self.n.sib)
+
+    def begin(self):
+        n = self.n
+
+        @pl.when(n.z % 2 == n.c)
+        def _():
+            local = pltpu.make_async_copy(self.own, self.at(n.p, n.z), self.loc)
+            local.start()
+            local.wait()
+
+            @pl.when(n.z < 3)
+            def _():
+                self.zcopy(n.z, True).start()
+
+            @pl.when(n.z > 0)
+            def _():
+                self.zcopy(n.z, False).start()
+
+    def arrive(self, z):
+        n = self.n
+
+        @pl.when(z != n.z)
+        def _():
+            self.zcopy(z, True).wait_recv()
+
+            @pl.when((z < n.z) & (n.z < 3))
+            def _():
+                self.zcopy(z, True).start()
+
+            @pl.when((z > n.z) & (n.z > 0))
+            def _():
+                self.zcopy(z, False).start()
+
+        self.hop(n.p, z, n.x_to, 0).start()
+        self.hop(n.p, z, n.y_to, 1).start()
+        self.across(n.p, z).start()
+
+    def turn(self, z):
+        n = self.n
+        self.hop(n.px, z, n.x_to, 0).wait_recv()
+
+        @pl.when(z < 2)
+        def _():
+            self.hop(n.px, z, n.y_to, 2).start()
+
+        self.across(n.px, z).start()
+        self.hop(n.py, z, n.y_to, 1).wait_recv()
+
+        @pl.when(z >= 2)
+        def _():
+            self.hop(n.py, z, n.x_to, 2).start()
+
+        self.across(n.py, z).start()
+
+    def last(self, z):
+        n = self.n
+        self.hop(n.pd, z, n.x_to, 2).wait_recv()
+        self.across(n.pd, z).start()
+
+    def ready(self):
+        n = self.n
+        for half in range(2):
+            for p in range(4):
+                self.across(p, 1 - n.c + 2 * half).wait_recv()
+
+    def drain(self):
+        n = self.n
+        for half in range(2):
+            z = n.c + 2 * half
+
+            @pl.when((z <= n.z) & (n.z < 3))
+            def _():
+                self.zcopy(z, True).wait_send()
+
+            @pl.when((z >= n.z) & (n.z > 0))
+            def _():
+                self.zcopy(z, False).wait_send()
+
+            for k, to in enumerate((n.x_to, n.y_to, n.x_to)):
+                self.hop(n.p, z, to, k).wait_send()
+            for p in range(4):
+                self.across(p, z).wait_send()
+
+
+def gather_sems():
+    dma = pltpu.SemaphoreType.DMA
+    return [dma((2, 2)), dma((2,)), dma((2, 3)), dma((2, 3)), dma((4, 2)), dma((4, 2)), dma]
+
+
+class ToSequences:
+    def __init__(self, net, src, dst, sems):
+        self.n, self.src, self.dst = net, src, dst
+        self.ss, self.rs = sems
+        self.rows = src.shape[1]
+
+    def parts(self):
+        n = self.n
+        for j in range(2):
+            to = (2 * n.p + n.z // 2, 2 * n.c + j)
+            yield j, to, (to[0] == n.d) & (to[1] == n.z)
+
+    def place(self, t):
+        return self.dst.at[pl.ds(pl.multiple_of(t * self.rows, 16), self.rows)]
+
+    def remote(self, j, to):
+        t = self.n.z % 2
+        return pltpu.make_async_remote_copy(
+            self.src.at[j],
+            self.place(t),
+            self.ss.at[j],
+            self.rs.at[t],
+            device_id=to,
+            device_id_type=MESH,
+        )
+
+    def start(self):
+        for j, to, here in self.parts():
+
+            @pl.when(here)
+            def _():
+                t = self.n.z % 2
+                pltpu.make_async_copy(self.src.at[j], self.place(t), self.rs.at[t]).start()
+
+            @pl.when(jnp.logical_not(here))
+            def _():
+                self.remote(j, to).start()
+
+    def wait(self):
+        for t in range(2):
+            pltpu.make_async_copy(self.src.at[0], self.place(t), self.rs.at[t]).wait()
+
+    def drain(self):
+        for j, to, here in self.parts():
+
+            @pl.when(jnp.logical_not(here))
+            def _():
+                self.remote(j, to).wait_send()
+
+
+class FromSequences:
+    def __init__(self, net, src, dst, sems):
+        self.n, self.src, self.dst = net, src, dst
+        self.ss, self.rs = sems
+        self.rows = dst.shape[1]
+
+    def parts(self):
+        n = self.n
+        for t in range(2):
+            to = (2 * n.p + n.z // 2, 2 * n.c + t)
+            yield t, to, (to[0] == n.d) & (to[1] == n.z)
+
+    def piece(self, t):
+        return self.src.at[pl.ds(t * self.rows, self.rows)]
+
+    def remote(self, t, to):
+        j = self.n.z % 2
+        return pltpu.make_async_remote_copy(
+            self.piece(t),
+            self.dst.at[j],
+            self.ss.at[t],
+            self.rs.at[j],
+            device_id=to,
+            device_id_type=MESH,
+        )
+
+    def start(self):
+        for t, to, here in self.parts():
+
+            @pl.when(here)
+            def _():
+                j = self.n.z % 2
+                pltpu.make_async_copy(self.piece(t), self.dst.at[j], self.rs.at[j]).start()
+
+            @pl.when(jnp.logical_not(here))
+            def _():
+                self.remote(t, to).start()
+
+    def wait(self):
+        for j in range(2):
+            pltpu.make_async_copy(self.piece(0), self.dst.at[j], self.rs.at[j]).wait()
+
+    def drain(self):
+        for t, to, here in self.parts():
+
+            @pl.when(jnp.logical_not(here))
+            def _():
+                self.remote(t, to).wait_send()
+
+
+def by_rows(total, step, body):
+    def one(i, carry):
+        body(pl.ds(pl.multiple_of(i * step, step), step))
+        return carry
+
+    lax.fori_loop(0, total // step, one, 0)
+
+
+def by_columns(total, body, step=256):
+    def one(i, carry):
+        body(pl.multiple_of(i * step, LANES), step)
+        return carry
+
+    lax.fori_loop(0, total // step, one, 0)
+    if total % step:
+        body(total // step * step, total % step)
+
+
+def normalised(values):
+    average = jnp.mean(values, axis=-1, keepdims=True)
+    centred = values - average
+    variance = jnp.mean(centred * centred, axis=-1, keepdims=True)
+    return centred * lax.rsqrt(variance + eps_norm)
+
+
+def place_run(block, source, phase, count):
+    moved = pltpu.roll(block, (phase - source) % block.shape[1], axis=1)
+    tiles = -(-(phase + count) // LANES) * LANES
+    moved = moved[:, :tiles]
+    lane = lax.broadcasted_iota(jnp.int32, moved.shape, 1)
+    return jnp.where((lane >= phase) & (lane < phase + count), moved, 0.0)
+
+
+def attend_pair(s, i, q_ref, kv_ref, bias_ref, att_ref, lse_ref, top_ref):
+    lanes = pl.ds(pl.multiple_of(i * LANES, LANES), LANES)
+    keys, values, queries = kv_ref[0, :, lanes], kv_ref[1, :, lanes], q_ref[:, lanes]
+    lane = lax.broadcasted_iota(jnp.int32, queries.shape, 1)
+    outs = []
+    for side in range(2):
+        mine = (lane >= HD) if side else (lane < HD)
+        picked = jnp.where(mine, queries, jnp.zeros_like(queries)) * bf16(HD**-0.5)
+        scores = nt(keys, picked) + bias_ref[...]
+        top = jnp.max(scores, axis=0, keepdims=True)
+        weights = jnp.exp(scores - top)
+        total = jnp.sum(weights, axis=0, keepdims=True)
+        mixed = tn(values[:, side * HD : (side + 1) * HD], weights.astype(bf16))
+        outs.append(mixed * (1.0 / total))
+        lse_ref[i, side : side + 1, :] = top + jnp.log(total)
+        top_ref[i, side : side + 1, :] = top
+    att_ref[:, lanes] = jnp.concatenate(outs, axis=0).T.astype(bf16)
+
+
+def forward_kernel(s, *refs):
+    (own_a, own_b, own_c, small, inp, cot, kinfo, qinfo) = refs[:8]
+    (wa, wb, wc, x_o, cot_o, vec, normed_o, q_o, kv_o, att_o, res_o, two_o, slope_o, hid_o) = refs[8:22]
+    (lse, top, out_o) = refs[22:25]
+    (x, normed, pre, q, kv, bias, att, res, two, slope, hid, wt, ct, out, smalls) = refs[25:40]
+    sems = refs[40:]
+    net = Net()
+    A, B, C = [
+        Gather(net, s, w, own, swapped, sems[7 * g : 7 * g + 7])
+        for g, (w, own, swapped) in enumerate(
+            ((wa, own_a, False), (wb, own_b, False), (wc, own_c, True))
+        )
+    ]
+    seq_x = ToSequences(net, inp, x, sems[21:23])
+    seq_cot = ToSequences(net, cot, cot_o, sems[23:25])
+    seq_out = FromSequences(net, out, out_o, sems[25:27])
+    small_s, small_r, kv_s, kv_r, load, save = sems[27:33]
+    near, far = net.near, net.far
+    saves = []
+
+    def keep(src, dst):
+        copy = pltpu.make_async_copy(src, dst, save.at[len(saves)])
+        copy.start()
+        saves.append(copy)
+
+    def small_copy(z):
+        return pltpu.make_async_remote_copy(
+            small,
+            smalls.at[net.z],
+            small_s.at[z],
+            small_r.at[net.z],
+            device_id=(net.d, z),
+            device_id_type=MESH,
+        )
+
+    enter(net)
+    A.begin()
+    for z in range(4):
+
+        @pl.when(z != net.z)
+        def _():
+            small_copy(z).start()
+
+        @pl.when(z == net.z)
+        def _():
+            pltpu.make_async_copy(small, smalls.at[z], small_r.at[z]).start()
+
+    A.arrive(near)
+    seq_x.start()
+    A.arrive(far)
+    B.begin()
+    diff = qinfo[0:1, :] - kinfo[:, 0:1]
+    fine = (diff >= 0) & (diff <= kinfo[:, 1:2])
+    bias[...] = jnp.where(fine, 0.0, masked_fill)
+    A.turn(near)
+    B.arrive(near)
+
+    for z in range(4):
+        pltpu.make_async_copy(small, smalls.at[z], small_r.at[z]).wait()
+    row = lax.broadcasted_iota(jnp.int32, (3 * LANES, s.wide), 0)
+    col = lax.broadcasted_iota(jnp.int32, (3 * LANES, s.wide), 1)
+    rows = 0.0
+    for z in range(4):
+        spread = jnp.where((col == row + z * s.out) & (row < s.out), 1.0, 0.0).astype(bf16)
+        rows = rows + product(smalls[z, :, : 3 * LANES], spread)
+    vec[...] = rows
+
+    seq_x.wait()
+    keep(x, x_o)
+    by_rows(
+        s.half,
+        LANES,
+        lambda r: normed.__setitem__(
+            (r, slice(None)),
+            to_low(
+                normalised(x[r, :].astype(f32)) * vec[0:1, : s.width] + vec[1:2, : s.width]
+            ),
+        ),
+    )
+    keep(normed, normed_o)
+    A.turn(far)
+    A.last(near)
+    B.arrive(far)
+    A.last(far)
+    C.begin()
+    pre[...] = jnp.zeros_like(pre)
+    A.ready()
+
+    def tile_a(z):
+        return pltpu.make_async_copy(
+            wa.at[:, pl.ds(z * s.cols, s.cols)], wt.at[z % 2], load.at[z % 2]
+        )
+
+    def tile_b(z):
+        return pltpu.make_async_copy(
+            wb.at[:, pl.ds(z * s.cols, s.cols)], wt.at[z % 2], load.at[z % 2]
+        )
+
+    tile_a(0).start()
+    for z in range(4):
+        if z < 3:
+            tile_a(z + 1).start()
+        tile_a(z).wait()
+
+        def part(start, size):
+            res[:, pl.ds(start, size)] = product(normed[...], wt[z % 2, :, pl.ds(start, size)])
+
+        by_columns(s.qkv_cols, part)
+        for source, target, count in s.qkv_runs(z):
+            base = target // LANES * LANES
+            moved = place_run(res[:, : s.qkv_cols], source, target - base, count)
+            pre[:, base : base + moved.shape[1]] += moved
+        if z == 1:
+            seq_cot.start()
+    tile_a(0).start()
+    kv[0, : s.half, :] = to_low(pre[:, s.wide : 2 * s.wide])
+    kv[1, : s.half, :] = to_low(pre[:, 2 * s.wide :] + vec[3:4, :])
+    share = pltpu.make_async_remote_copy(
+        kv.at[:, pl.ds(0, s.half)],
+        kv.at[:, pl.ds(s.half, s.half)],
+        kv_s,
+        kv_r,
+        device_id=net.sib,
+        device_id_type=MESH,
+    )
+    share.start()
+    q[...] = to_low(pre[:, : s.wide] + vec[2:3, :])
+    B.turn(near)
+    C.arrive(near)
+    share.wait()
+    keep(q, q_o)
+    keep(kv, kv_o)
+
+    def pair(i, carry):
+        attend_pair(s, i, q, kv, bias, att, lse, top)
+
+        @pl.when(i == 1)
+        def _():
+            B.turn(far)
+            B.last(near)
+
+        @pl.when(i == 4)
+        def _():
+            C.arrive(far)
+
+        @pl.when(i == 6)
+        def _():
+            B.last(far)
+
+        return carry
+
+    lax.fori_loop(0, s.pairs, pair, 0)
+    keep(att, att_o)
+    C.turn(near)
+
+    res[...] = jnp.zeros_like(res)
+    for z in range(4):
+        if z < 3:
+            tile_a(z + 1).start()
+        tile_a(z).wait()
+        block = product(att[:, : s.width], wt[z % 2, :, s.out_tile :])
+        target = z * s.out
+        base = target // LANES * LANES
+        moved = place_run(block, s.qkv - s.out_tile, target - base, s.out)
+        res[:, base : base + moved.shape[1]] += moved
+    B.ready()
+    tile_b(0).start()
+
+    def second(r):
+        total = res[r, : s.width] + x[r, :].astype(f32) + vec[4:5, : s.width]
+        res[r, : s.width] = total
+        two[r, :] = to_low(normalised(total) * vec[5:6, : s.width] + vec[6:7, : s.width])
+
+    by_rows(s.half, LANES, second)
+    keep(res, res_o)
+    keep(two, two_o)
+
+    for z in range(4):
+        if z < 3:
+            tile_b(z + 1).start()
+        tile_b(z).wait()
+
+        def part(start, size):
+            u = product(two[...], wt[z % 2, :, pl.ds(start, size)])
+            u = u + smalls[z, 8:9, pl.ds(start, size)].astype(f32)
+            inner = math.sqrt(2 / math.pi) * (u + 0.044715 * u * u * u)
+            t = jnp.tanh(inner)
+            bend = math.sqrt(2 / math.pi) * (1 + 3 * 0.044715 * u * u)
+            lanes = pl.ds(pl.multiple_of(z * s.cols + start, LANES), size)
+            hid[:, lanes] = to_low(0.5 * u * (1 + t))
+            slope[:, lanes] = to_low(0.5 * (1 + t) + 0.5 * u * (1 - t * t) * bend)
+
+        by_columns(s.cols, part)
+        if z == 1:
+            C.turn(far)
+            C.last(near)
+    keep(hid, hid_o)
+    keep(slope, slope_o)
+    C.last(far)
+    C.ready()
+
+    def tile_c(k):
+        count = min(3 * LANES, s.width - k * 3 * LANES)
+        return pltpu.make_async_copy(
+            wc.at[pl.ds(k * 3 * LANES, count)], ct.at[k % 2, pl.ds(0, count)], load.at[k % 2]
+        )
+
+    tile_c(0).start()
+    for k in range(3):
+        if k < 2:
+            tile_c(k + 1).start()
+        tile_c(k).wait()
+        at, count = k * 3 * LANES, min(3 * LANES, s.width - k * 3 * LANES)
+        block = nt(hid[...], ct[k % 2, :count, :])
+        total = res[:, at : at + count] + block + vec[7:8, at : at + count]
+        out[:, at : at + count] = to_low(total)
+    seq_out.start()
+    seq_cot.wait()
+    for group in (A, B, C):
+        group.drain()
+    for z in range(4):
+
+        @pl.when(z != net.z)
+        def _():
+            small_copy(z).wait_send()
+
+    seq_x.drain()
+    seq_cot.drain()
+    for copy in saves:
+        copy.wait()
+    seq_out.wait()
+    seq_out.drain()
+
+
+def forward_call(s, own_a, own_b, own_c, small, inp, cot, kinfo, qinfo):
+    dma = pltpu.SemaphoreType.DMA
+    rows = s.half
+    full = s.ctx * s.cols
+
+    def low(*shape):
+        return jax.ShapeDtypeStruct(shape, bf16)
+
+    def high(*shape):
+        return jax.ShapeDtypeStruct(shape, f32)
+
+    out_shape = [low(s.width, full)] * 3 + [
+        low(rows, s.width),
+        low(rows, s.width),
+        high(16, s.wide),
+        low(rows, s.width),
+        low(rows, s.wide),
+        low(2, 2 * rows, s.wide),
+        low(rows, s.wide),
+        high(rows, s.wide),
+        low(rows, s.width),
+        low(rows, full),
+        low(rows, full),
+        high(s.pairs, 2, rows),
+        high(s.pairs, 2, rows),
+        low(*inp.shape),
+    ]
+    anywhere = pl.BlockSpec(memory_space=pl.ANY)
+    local = pl.BlockSpec(memory_space=pltpu.VMEM)
+    out_specs = [local if i in (5, 14, 15) else anywhere for i in range(len(out_shape))]
+    return pl.pallas_call(
+        partial(forward_kernel, s),
+        out_shape=out_shape,
+        in_specs=[anywhere] * 6 + [local] * 2,
+        out_specs=out_specs,
+        scratch_shapes=[
+            pltpu.VMEM((rows, s.width), bf16),
+            pltpu.VMEM((rows, s.width), bf16),
+            pltpu.VMEM((rows, 3 * s.wide), f32),
+            pltpu.VMEM((rows, s.wide), bf16),
+            pltpu.VMEM((2, 2 * rows, s.wide), bf16),
+            pltpu.VMEM((2 * rows, rows), f32),
+            pltpu.VMEM((rows, s.wide), bf16),
+            pltpu.VMEM((rows, s.wide), f32),
+            pltpu.VMEM((rows, s.width), bf16),
+            pltpu.VMEM((rows, full), bf16),
+            pltpu.VMEM((rows, full), bf16),
+            pltpu.VMEM((2, s.width, s.cols), bf16),
+            pltpu.VMEM((2, 3 * LANES, full), bf16),
+            pltpu.VMEM((rows, s.width), bf16),
+            pltpu.VMEM((4, 16, s.wide), bf16),
+        ]
+        + gather_sems() * 3
+        + [dma((2,))] * 6
+        + [dma((4,)), dma((4,)), dma, dma, dma((2,)), dma((12,))],
+        compiler_params=pltpu.CompilerParams(
+            collective_id=1, has_side_effects=True, vmem_limit_bytes=61 * 2**20
+        ),
+        name="forward",
+    )(own_a, own_b, own_c, small, inp, cot, kinfo, qinfo)
+
+
+def slot_info(moves, segment_ids, padding, stretch_order):
+    core, place, local_seqs = moves.core, moves.z, segment_ids.shape[0]
+    length = segment_ids.shape[1]
+    half = length // 2
+    info = jnp.stack([segment_ids, padding], axis=0)
+    info_there = moves.swap_core(info)
+    info = jnp.where(place // local_seqs == core, info, info_there)
+    info = lax.dynamic_index_in_dim(info, place % local_seqs, 1, False)
+    stretches = stretch_order.shape[0]
+    stretch_len = length // stretches
+    info = jnp.take(info.reshape(2, stretches, stretch_len), stretch_order, axis=1)
+    positions = stretch_order[:, None] * stretch_len + jnp.arange(stretch_len, dtype=jnp.int32)
+    code = (info[0] * (2 * length) + positions).reshape(2, half)
+    reach = (info[1] * (length - 1)).reshape(2, half)
+    code_own = lax.dynamic_index_in_dim(code, core, 0, False)
+    code_sib = lax.dynamic_index_in_dim(code, 1 - core, 0, False)
+    reach_own = lax.dynamic_index_in_dim(reach, core, 0, False)
+    reach_sib = lax.dynamic_index_in_dim(reach, 1 - core, 0, False)
+    kinfo = jnp.stack(
+        [jnp.concatenate([code_own, code_sib]), jnp.concatenate([reach_own, reach_sib])], axis=1
+    )
+    return kinfo, code_own[None]
+
+
+def pack_blocks(moves, s, w_qkv, w_out, w_up, w_down, vectors, bias_up):
+    rows = w_qkv.shape[0]
+
+    def filled(values):
+        return jnp.pad(values, ((0, 0), (0, s.cols - values.shape[1])))
+
+    turned = w_down.T
+    parts = jnp.concatenate(
+        [
+            filled(jnp.concatenate([w_qkv, w_out], axis=1)),
+            filled(w_up),
+            filled(jnp.concatenate([turned[:rows], turned[rows:]], axis=1)),
+        ],
+        axis=0,
+    )
+    there = moves.swap_core(parts)
+    even = jnp.where(moves.core == 0, parts, there)
+    odd = jnp.where(moves.core == 0, there, parts)
+    own_a = jnp.concatenate([even[:rows], odd[:rows]], axis=0)
+    own_b = jnp.concatenate([even[rows : 2 * rows], odd[rows : 2 * rows]], axis=0)
+    ff = turned.shape[1]
+    own_c = filled(
+        jnp.concatenate(
+            [
+                jnp.concatenate([v[2 * rows :, :ff], v[2 * rows :, ff : 2 * ff]], axis=0)
+                for v in (even, odd)
+            ],
+            axis=1,
+        )
+    )
+    small = jnp.concatenate([jnp.pad(vectors, ((0, 0), (0, s.cols - vectors.shape[1]))), filled(bias_up[None])], axis=0)
+    small = jnp.pad(small, ((0, 16 - small.shape[0]), (0, 0)))
+    return own_a, own_b, own_c, small
+
+
+def fast_shards(
+    dp,
+    ctx,
+    inputs,
+    cotangent,
+    w_qkv,
+    w_out,
+    w_up,
+    w_down,
+    vectors,
+    bias_up,
+    segment_ids,
+    padding,
+    stretch_order,
+):
+    local_seqs, query_len, width = inputs.shape
+    heads = width // HD
+    s = Sizes(width, w_up.shape[1] * ctx, ctx, dp, segment_ids.shape[1])
+    moves = Moves(dp, ctx, local_seqs)
+    core, place = moves.core, moves.z
+    wide = s.wide
+    kinfo, qinfo = slot_info(moves, segment_ids, padding, stretch_order)
+    own_a, own_b, own_c, small = pack_blocks(moves, s, w_qkv, w_out, w_up, w_down, vectors, bias_up)
+    (wa, wb, wc, x_low, cot, vec, normed, queries, kv, attended, residual, normed_two, slope, hidden, lse, tops, output) = forward_call(
+        s, own_a, own_b, own_c, small, inputs, cotangent, kinfo, qinfo
+    )
+    vec_rows = vec[:8, :width]
+    attended = attended[:, :width]
+    residual = residual[:, :width]
+
+    def unpad(values, size):
+        return values.reshape(values.shape[0], ctx, s.cols)[:, :, :size].reshape(values.shape[0], -1)
+
+    wide_qkv = unpad(wa, s.qkv)
+    wide_out = wa.reshape(width, ctx, s.cols)[:, :, s.qkv : s.qkv + s.out].reshape(width, -1)
+    wide_up = unpad(wb, s.up)
+    down_t = unpad(wc, s.up)
+    hidden = unpad(hidden, s.up)
+    slope = unpad(slope, s.up)
+    x_flat = x_low.astype(f32)
+    own, sib = kv[:, : s.half], kv[:, s.half :]
+    cols_q, cols_d, cols_f = w_qkv.shape[1], w_out.shape[1], w_up.shape[1]
+    rows_d, ratio = w_qkv.shape[0], w_down.shape[0] // w_qkv.shape[0]
+    block_top = jnp.max(tops, axis=2).reshape(-1)[:heads]
+    global_top = lax.pmax(block_top, AXES)
+
+    def padded(values):
+        return jnp.pad(to_low(values), ((0, 0), (0, wide - width)))
+
+    grad_output = cot.astype(f32)
+    grad_bias_two = column_sum(cot)
+    sum_down = moves.scatter_dp(moves.weight_terms(hidden, cot))
+    grad_hidden = product(cot, down_t)
+    grad_pre = to_low(grad_hidden * slope.astype(f32))
+    grad_bias_up = column_sum(grad_pre)
+    sum_up = moves.weight_terms(normed_two, grad_pre)
+    sum_up = moves.scatter_dp(sum_up)
+    unused, norm_back_two = jax.vjp(layer_norm, residual, vec_rows[5], vec_rows[6])
+    back_two = norm_back_two(contract_cols(grad_pre, wide_up))
+    grad_residual = grad_output + back_two[0]
+    grad_branch = to_low(grad_residual)
+    sum_out = moves.weight_terms(attended, grad_branch)
+    sum_out = moves.scatter_dp(sum_out)
+    grad_attended = padded(contract_cols(grad_branch, wide_out))
+    dq, d_own, d_sib = attend_backward(
+        heads, kinfo, qinfo, queries, own, sib, grad_attended, lse
+    )
+    d_came = moves.swap_core(d_sib)
+    d_own = to_low(d_own.astype(f32) + d_came.astype(f32))
+    grad_proj = jnp.concatenate([dq[:, :width], d_own[0, :, :width], d_own[1, :, :width]], axis=1)
+    sum_qkv = moves.weight_terms(normed, grad_proj)
+    sum_qkv = moves.scatter_dp(sum_qkv)
+    unused, norm_back_one = jax.vjp(layer_norm, x_flat, vec_rows[0], vec_rows[1])
+    back_one = norm_back_one(contract_cols(grad_proj, wide_qkv))
+    grad_input = to_low(grad_residual + back_one[0])
+    grad_input = moves.from_sequences(grad_input).astype(f32)
+    grad_vectors = jnp.stack(
+        [
+            back_one[1],
+            back_one[2],
+            column_sum(dq[:, :width]),
+            column_sum(d_own[1, :, :width]),
+            column_sum(grad_branch),
+            back_two[1],
+            back_two[2],
+            grad_bias_two,
+        ]
+    )
+
+    def by_place(values):
+        return jnp.swapaxes(values.reshape(values.shape[0], ctx, -1), 0, 1)
+
+    blocks_down = sum_down.reshape(ratio, rows_d, ctx, cols_d)
+    blocks_down = jnp.transpose(blocks_down, (2, 1, 0, 3)).reshape(ctx, rows_d, -1)
+    later = jnp.concatenate([by_place(sum_up), blocks_down, by_place(sum_out)], axis=2)
+    later = moves.scatter_ctx(later)
+    grad_up = later[:, :cols_f]
+    grad_down = later[:, cols_f : 2 * cols_f].reshape(rows_d, ratio, cols_d)
+    grad_down = jnp.swapaxes(grad_down, 0, 1).reshape(ratio * rows_d, cols_d)
+    grad_out = later[:, 2 * cols_f :]
+    grad_qkv = moves.scatter_ctx(by_place(sum_qkv))
+
+    tiny = jnp.concatenate([grad_vectors, grad_bias_up.reshape(-1, width)], axis=0)
+    tiny = lax.psum(tiny, AXES)
+    grad_vectors = lax.dynamic_slice_in_dim(tiny[:8], place * cols_d, cols_d, 1)
+    grad_bias = lax.dynamic_slice_in_dim(tiny[8:].reshape(-1), place * cols_f, cols_f)
+
+    factor = clip_limit / jnp.maximum(global_top, clip_limit)
+    per_column = jnp.repeat(jnp.sqrt(factor), HD)
+    column_scale = jnp.concatenate([per_column, per_column, jnp.ones((width,), f32)])
+    local_scale = lax.dynamic_slice_in_dim(column_scale, place * cols_q, cols_q)
+    clipped_qkv = to_low(w_qkv.astype(f32) * local_scale[None, :])
+    bias_scale = lax.dynamic_slice_in_dim(per_column, place * cols_d, cols_d)
+    clipped_bias = to_low(vectors[2].astype(f32) * bias_scale)
+    return (
+        output,
+        grad_input,
+        grad_qkv,
+        grad_out,
+        grad_up,
+        grad_down,
+        grad_vectors,
+        grad_bias,
+        clipped_qkv,
+        clipped_bias,
+        global_top,
+    )
+
+
 def shards(
     dp,
     ctx,
@@ -538,8 +1351,10 @@
 
 
 def solution(mesh):
+    dp, ctx = mesh.shape["dp"], mesh.shape["ctx"]
+    body = fast_shards if (dp, ctx) == (8, 4) else shards
     return jax.shard_map(
-        partial(shards, mesh.shape["dp"], mesh.shape["ctx"]),
+        partial(body, dp, ctx),
         mesh=mesh,
         in_specs=(
             P("dp", "ctx", None),

time: 882 us -> 898 us (1.018)
  Pallas kernels: 54.8 us -> 278 us
  starting transfers between devices: 160 us -> 54.2 us
  waiting for transfers between devices: 176 us -> 112 us
  other arithmetic: 107 us -> 67.2 us
  local copies, waits for them, and re-layouts: 169 us -> 207 us
  matrix products: 110 us -> 74.4 us
    pallas_call x1, Pallas kernels: 20.3 us -> 243 us  [forward_call(): pl.pallas_call(partial(forward_kernel, s), out_shape=out_shape, in_specs=...]
    ppermute x75 -> x37, starting transfers between devices: 160 us -> 54.2 us  [permute(): return lax.ppermute(values, AXES, pairs)]
    reshape x19 -> x16, local copies, waits for them, and re-layouts: 20.8 us -> 95.6 us  [the longest x6 74.5 us: unpad(): values.reshape(values.shape[0], ctx, s.cols)[:, :, :size]]
    ppermute x75 -> x37, waiting for transfers between devices: 176 us -> 112 us  [permute(): return lax.ppermute(values, AXES, pairs)]
    another operation x12 -> x3, other arithmetic: 47.3 us -> 4.29 us  [the longest x8 43.6 us: gather_dp(): return jnp.stack([first, second], axis=1).reshape(8 * rows, cols)]
    dot_general x4 -> x1, matrix products: 39.3 us -> 13.5 us  [product(): return jnp.dot(left, right, preferred_element_type=f32)]
    dynamic_update_slice x12 -> x0, local copies, waits for them, and re-layouts: 19.9 us -> none  [gather_dp(): mine = lax.dynamic_update_slice(mine, part[None], (here ^ step, 0, 0))]
    unnamed x202 -> x135, local copies, waits for them, and re-layouts: 25.6 us -> 10.2 us
  transfers between devices with their start and end apart: 75 -> 37, of which waited for: 23 -> 13; matrix products, arithmetic and copies ran while one was open for 43% -> 32% of each run, Pallas kernels for 6% -> 4%
where the time goes in v2:
time: 898 us; the launch traced here: 881 us
  Pallas kernels  278 us (31%)
  local copies, waits for them, and re-layouts  207 us (23%)
  waiting for transfers between devices  112 us (12%)
  blocking collectives  86.5 us (10%)
  matrix products  74.4 us (8%)
  other arithmetic  67.2 us (7%)
  starting transfers between devices  54.2 us (6%)
    pallas_call x1, Pallas kernels, forward_call(): pl.pallas_call(partial(forward_kernel, s), out_shape=out_shape, in_specs=...  243 us
    ppermute x37, waiting for transfers between devices, permute(): return lax.ppermute(values, AXES, pairs)  112 us
    reshape x6, local copies, waits for them, and re-layouts, unpad(): values.reshape(values.shape[0], ctx, s.cols)[:, :, :size]  74.5 us
    ppermute x37, starting transfers between devices, permute(): return lax.ppermute(values, AXES, pairs)  54.2 us
    pmax x1, blocking collectives, fast_shards(): global_top = lax.pmax(block_top, AXES)  46 us
    psum x1, blocking collectives, fast_shards(): tiny = lax.psum(tiny, AXES)  40.5 us
    dot_general x8, matrix products, contract_rows(): lax.dot_general(left, right, (((0,), (0,)), ((), ())), preferred_element_...  37.2 us
    pallas_call x1, Pallas kernels, attend_backward(): pl.pallas_call(partial(attend_backward_kernel, heads), grid=(pairs,), in_...  34.3 us
  transfers between devices with their start and end apart: 37, of which 13 were waited for; matrix products, arithmetic and copies ran while one was open for 32% of the time, Pallas kernels for 4%

profile of v2, /device:TPU:0, one launch (start us, length us, event | category | flops | bytes accessed | tf_op | source)
XLA Modules:
  0.0 881.3 jit_solution(9236726253309733779)
XLA Ops:
  16.3 243.4 %forward.1 = (bf16[1088,4608]{1,0:T(8,128)(2,1)}, bf16[1088,4608]{1,0:T(8,128)(2,1)}, bf16[1088,4608]{1,0:T(8,128)(2,1)}, bf16[512,1088]{1,0:T(8,128)(2,1)}, bf1...) custom-call(bf16[272,1152]{1,0:T(8,128)(2,1)} %pad_maximum_fusion.3., ...), custom_call_target="tpu_custom_call" | custom-call | tf_op jit(solution)/shard_map/forward/pallas_call | solution.py:953
  259.8 2.5 copy.164
  266.7 46.0 %pmax.7 = f32[17]{0:T(128)S(1)} all-reduce(f32[17]{0:T(128)S(1)} %bitcast.286), channel_id=1, replica_groups=mesh['dp'=8,'ctx'=4] {'dp','ctx'}, use_global_device_ids=true, to_apply=%region_19.20 | all-reduce | flops 17 | bytes 136 | tf_op jit(solution)/shard_map/pmax | solution.py:1088
  322.3 6.6 copy.166
  328.9 2.5 slice.220
  331.5 5.0 bitcast_convert_fusion
  336.4 9.2 %copy.138 = f32[512,4352]{1,0:T(8,128)} copy(f32[512,4352]{0,1:T(8,128)} %bitcast_convert_fusion) | data formatting | bytes 17825792 | tf_op jit(solution)/shard_map/convert_element_type | solution.py:1097
  345.7 6.7 copy.167
  352.3 2.7 slice.234
  356.8 2.5 fusion.65
  359.3 5.0 convolution_convert_fusion
  364.3 14.0 %reshape.287 = bf16[1088,4,1152]{2,1,0:T(4,128)(2,1)} reshape(bf16[1088,4608]{1,0:T(8,128)(2,1)} %get-tuple-element.33) | data formatting | bytes 20054016 | tf_op jit(solution)/shard_map/reshape | solution.py:1075
  378.3 16.6 %reshape.288 = bf16[1088,4352]{1,0:T(8,128)(2,1)} reshape(bf16[1088,4,1088]{2,1,0:T(4,128)(2,1)} %bitcast.238) | data formatting | bytes 18939904 | tf_op jit(solution)/shard_map/reshape | solution.py:1075
  394.9 13.5 %convert_reduce_fusion = (f32[4352]{0:T(1024)}, bf16[512,4352]{1,0:T(8,128)(2,1)}) fusion(f32[512,4352]{1,0:T(8,128)} %copy.138, bf16[512,1088]{1,0:T(8,128)(2,1)S(1)} %copy-done.16, bf16[1088,4352]{1,0:T(8,128)(2,1)} %reshape.288), kind=kOutput, calls=%fused_computation.4 | convolution fusion | flops 4857524224 | bytes 23970816 | tf_op jit(solution)/shard_map/dot_general | solution.py:34
  409.9 7.2 convolution_convert_fusion.1
  417.6 14.0 %reshape.290 = bf16[1088,4,1152]{2,1,0:T(4,128)(2,1)} reshape(bf16[1088,4608]{1,0:T(8,128)(2,1)} %get-tuple-element.35) | data formatting | bytes 20054016 | tf_op jit(solution)/shard_map/reshape | solution.py:1075
  431.6 16.6 %reshape.291 = bf16[1088,4352]{1,0:T(8,128)(2,1)} reshape(bf16[1088,4,1088]{2,1,0:T(4,128)(2,1)} %bitcast.239) | data formatting | bytes 18939904 | tf_op jit(solution)/shard_map/reshape | solution.py:1075
  448.2 11.4 %fusion.73 = (f32[1088]{0:T(1024)}, f32[512,1088]{0,1:T(8,128)}) fusion(bf16[512,4352]{1,0:T(8,128)(2,1)} %get-tuple-element.181, bf16[1088,4352]{1,0:T(8,128)(2,1)} %reshape.291), kind=kOutput, calls=%fused_computation.235 | convolution fusion | flops 4849171456 | bytes 16158976 | tf_op jit(solution)/shard_map/dot_general | solution.py:42
  459.6 3.0 copy.139
  462.6 3.1 multiply_reduce_fusion
  470.0 14.2 %copy.168 = bf16[1088,4608]{0,1:T(8,128)(2,1)} copy(bf16[1088,4608]{1,0:T(8,128)(2,1)} %get-tuple-element.40) | data formatting | bytes 20054016 | tf_op jit(solution)/shard_map/reshape | solution.py:1078
  486.1 2.7 convolution_convert_fusion.4
  490.7 34.3 %attend_backward.1 = (bf16[512,1152]{1,0:T(8,128)(2,1)S(1)}, bf16[2,512,1152]{2,1,0:T(8,128)(2,1)}, bf16[2,512,1152]{2,1,0:T(8,128)(2,1)}) custom-call(s32[1024,2]{1,0:T(8,128)S(1)} %copy-done, s32[1,512]{1,0:T(1,128)S(1)} %copy-done.2, bf16[512,1152]{1,0:T(8,128)(2,1)S(1)} %copy-done.3, bf16[2,512,1152]{2,1,0:T(8,128)(2,1)} %get-tuple-element.123.own_ref, ...), custom_call_target="tpu_custom_call" | custom-call | flops 12079595520 | bytes 12976128 | tf_op jit(solution)/shard_map/attend_backward/pallas_call | solution.py:336
  525.1 6.9 slice.225
  539.0 2.2 add_convert_fusion.4
  541.3 2.3 collective-permute-start.29
  546.0 4.5 collective-permute-done.29
  552.4 3.1 collective-permute-done.27
  557.2 3.9 collective-permute-done.28
  562.3 2.9 add_convert_fusion.3
  567.3 6.4 concatenate.68
  573.7 9.6 %fusion.72 = (f32[1088]{0:T(1024)S(1)}, f32[512,1088]{0,1:T(8,128)}) fusion(bf16[512,3264]{1,0:T(8,128)(2,1)} %concatenate.68, bf16[1088,3264]{0,1:T(8,128)(2,1)} %bitcast.245), kind=kOutput, calls=%fused_computation.234 | convolution fusion | flops 3637017600 | bytes 12677376 | tf_op jit(solution)/shard_map/dot_general | solution.py:42
  588.6 2.1 convert_reduce_fusion.2
  592.4 40.5 %psum.7 = f32[12,1088]{1,0:T(8,128)S(1)} all-reduce(f32[12,1088]{1,0:T(8,128)S(1)} %concatenate.74), channel_id=1, replica_groups=mesh['dp'=8,'ctx'=4] {'dp','ctx'}, use_global_device_ids=true, to_apply=%region_17.18 | all-reduce | flops 13056 | bytes 104448 | tf_op jit(solution)/shard_map/psum | solution.py:1147
  632.9 2.5 constant_dynamic-slice_fusion.13
  635.4 2.1 copy.146
  637.6 2.1 copy.145
  641.4 5.0 convolution_convert_fusion.2
  646.4 2.6 collective-permute-start.5
  650.4 5.0 collective-permute-done.3
  656.5 7.3 add_convert_fusion
  663.8 8.7 copy.154
  674.5 2.1 slice.237
  676.6 2.5 collective-permute-start.24
  680.8 4.5 add_convert_fusion.1
  686.6 8.1 collective-permute-done.24
  695.1 2.3 collective-permute-start.25
  697.5 4.1 add_convert_fusion.2
  705.6 14.5 %collective-permute-done.19 = bf16[2,136,2176]{2,1,0:T(8,128)(2,1)S(1)} collective-permute-done((bf16[2,136,2176]{2,1,0:T(8,128)(2,1)S(1)}, bf16[2,136,2176]{2,1,0:T(8,128)(2,1)S(1)}, u32[]{:S(2)}, u32[]{:S(2)}) %collective-permute-start.19) | collective-permute-done | bytes 1183776 | tf_op jit(solution)/shard_map/ppermute | solution.py:66
  720.1 2.3 collective-permute-start.6
  722.7 6.1 collective-permute-done.17
  732.6 8.2 collective-permute-done.25
  741.8 31.1 %collective-permute-done.20 = bf16[136,2176]{1,0:T(8,128)(2,1)S(1)} collective-permute-done((bf16[136,2176]{1,0:T(8,128)(2,1)S(1)}, bf16[136,2176]{1,0:T(8,128)(2,1)S(1)}, u32[]{:S(2)}, u32[]{:S(2)}) %collective-permute-start.20) | collective-permute-done | bytes 591904 | tf_op jit(solution)/shard_map/ppermute | solution.py:66
  774.3 3.9 reshape.301
  789.3 2.5 reshape.305
  791.8 8.4 concatenate.73
  800.2 11.3 %constant_dynamic-slice_fusion.6 = (bf16[1,136,2448]{2,0,1:T(2,128)(2,1)}, bf16[1,136,2448]{2,0,1:T(2,128)(2,1)}, bf16[1,136,2448]{2,0,1:T(2,128)(2,1)}, bf16[1,...) fusion(bf16[4,136,2448]{2,0,1:T(4,128)(2,1)S(1)} %concatenate.7, ...), kind=kLoop, calls=%fused_computation.178 | loop fusion | flops 332928 | bytes 9987868 | tf_op jit(solution)/shard_map/jit(dynamic_index_in_dim)/dynamic_slice | solution.py:153
  818.7 3.5 constant_dynamic-slice_fusion.12
  824.5 3.5 collective-permute-start.35
  830.0 9.1 %collective-permute-start.14 = (bf16[136,816]{1,0:T(8,128)(2,1)S(1)}, bf16[136,816]{1,0:T(8,128)(2,1)S(1)}, u32[]{:S(2)}, u32[]{:S(2)}) collective-permute-start(bf16[136,816]{1,0:T(8,128)(2,1)S(1)} %fusion.43), channel_id=1, source_target_pairs={{0,1},{1,2},{4,5},{5,6},{8,9},{9,10},{12,13},{13,14},{16,17},{17,1... | collective-permute-start | bytes 665864 | tf_op jit(solution)/shard_map/ppermute | solution.py:66
  840.0 10.1 %collective-permute-done.14 = bf16[136,816]{1,0:T(8,128)(2,1)S(1)} collective-permute-done((bf16[136,816]{1,0:T(8,128)(2,1)S(1)}, bf16[136,816]{1,0:T(8,128)(2,1)S(1)}, u32[]{:S(2)}, u32[]{:S(2)}) %collective-permute-start.14) | collective-permute-done | bytes 221984 | tf_op jit(solution)/shard_map/ppermute | solution.py:66
  850.1 4.4 collective-permute-start.15
  854.7 2.3 collective-permute-start.36
  861.4 15.2 %collective-permute-done.12 = bf16[136,816]{1,0:T(8,128)(2,1)S(1)} collective-permute-done((bf16[136,816]{1,0:T(8,128)(2,1)S(1)}, bf16[136,816]{1,0:T(8,128)(2,1)S(1)}, u32[]{:S(2)}, u32[]{:S(2)}) %collective-permute-start.12) | collective-permute-done | bytes 221984 | tf_op jit(solution)/shard_map/ppermute | solution.py:66
  (342 shorter events, 116.5 us)
Async XLA Ops:
  0.7 4.7 copy-start.53
  0.7 5.3 copy-start.56
  0.7 5.6 copy-start.33
  1.5 8.2 collective-permute-start.1
  5.2 6.5 collective-permute-start
  259.7 5.1 copy-start.5
  262.2 53.4 %copy-start.30 = (bf16[512,1088]{1,0:T(8,128)(2,1)S(1)}, bf16[512,1088]{1,0:T(8,128)(2,1)}, u32[]{:S(2)}) copy-start(bf16[512,1088]{1,0:T(8,128)(2,1)} %get-tuple-element.46) | copy-start | bytes 3342340
  364.3 292.2 %collective-permute-start.21 = (bf16[2176,1088]{0,1:T(8,128)(2,1)}, bf16[2176,1088]{0,1:T(8,128)(2,1)}, u32[]{:S(2)}, u32[]{:S(2)}) collective-permute-start(bf16[2176,1088]{0,1:T(8,128)(2,1)} %convolution_convert_fusion), channel_id=1, source_target_pairs={{0,4},{1,5},{2,6},{3,7},{4,0},{5,1},{6,2},{7,3},{8,12},{9,13},{10,... | collective-permute-start | bytes 14204936 | tf_op jit(solution)/shard_map/ppermute | solution.py:66
  417.1 263.7 %collective-permute-start.16 = (bf16[544,4352]{1,0:T(8,128)(2,1)}, bf16[544,4352]{1,0:T(8,128)(2,1)}, u32[]{:S(2)}, u32[]{:S(2)}) collective-permute-start(bf16[544,4352]{1,0:T(8,128)(2,1)} %convolution_convert_fusion.1), channel_id=1, source_target_pairs={{0,4},{1,5},{2,6},{3,7},{4,0},{5,1},{6,2},{7,3},{8,12},{9,13},{10,... | collective-permute-start | bytes 14204936 | tf_op jit(solution)/shard_map/ppermute | solution.py:66
  468.0 18.1 %copy-start.31 = (bf16[512,1088]{1,0:T(8,128)(2,1)}, bf16[512,1088]{1,0:T(8,128)(2,1)S(1)}, u32[]{:S(2)}) copy-start(bf16[512,1088]{1,0:T(8,128)(2,1)S(1)} %get-tuple-element.117) | copy-start | bytes 3342340
  470.0 69.0 %collective-permute-start.26 = (bf16[544,1088]{1,0:T(8,128)(2,1)}, bf16[544,1088]{1,0:T(8,128)(2,1)}, u32[]{:S(2)}, u32[]{:S(2)}) collective-permute-start(bf16[544,1088]{1,0:T(8,128)(2,1)} %convolution_convert_fusion.3), channel_id=1, source_target_pairs={{0,4},{1,5},{2,6},{3,7},{4,0},{5,1},{6,2},{7,3},{8,12},{9,13},{10,... | collective-permute-start | bytes 3551240 | tf_op jit(solution)/shard_map/ppermute | solution.py:66
  525.0 6.9 copy-start.54
  525.0 7.5 copy-start.43
  525.0 8.1 copy-start.44
  525.0 10.2 %copy-start.9 = (bf16[512,1088]{1,0:T(8,128)(2,1)S(1)}, bf16[512,1088]{1,0:T(8,128)(2,1)}, u32[]{:S(2)}) copy-start(bf16[512,1088]{1,0:T(8,128)(2,1)} %get-tuple-element.45) | copy-start | bytes 3342340
  531.9 5.4 copy-start.19
  534.5 27.8 %collective-permute-start.2 = (bf16[2,512,1152]{2,1,0:T(8,128)(2,1)}, bf16[2,512,1152]{2,1,0:T(8,128)(2,1)}, u32[]{:S(2)}, u32[]{:S(2)}) collective-permute-start(bf16[2,512,1152]{2,1,0:T(8,128)(2,1)} %get-tuple-element.44), channel_id=1, source_target_pairs={{0,4},{1,5},{2,6},{3,7},{4,0},{5,1},{6,2},{7,3},{8,12},{9,13},{10,... | collective-permute-start | bytes 7077896 | tf_op jit(solution)/shard_map/ppermute | solution.py:66
  541.3 9.2 %collective-permute-start.29 = (bf16[2,136,448]{2,1,0:T(8,128)(2,1)S(1)}, bf16[2,136,448]{2,1,0:T(8,128)(2,1)S(1)}, u32[]{:S(2)}, u32[]{:S(2)}) collective-permute-start(bf16[2,136,448]{2,1,0:T(8,128)(2,1)S(1)} %dynamic-slice_bitcast_fusion.13), channel_id=1, source_target_pairs={{0,16},{1,17},{2,18},{3,19},{4,20},{5,21},{6,22},{7,23},{8,24},{9,... | collective-permute-start | bytes 731144 | tf_op jit(solution)/shard_map/ppermute | solution.py:66
  544.4 11.1 %collective-permute-start.27 = (bf16[2,136,640]{2,1,0:T(8,128)(2,1)S(1)}, bf16[2,136,640]{2,1,0:T(8,128)(2,1)S(1)}, u32[]{:S(2)}, u32[]{:S(2)}) collective-permute-start(bf16[2,136,640]{2,1,0:T(8,128)(2,1)S(1)} %dynamic-slice_bitcast_fusion.12), channel_id=1, source_target_pairs={{0,8},{1,9},{2,10},{3,11},{4,12},{5,13},{6,14},{7,15},{8,0},{9,1},... | collective-permute-start | bytes 1044488 | tf_op jit(solution)/shard_map/ppermute | solution.py:66
  550.5 6.6 collective-permute-start.30
  555.6 5.5 collective-permute-start.28
  632.8 6.8 copy-start.39
  632.9 8.5 copy-start.24
  639.6 15.7 %collective-permute-start.3 = (bf16[256,1088]{0,1:T(8,128)(2,1)}, bf16[256,1088]{0,1:T(8,128)(2,1)S(1)}, u32[]{:S(2)}, u32[]{:S(2)}) collective-permute-start(bf16[256,1088]{0,1:T(8,128)(2,1)} %bitcast.272), channel_id=1, source_target_pairs={{0,1},{1,0},{2,5},{3,4},{4,3},{5,2},{6,7},{7,6},{8,9},{9,8},{10,13... | collective-permute-start | bytes 1671176 | tf_op jit(solution)/shard_map/ppermute | solution.py:66
  639.7 15.7 %collective-permute-start.4 = (bf16[256,1088]{0,1:T(8,128)(2,1)}, bf16[256,1088]{0,1:T(8,128)(2,1)S(1)}, u32[]{:S(2)}, u32[]{:S(2)}) collective-permute-start(bf16[256,1088]{0,1:T(8,128)(2,1)} %bitcast.271), channel_id=1, source_target_pairs={{0,0},{1,1},{2,4},{3,5},{4,2},{5,3},{6,6},{7,7},{8,8},{9,9},{10,12... | collective-permute-start | bytes 1671176 | tf_op jit(solution)/shard_map/ppermute | solution.py:66
  641.4 8.3 slice-start.2
  641.4 15.1 %copy-start.28 = (bf16[512,4,1,544]{0,3,2,1:T(8,128)(2,1)S(1)}, bf16[512,4,1,544]{0,3,2,1:T(8,128)(2,1)}, u32[]{:S(2)}) copy-start(bf16[512,4,1,544]{0,3,2,1:T(8,128)(2,1)} %get-tuple-element.125) | copy-start | bytes 6684676
  646.4 10.1 %copy-start.18 = (bf16[512,1088]{1,0:T(8,128)(2,1)S(1)}, bf16[512,1088]{1,0:T(8,128)(2,1)}, u32[]{:S(2)}) copy-start(bf16[512,1088]{1,0:T(8,128)(2,1)} %get-tuple-element.32) | copy-start | bytes 3342340
  646.4 51.1 %collective-permute-start.5 = (bf16[544,3264]{1,0:T(8,128)(2,1)}, bf16[544,3264]{1,0:T(8,128)(2,1)}, u32[]{:S(2)}, u32[]{:S(2)}) collective-permute-start(bf16[544,3264]{1,0:T(8,128)(2,1)} %convolution_convert_fusion.2), channel_id=1, source_target_pairs={{0,4},{1,5},{2,6},{3,7},{4,0},{5,1},{6,2},{7,3},{8,12},{9,13},{10,... | collective-permute-start | bytes 10653704 | tf_op jit(solution)/shard_map/ppermute | solution.py:66
  672.5 8.2 slice-start.3
  674.5 6.3 slice-start.4
  676.6 18.1 %collective-permute-start.24 = (bf16[2,544,448]{2,1,0:T(8,128)(2,1)S(1)}, bf16[2,544,448]{2,1,0:T(8,128)(2,1)S(1)}, u32[]{:S(2)}, u32[]{:S(2)}) collective-permute-start(bf16[2,544,448]{2,1,0:T(8,128)(2,1)S(1)} %dynamic-slice_bitcast_fusion.3), channel_id=1, source_target_pairs={{0,16},{1,17},{2,18},{3,19},{4,20},{5,21},{6,22},{7,23},{8,24},{9,... | collective-permute-start | bytes 2924552 | tf_op jit(solution)/shard_map/ppermute | solution.py:66
  679.2 51.4 %collective-permute-start.22 = (bf16[2,544,640]{2,1,0:T(8,128)(2,1)S(1)}, bf16[2,544,640]{2,1,0:T(8,128)(2,1)S(1)}, u32[]{:S(2)}, u32[]{:S(2)}) collective-permute-start(bf16[2,544,640]{2,1,0:T(8,128)(2,1)S(1)} %dynamic-slice_bitcast_fusion), channel_id=1, source_target_pairs={{0,8},{1,9},{2,10},{3,11},{4,12},{5,13},{6,14},{7,15},{8,0},{9,1},... | collective-permute-start | bytes 4177928 | tf_op jit(solution)/shard_map/ppermute | solution.py:66
  685.7 34.4 %collective-permute-start.19 = (bf16[2,136,2176]{2,1,0:T(8,128)(2,1)S(1)}, bf16[2,136,2176]{2,1,0:T(8,128)(2,1)S(1)}, u32[]{:S(2)}, u32[]{:S(2)}) collective-permute-start(bf16[2,136,2176]{2,1,0:T(8,128)(2,1)S(1)} %dynamic-slice_bitcast_fusion.1), channel_id=1, source_target_pairs={{0,16},{1,17},{2,18},{3,19},{4,20},{5,21},{6,22},{7,23},{8,24},{9,... | collective-permute-start | bytes 3551240 | tf_op jit(solution)/shard_map/ppermute | solution.py:66
  686.4 11.0 %copy-start.36 = (bf16[512,4,1,136]{0,3,2,1:T(8,128)(2,1)S(1)}, bf16[512,4,1,136]{0,3,2,1:T(8,128)(2,1)}, u32[]{:S(2)}) copy-start(bf16[512,4,1,136]{0,3,2,1:T(8,128)(2,1)} %get-tuple-element.148) | copy-start | bytes 1671172
  686.4 42.4 %collective-permute-start.17 = (bf16[2,136,2176]{2,1,0:T(8,128)(2,1)S(1)}, bf16[2,136,2176]{2,1,0:T(8,128)(2,1)S(1)}, u32[]{:S(2)}, u32[]{:S(2)}) collective-permute-start(bf16[2,136,2176]{2,1,0:T(8,128)(2,1)S(1)} %dynamic-slice_bitcast_fusion.2), channel_id=1, source_target_pairs={{0,8},{1,9},{2,10},{3,11},{4,12},{5,13},{6,14},{7,15},{8,0},{9,1},... | collective-permute-start | bytes 3551240 | tf_op jit(solution)/shard_map/ppermute | solution.py:66
  695.1 45.7 %collective-permute-start.25 = (bf16[544,448]{1,0:T(8,128)(2,1)S(1)}, bf16[544,448]{1,0:T(8,128)(2,1)S(1)}, u32[]{:S(2)}, u32[]{:S(2)}) collective-permute-start(bf16[544,448]{1,0:T(8,128)(2,1)S(1)} %dynamic-slice_bitcast_fusion.9), channel_id=1, source_target_pairs={{0,8},{1,9},{2,10},{3,11},{4,12},{5,13},{6,14},{7,15},{8,0},{9,1},... | collective-permute-start | bytes 1462280 | tf_op jit(solution)/shard_map/ppermute | solution.py:66
  704.2 74.0 %collective-permute-start.8 = (bf16[2,136,1600]{2,1,0:T(8,128)(2,1)}, bf16[2,136,1600]{2,1,0:T(8,128)(2,1)}, u32[]{:S(2)}, u32[]{:S(2)}) collective-permute-start(bf16[2,136,1600]{2,1,0:T(8,128)(2,1)} %dynamic-slice_bitcast_fusion.4), channel_id=1, source_target_pairs={{0,16},{1,17},{2,18},{3,19},{4,20},{5,21},{6,22},{7,23},{8,24},{9,... | collective-permute-start | bytes 2611208 | tf_op jit(solution)/shard_map/ppermute | solution.py:66
  720.1 62.0 %collective-permute-start.6 = (bf16[2,136,1664]{2,1,0:T(8,128)(2,1)}, bf16[2,136,1664]{2,1,0:T(8,128)(2,1)}, u32[]{:S(2)}, u32[]{:S(2)}) collective-permute-start(bf16[2,136,1664]{2,1,0:T(8,128)(2,1)} %dynamic-slice_bitcast_fusion.5), channel_id=1, source_target_pairs={{0,8},{1,9},{2,10},{3,11},{4,12},{5,13},{6,14},{7,15},{8,0},{9,1},... | collective-permute-start | bytes 2715656 | tf_op jit(solution)/shard_map/ppermute | solution.py:66
  728.9 44.0 %collective-permute-start.20 = (bf16[136,2176]{1,0:T(8,128)(2,1)S(1)}, bf16[136,2176]{1,0:T(8,128)(2,1)S(1)}, u32[]{:S(2)}, u32[]{:S(2)}) collective-permute-start(bf16[136,2176]{1,0:T(8,128)(2,1)S(1)} %dynamic-slice_bitcast_fusion.7), channel_id=1, source_target_pairs={{0,8},{1,9},{2,10},{3,11},{4,12},{5,13},{6,14},{7,15},{8,0},{9,1},... | collective-permute-start | bytes 1775624 | tf_op jit(solution)/shard_map/ppermute | solution.py:66
  730.6 42.4 %collective-permute-start.18 = (bf16[136,2176]{1,0:T(8,128)(2,1)S(1)}, bf16[136,2176]{1,0:T(8,128)(2,1)S(1)}, u32[]{:S(2)}, u32[]{:S(2)}) collective-permute-start(bf16[136,2176]{1,0:T(8,128)(2,1)S(1)} %dynamic-slice_bitcast_fusion.8), channel_id=1, source_target_pairs={{0,16},{1,17},{2,18},{3,19},{4,20},{5,21},{6,22},{7,23},{8,24},{9,... | collective-permute-start | bytes 1775624 | tf_op jit(solution)/shard_map/ppermute | solution.py:66
  740.8 44.3 %collective-permute-start.23 = (bf16[544,640]{1,0:T(8,128)(2,1)}, bf16[544,640]{1,0:T(8,128)(2,1)}, u32[]{:S(2)}, u32[]{:S(2)}) collective-permute-start(bf16[544,640]{1,0:T(8,128)(2,1)} %dynamic-slice_bitcast_fusion.6), channel_id=1, source_target_pairs={{0,16},{1,17},{2,18},{3,19},{4,20},{5,21},{6,22},{7,23},{8,24},{9,... | collective-permute-start | bytes 2088968 | tf_op jit(solution)/shard_map/ppermute | solution.py:66
  780.8 5.6 copy-start.25
  780.8 34.7 %collective-permute-start.9 = (bf16[136,1600]{1,0:T(8,128)(2,1)}, bf16[136,1600]{1,0:T(8,128)(2,1)}, u32[]{:S(2)}, u32[]{:S(2)}) collective-permute-start(bf16[136,1600]{1,0:T(8,128)(2,1)} %dynamic-slice_bitcast_fusion.10), channel_id=1, source_target_pairs={{0,8},{1,9},{2,10},{3,11},{4,12},{5,13},{6,14},{7,15},{8,0},{9,1},... | collective-permute-start | bytes 1305608 | tf_op jit(solution)/shard_map/ppermute | solution.py:66
  784.5 32.2 %collective-permute-start.7 = (bf16[136,1664]{1,0:T(8,128)(2,1)}, bf16[136,1664]{1,0:T(8,128)(2,1)}, u32[]{:S(2)}, u32[]{:S(2)}) collective-permute-start(bf16[136,1664]{1,0:T(8,128)(2,1)} %dynamic-slice_bitcast_fusion.11), channel_id=1, source_target_pairs={{0,16},{1,17},{2,18},{3,19},{4,20},{5,21},{6,22},{7,23},{8,24},{9,... | collective-permute-start | bytes 1357832 | tf_op jit(solution)/shard_map/ppermute | solution.py:66
  813.4 10.9 %collective-permute-start.34 = (bf16[136,2448]{1,0:T(8,128)(2,1)}, bf16[136,2448]{1,0:T(8,128)(2,1)S(1)}, u32[]{:S(2)}, u32[]{:S(2)}) collective-permute-start(bf16[136,2448]{1,0:T(8,128)(2,1)} %bitcast.225), channel_id=1, source_target_pairs={{0,1},{4,5},{8,9},{12,13},{16,17},{20,21},{24,25},{28,29}} | collective-permute-start | bytes 1997576 | tf_op jit(solution)/shard_map/ppermute | solution.py:66
  814.8 13.3 %collective-permute-start.31 = (bf16[136,2448]{1,0:T(8,128)(2,1)}, bf16[136,2448]{1,0:T(8,128)(2,1)S(1)}, u32[]{:S(2)}, u32[]{:S(2)}) collective-permute-start(bf16[136,2448]{1,0:T(8,128)(2,1)} %bitcast.226), channel_id=1, source_target_pairs={{3,2},{7,6},{11,10},{15,14},{19,18},{23,22},{27,26},{31,30}} | collective-permute-start | bytes 1997576 | tf_op jit(solution)/shard_map/ppermute | solution.py:66
  818.7 5.7 copy-start.15
  822.1 5.9 copy-start.14
  822.2 7.7 collective-permute-start.13
  823.7 15.4 %collective-permute-start.10 = (bf16[136,816]{1,0:T(8,128)(2,1)S(1)}, bf16[136,816]{1,0:T(8,128)(2,1)S(1)}, u32[]{:S(2)}, u32[]{:S(2)}) collective-permute-start(bf16[136,816]{1,0:T(8,128)(2,1)S(1)} %bitcast.274), channel_id=1, source_target_pairs={{3,2},{7,6},{11,10},{15,14},{19,18},{23,22},{27,26},{31,30}} | collective-permute-start | bytes 665864 | tf_op jit(solution)/shard_map/ppermute | solution.py:66
  824.5 30.0 %collective-permute-start.35 = (bf16[136,2448]{1,0:T(8,128)(2,1)S(1)}, bf16[136,2448]{1,0:T(8,128)(2,1)S(1)}, u32[]{:S(2)}, u32[]{:S(2)}) collective-permute-start(bf16[136,2448]{1,0:T(8,128)(2,1)S(1)} %fusion.17), channel_id=1, source_target_pairs={{0,1},{1,2},{4,5},{5,6},{8,9},{9,10},{12,13},{13,14},{16,17},{17,1... | collective-permute-start | bytes 1997576 | tf_op jit(solution)/shard_map/ppermute | solution.py:66
  828.1 26.5 %copy-start.13 = (bf16[1,136,2448]{2,0,1:T(2,128)(2,1)S(1)}, bf16[1,136,2448]{2,0,1:T(2,128)(2,1)}, u32[]{:S(2)}) copy-start(bf16[1,136,2448]{2,0,1:T(2,128)(2,1)} %get-tuple-element.132) | copy-start | bytes 1997572
  828.2 28.8 %collective-permute-start.32 = (bf16[136,2448]{1,0:T(8,128)(2,1)S(1)}, bf16[136,2448]{1,0:T(8,128)(2,1)S(1)}, u32[]{:S(2)}, u32[]{:S(2)}) collective-permute-start(bf16[136,2448]{1,0:T(8,128)(2,1)S(1)} %fusion.19), channel_id=1, source_target_pairs={{2,1},{3,2},{6,5},{7,6},{10,9},{11,10},{14,13},{15,14},{18,17},{19... | collective-permute-start | bytes 1997576 | tf_op jit(solution)/shard_map/ppermute | solution.py:66
  830.0 20.1 %collective-permute-start.14 = (bf16[136,816]{1,0:T(8,128)(2,1)S(1)}, bf16[136,816]{1,0:T(8,128)(2,1)S(1)}, u32[]{:S(2)}, u32[]{:S(2)}) collective-permute-start(bf16[136,816]{1,0:T(8,128)(2,1)S(1)} %fusion.43), channel_id=1, source_target_pairs={{0,1},{1,2},{4,5},{5,6},{8,9},{9,10},{12,13},{13,14},{16,17},{17,1... | collective-permute-start | bytes 665864 | tf_op jit(solution)/shard_map/ppermute | solution.py:66
  839.1 18.0 %copy-start.12 = (bf16[1,136,2448]{2,0,1:T(2,128)(2,1)S(1)}, bf16[1,136,2448]{2,0,1:T(2,128)(2,1)}, u32[]{:S(2)}) copy-start(bf16[1,136,2448]{2,0,1:T(2,128)(2,1)} %get-tuple-element.128) | copy-start | bytes 1997572
  839.1 19.4 %collective-permute-start.11 = (bf16[136,816]{1,0:T(8,128)(2,1)S(1)}, bf16[136,816]{1,0:T(8,128)(2,1)S(1)}, u32[]{:S(2)}, u32[]{:S(2)}) collective-permute-start(bf16[136,816]{1,0:T(8,128)(2,1)S(1)} %fusion.45), channel_id=1, source_target_pairs={{2,1},{3,2},{6,5},{7,6},{10,9},{11,10},{14,13},{15,14},{18,17},{19... | collective-permute-start | bytes 665864 | tf_op jit(solution)/shard_map/ppermute | solution.py:66
  850.1 11.3 %collective-permute-start.15 = (bf16[136,816]{1,0:T(8,128)(2,1)S(1)}, bf16[136,816]{1,0:T(8,128)(2,1)S(1)}, u32[]{:S(2)}, u32[]{:S(2)}) collective-permute-start(bf16[136,816]{1,0:T(8,128)(2,1)S(1)} %fusion.44), channel_id=1, source_target_pairs={{0,1},{1,2},{2,3},{4,5},{5,6},{6,7},{8,9},{9,10},{10,11},{12,13},{... | collective-permute-start | bytes 665864 | tf_op jit(solution)/shard_map/ppermute | solution.py:66
  854.7 5.2 copy-start.26
  854.7 5.2 copy-start.27
  854.7 22.7 %collective-permute-start.36 = (bf16[136,2448]{1,0:T(8,128)(2,1)S(1)}, bf16[136,2448]{1,0:T(8,128)(2,1)S(1)}, u32[]{:S(2)}, u32[]{:S(2)}) collective-permute-start(bf16[136,2448]{1,0:T(8,128)(2,1)S(1)} %fusion.18), channel_id=1, source_target_pairs={{0,1},{1,2},{2,3},{4,5},{5,6},{6,7},{8,9},{9,10},{10,11},{12,13},{... | collective-permute-start | bytes 1997576 | tf_op jit(solution)/shard_map/ppermute | solution.py:66
  857.2 20.2 %collective-permute-start.33 = (bf16[136,2448]{1,0:T(8,128)(2,1)S(1)}, bf16[136,2448]{1,0:T(8,128)(2,1)S(1)}, u32[]{:S(2)}, u32[]{:S(2)}) collective-permute-start(bf16[136,2448]{1,0:T(8,128)(2,1)S(1)} %fusion.20), channel_id=1, source_target_pairs={{1,0},{2,1},{3,2},{5,4},{6,5},{7,6},{9,8},{10,9},{11,10},{13,12},{... | collective-permute-start | bytes 1997576 | tf_op jit(solution)/shard_map/ppermute | solution.py:66
  858.6 18.0 %collective-permute-start.12 = (bf16[136,816]{1,0:T(8,128)(2,1)S(1)}, bf16[136,816]{1,0:T(8,128)(2,1)S(1)}, u32[]{:S(2)}, u32[]{:S(2)}) collective-permute-start(bf16[136,816]{1,0:T(8,128)(2,1)S(1)} %fusion.46), channel_id=1, source_target_pairs={{1,0},{2,1},{3,2},{5,4},{6,5},{7,6},{9,8},{10,9},{11,10},{13,12},{... | collective-permute-start | bytes 665864 | tf_op jit(solution)/shard_map/ppermute | solution.py:66
  859.9 17.5 %copy-start.11 = (bf16[1,136,2448]{2,0,1:T(2,128)(2,1)S(1)}, bf16[1,136,2448]{2,0,1:T(2,128)(2,1)}, u32[]{:S(2)}) copy-start(bf16[1,136,2448]{2,0,1:T(2,128)(2,1)} %get-tuple-element.126) | copy-start | bytes 1997572
  (37 other events, 100.6 us)

commit v3 on v2

--- a/solution.py
+++ b/solution.py
@@ -328,7 +328,7 @@
     )(kinfo, qinfo, queries, own, sib)
 
 
-def attend_backward(heads, kinfo, qinfo, queries, own, sib, grad, lse):
+def attend_backward(heads, kinfo, qinfo, queries, kv, grad, lse):
     rows, width = queries.shape
     pairs = width // LANES
     flat, double, per_head = pair_specs(rows)
@@ -341,7 +341,7 @@
             pl.BlockSpec(qinfo.shape, lambda i: (0, 0)),
             flat,
             double,
-            double,
+            pl.BlockSpec((2, rows, LANES), lambda i: (0, 1, i)),
             flat,
             per_head,
         ],
@@ -355,7 +355,7 @@
             transcendentals=pairs * 4 * rows * rows,
         ),
         name="attend_backward",
-    )(kinfo, qinfo, queries, own, sib, grad, lse)
+    )(kinfo, qinfo, queries, kv, kv, grad, lse)
 
 
 MESH = pl.DeviceIdType.MESH
@@ -375,6 +375,7 @@
         self.pairs = self.wide // LANES
         self.out_tile = self.qkv // LANES * LANES
         self.qkv_cols = 1024
+        self.qkv_pad = -(-self.qkv // LANES) * LANES
 
     def qkv_runs(self, z):
         runs, at = [], z * self.qkv
@@ -686,6 +687,36 @@
     att_ref[:, lanes] = jnp.concatenate(outs, axis=0).T.astype(bf16)
 
 
+def forward_plan(A, B, C, near, far, seq_x, seq_cot):
+    def do(method, *args):
+        return partial(method, *args)
+
+    return {
+        ("start", 0): (
+            do(A.arrive, near),
+            do(B.begin),
+            do(A.arrive, far),
+            do(seq_x.start),
+        ),
+        ("vectors", 0): (
+            do(A.turn, near),
+            do(B.arrive, near),
+            do(C.begin),
+            do(A.turn, far),
+            do(A.last, near),
+            do(B.arrive, far),
+            do(A.last, far),
+        ),
+        ("normed", 0): (do(B.turn, near),),
+        ("project", 1): (do(C.arrive, near),),
+        ("share", 0): (do(B.turn, far), do(B.last, near)),
+        ("pair", 0): (do(C.arrive, far), do(seq_cot.start)),
+        ("pair", 2): (do(B.last, far), do(C.turn, near)),
+        ("pair", 6): (do(C.turn, far), do(C.last, near)),
+        ("down", 0): (do(C.last, far),),
+    }
+
+
 def forward_kernel(s, *refs):
     (own_a, own_b, own_c, small, inp, cot, kinfo, qinfo) = refs[:8]
     (wa, wb, wc, x_o, cot_o, vec, normed_o, q_o, kv_o, att_o, res_o, two_o, slope_o, hid_o) = refs[8:22]
@@ -701,8 +732,7 @@
     ]
     seq_x = ToSequences(net, inp, x, sems[21:23])
     seq_cot = ToSequences(net, cot, cot_o, sems[23:25])
-    seq_out = FromSequences(net, out, out_o, sems[25:27])
-    small_s, small_r, kv_s, kv_r, load, save = sems[27:33]
+    small_s, small_r, kv_s, kv_r, load, save = sems[25:31]
     near, far = net.near, net.far
     saves = []
 
@@ -721,6 +751,12 @@
             device_id_type=MESH,
         )
 
+    plan = forward_plan(A, B, C, near, far, seq_x, seq_cot)
+
+    def at(name, step=0):
+        for act in plan.get((name, step), ()):
+            act()
+
     enter(net)
     A.begin()
     for z in range(4):
@@ -733,15 +769,12 @@
         def _():
             pltpu.make_async_copy(small, smalls.at[z], small_r.at[z]).start()
 
-    A.arrive(near)
-    seq_x.start()
-    A.arrive(far)
-    B.begin()
+    at("start")
     diff = qinfo[0:1, :] - kinfo[:, 0:1]
     fine = (diff >= 0) & (diff <= kinfo[:, 1:2])
     bias[...] = jnp.where(fine, 0.0, masked_fill)
-    A.turn(near)
-    B.arrive(near)
+    pre[...] = jnp.zeros_like(pre)
+    at("vectors")
 
     for z in range(4):
         pltpu.make_async_copy(small, smalls.at[z], small_r.at[z]).wait()
@@ -766,12 +799,7 @@
         ),
     )
     keep(normed, normed_o)
-    A.turn(far)
-    A.last(near)
-    B.arrive(far)
-    A.last(far)
-    C.begin()
-    pre[...] = jnp.zeros_like(pre)
+    at("normed")
     A.ready()
 
     def tile_a(z):
@@ -798,8 +826,7 @@
             base = target // LANES * LANES
             moved = place_run(res[:, : s.qkv_cols], source, target - base, count)
             pre[:, base : base + moved.shape[1]] += moved
-        if z == 1:
-            seq_cot.start()
+        at("project", z)
     tile_a(0).start()
     kv[0, : s.half, :] = to_low(pre[:, s.wide : 2 * s.wide])
     kv[1, : s.half, :] = to_low(pre[:, 2 * s.wide :] + vec[3:4, :])
@@ -813,8 +840,7 @@
     )
     share.start()
     q[...] = to_low(pre[:, : s.wide] + vec[2:3, :])
-    B.turn(near)
-    C.arrive(near)
+    at("share")
     share.wait()
     keep(q, q_o)
     keep(kv, kv_o)
@@ -822,24 +848,13 @@
     def pair(i, carry):
         attend_pair(s, i, q, kv, bias, att, lse, top)
 
-        @pl.when(i == 1)
-        def _():
-            B.turn(far)
-            B.last(near)
-
-        @pl.when(i == 4)
-        def _():
-            C.arrive(far)
-
-        @pl.when(i == 6)
-        def _():
-            B.last(far)
-
+        for k in range(s.pairs):
+            if ("pair", k) in plan:
+                pl.when(i == k)(partial(at, "pair", k))
         return carry
 
     lax.fori_loop(0, s.pairs, pair, 0)
     keep(att, att_o)
-    C.turn(near)
 
     res[...] = jnp.zeros_like(res)
     for z in range(4):
@@ -851,6 +866,7 @@
         base = target // LANES * LANES
         moved = place_run(block, s.qkv - s.out_tile, target - base, s.out)
         res[:, base : base + moved.shape[1]] += moved
+    at("second")
     B.ready()
     tile_b(0).start()
 
@@ -879,12 +895,10 @@
             slope[:, lanes] = to_low(0.5 * (1 + t) + 0.5 * u * (1 - t * t) * bend)
 
         by_columns(s.cols, part)
-        if z == 1:
-            C.turn(far)
-            C.last(near)
+        at("up", z)
     keep(hid, hid_o)
     keep(slope, slope_o)
-    C.last(far)
+    at("down")
     C.ready()
 
     def tile_c(k):
@@ -902,7 +916,7 @@
         block = nt(hid[...], ct[k % 2, :count, :])
         total = res[:, at : at + count] + block + vec[7:8, at : at + count]
         out[:, at : at + count] = to_low(total)
-    seq_out.start()
+    keep(out, out_o)
     seq_cot.wait()
     for group in (A, B, C):
         group.drain()
@@ -916,8 +930,6 @@
     seq_cot.drain()
     for copy in saves:
         copy.wait()
-    seq_out.wait()
-    seq_out.drain()
 
 
 def forward_call(s, own_a, own_b, own_c, small, inp, cot, kinfo, qinfo):
@@ -945,7 +957,7 @@
         low(rows, full),
         high(s.pairs, 2, rows),
         high(s.pairs, 2, rows),
-        low(*inp.shape),
+        low(rows, s.width),
     ]
     anywhere = pl.BlockSpec(memory_space=pl.ANY)
     local = pl.BlockSpec(memory_space=pltpu.VMEM)
@@ -973,13 +985,658 @@
             pltpu.VMEM((4, 16, s.wide), bf16),
         ]
         + gather_sems() * 3
-        + [dma((2,))] * 6
+        + [dma((2,))] * 4
         + [dma((4,)), dma((4,)), dma, dma, dma((2,)), dma((12,))],
         compiler_params=pltpu.CompilerParams(
             collective_id=1, has_side_effects=True, vmem_limit_bytes=61 * 2**20
         ),
         name="forward",
     )(own_a, own_b, own_c, small, inp, cot, kinfo, qinfo)
+
+
+class Scatter:
+    def __init__(self, net, s, own, ship, came, first, second, line, total, out, stage, sems):
+        self.n, self.s = net, s
+        self.own, self.ship_ref, self.came = own, ship, came
+        self.first_ref, self.second_ref, self.line = first, second, line
+        self.total, self.out, self.stage = total, out, stage
+        (self.ps, self.pr, self.fs, self.fr, self.hs, self.hr, self.zs, self.zr, self.ld, self.es, self.er, self.eo) = sems
+
+    def target(self, k):
+        return (self.n.far, self.n.near)[k]
+
+    def sibling_target(self, k):
+        n = self.n
+        return 1 - n.c + 2 * (n.z // 2 if k else 1 - n.z // 2)
+
+    def route(self, k):
+        n = self.n
+        early = self.target(k) < 2
+        one = jnp.where(early, n.py, n.px)
+        two = jnp.where(early, n.px, n.py)
+        return (one, (2 * one + n.c, n.z)), (two, (2 * two + n.c, n.z))
+
+    def block(self, k, p):
+        rows = self.s.rows
+        return self.own.at[k, pl.ds(pl.multiple_of(p * rows, 16), rows)]
+
+    def remote(self, src, dst, send, recv, to):
+        return pltpu.make_async_remote_copy(
+            src, dst, send, recv, device_id=to, device_id_type=MESH
+        )
+
+    def panel(self, k):
+        return self.remote(
+            self.ship_ref.at[k], self.came.at[k], self.ps.at[k], self.pr.at[k], self.n.sib
+        )
+
+    def pieces(self, k):
+        (one, to), _ = self.route(k)
+        for i, p in enumerate((one, self.n.pd)):
+            yield self.remote(
+                self.block(k, p), self.first_ref.at[k, i], self.fs.at[k, i], self.fr.at[k, i], to
+            )
+
+    def piece(self, k):
+        _, (two, to) = self.route(k)
+        return self.remote(
+            self.block(k, two), self.second_ref.at[k], self.hs.at[k], self.hr.at[k], to
+        )
+
+    def step(self, k, up):
+        n = self.n
+        t = self.target(k) // 2
+        to = (n.d, n.z + 1 if up else n.z - 1)
+        side = 0 if up else 1
+        return self.remote(
+            self.block(k, n.p), self.line.at[t, side], self.zs.at[k], self.zr.at[t, side], to
+        )
+
+    def ship(self, k):
+        self.panel(k).start()
+
+    def wait_panel(self, k):
+        self.panel(k).wait_recv()
+
+    def start(self, k):
+        for copy in self.pieces(k):
+            copy.start()
+
+    def add(self, k, p, other):
+        rows = self.s.rows
+
+        def some(r):
+            at = pl.ds(pl.multiple_of(p * rows + r.start, 16), r.size)
+            self.own[k, at, :] = to_low(
+                self.own[k, at, :].astype(f32) + other[r, :].astype(f32)
+            )
+
+        by_rows(rows, 16, some)
+
+    def turn(self, k):
+        for copy in self.pieces(k):
+            copy.wait_recv()
+        _, (two, _) = self.route(k)
+        self.add(k, two, self.first_ref.at[k, 1])
+        self.piece(k).start()
+        self.add(k, self.n.p, self.first_ref.at[k, 0])
+
+    def land(self, k):
+        self.piece(k).wait_recv()
+        self.add(k, self.n.p, self.second_ref.at[k])
+
+    def fetch(self, k, side):
+        t = self.target(k) // 2
+        n = self.n
+        block = self.block(k, n.p)
+        self.remote(block, self.line.at[t, side], self.zs.at[k], self.zr.at[t, side], n.sib).wait_recv()
+        load = pltpu.make_async_copy(self.line.at[t, side], self.stage, self.ld)
+        load.start()
+        load.wait()
+
+    def along(self, k):
+        n, z, t = self.n, self.n.z, self.target(k)
+
+        @pl.when(t < z)
+        def _():
+            @pl.when(z < 3)
+            def _():
+                self.fetch(k, 1)
+                self.add(k, n.p, self.stage)
+
+            self.step(k, False).start()
+
+        @pl.when(t > z)
+        def _():
+            @pl.when(z > 0)
+            def _():
+                self.fetch(k, 0)
+                self.add(k, n.p, self.stage)
+
+            self.step(k, True).start()
+
+        if k == 1:
+
+            @pl.when(t == z)
+            def _():
+                rows = self.s.rows
+
+                def begin(r):
+                    at = pl.ds(pl.multiple_of(n.p * rows + r.start, 16), r.size)
+                    self.total[r, :] = self.own[k, at, :].astype(f32)
+
+                by_rows(rows, 16, begin)
+
+                def more(r):
+                    self.total[r, :] += self.stage[r, :].astype(f32)
+
+                @pl.when(z > 0)
+                def _():
+                    self.fetch(k, 0)
+                    by_rows(rows, 16, more)
+
+                @pl.when(z < 3)
+                def _():
+                    self.fetch(k, 1)
+                    by_rows(rows, 16, more)
+
+                pltpu.make_async_copy(self.total, self.out, self.eo).start()
+                self.final().start()
+
+    def final(self):
+        return self.remote(self.total, self.out, self.es, self.er, self.n.sib)
+
+    def finish(self, panels=True):
+        n = self.n
+        mine = n.z % 2 == n.c
+
+        @pl.when(mine)
+        def _():
+            pltpu.make_async_copy(self.total, self.out, self.eo).wait()
+            self.final().wait_send()
+
+        @pl.when(jnp.logical_not(mine))
+        def _():
+            self.final().wait_recv()
+
+        for k in range(2):
+            if panels:
+                self.panel(k).wait_send()
+            for copy in self.pieces(k):
+                copy.wait_send()
+            self.piece(k).wait_send()
+
+            @pl.when(self.target(k) != n.z)
+            def _():
+                self.step(k, True).wait_send()
+
+
+def scatter_sems():
+    dma = pltpu.SemaphoreType.DMA
+    return [
+        dma((2,)), dma((2,)), dma((2, 2)), dma((2, 2)), dma((2,)), dma((2,)),
+        dma((2,)), dma((2, 2)), dma, dma, dma, dma,
+    ]
+
+
+def scatter_scratch(s, groups):
+    panels = (2, s.width, s.cols)
+    scratch = [pltpu.VMEM(panels, bf16)]
+    for group in range(groups):
+        scratch += [pltpu.VMEM(panels, bf16)] * (1 if group else 2)
+        scratch += [
+            pltpu.VMEM((2, 2, s.rows, s.cols), bf16),
+            pltpu.VMEM((2, s.rows, s.cols), bf16),
+        ]
+    return scratch + [pltpu.VMEM((s.rows, s.cols), f32), pltpu.VMEM((s.rows, s.cols), bf16)]
+
+
+def norm_back(values, grads, gain):
+    average = jnp.mean(values, axis=-1, keepdims=True)
+    centred = values - average
+    variance = jnp.mean(centred * centred, axis=-1, keepdims=True)
+    scale = lax.rsqrt(variance + eps_norm)
+    n = centred * scale
+    gn = grads * gain
+    inner = jnp.mean(gn * n, axis=-1, keepdims=True)
+    back = scale * (gn - jnp.mean(gn, axis=-1, keepdims=True) - n * inner)
+    return back, jnp.sum(grads * n, axis=0, keepdims=True), jnp.sum(grads, axis=0, keepdims=True)
+
+
+def fetch_all(pairs, sems):
+    copies = [pltpu.make_async_copy(src, dst, sems.at[i]) for i, (src, dst) in enumerate(pairs)]
+    for copy in copies:
+        copy.start()
+    return copies
+
+
+def middle_kernel(s, *refs):
+    (wa, wb, wc, cot_i, res_i, two_i, slope_i, hid_i, out_i, vec) = refs[:10]
+    (down_o, up_o, gres_o, branch_o, gatt_o, oz_o, sums, back_o, line_c, line_b) = refs[10:20]
+    (cot, res, two, gp, hid, cot_t, two_t, wt, acc, branch, oz) = refs[20:31]
+    (ship, own_c, came, first_c, second_c, own_b, first_b, second_b, total, stage) = refs[31:41]
+    sems = refs[41:]
+    net = Net()
+    C = Scatter(net, s, own_c, ship, came, first_c, second_c, line_c, total, down_o, stage, sems[:12])
+    B = Scatter(net, s, own_b, ship, came, first_b, second_b, line_b, total, up_o, stage, sems[12:24])
+    seq_out = FromSequences(net, out_i, back_o, sems[24:26])
+    load, tiles, save, credit = sems[26:30]
+    loads = fetch_all(
+        ((cot_i, cot), (hid_i, hid), (slope_i, gp), (two_i, two), (res_i, res)), load
+    )
+    enter(net)
+    seq_out.start()
+
+    def tile(w, j, first=0):
+        lanes = pl.ds(j * s.cols + first, s.cols - first)
+        return pltpu.make_async_copy(
+            w.at[:, lanes], wt.at[j % 2, :, pl.ds(0, s.cols - first)], tiles.at[j % 2]
+        )
+
+    tile(wc, 0).start()
+    loads[0].wait()
+    cot_t[...] = cot[...].T
+    loads[1].wait()
+    sums[...] = jnp.zeros_like(sums)
+
+    def down_panel(z, dst, k, came=None):
+        rows = pl.ds(pl.multiple_of(z * s.rows, 16), s.rows)
+        for p in range(4):
+            at = slice(p * s.rows, (p + 1) * s.rows)
+
+            def part(start, size):
+                lanes = pl.ds(start, size)
+                many = pl.ds(pl.multiple_of(p * s.cols + start, LANES), size)
+                value = product(cot_t[rows, :], hid[:, many])
+                if came is not None:
+                    value = value + came[k, at, lanes].astype(f32)
+                dst[k, at, lanes] = to_low(value)
+
+            by_columns(s.cols, part)
+
+    def up_panel(z, dst, k, came=None):
+        def part(start, size):
+            lanes = pl.ds(start, size)
+            many = pl.ds(pl.multiple_of(z * s.cols + start, LANES), size)
+            value = product(two_t[...], gp[:, many])
+            if came is not None:
+                value = value + came[k, :, lanes].astype(f32)
+            dst[k, :, lanes] = to_low(value)
+
+        by_columns(s.cols, part)
+
+    for k in range(2):
+        down_panel(C.sibling_target(k), ship, k)
+        C.ship(k)
+    loads[2].wait()
+
+    for j in range(4):
+        if j < 3:
+            tile(wc, j + 1).start()
+        tile(wc, j).wait()
+
+        def part(start, size):
+            lanes = pl.ds(pl.multiple_of(j * s.cols + start, LANES), size)
+            value = product(cot[...], wt[j % 2, :, pl.ds(start, size)])
+            value = to_low(value * gp[:, lanes].astype(f32))
+            gp[:, lanes] = value
+            sums[8 + j : 9 + j, pl.ds(start, size)] = jnp.sum(
+                value.astype(f32), axis=0, keepdims=True
+            )
+
+        by_columns(s.cols, part)
+    tile(wb, 0).start()
+    for k in range(2):
+        C.wait_panel(k)
+        down_panel(C.target(k), own_c, k, came)
+        pl.semaphore_signal(
+            credit.at[k], inc=1, device_id=net.sib, device_id_type=MESH
+        )
+        C.start(k)
+    loads[3].wait()
+    two_t[...] = two[...].T
+    for k in range(2):
+        C.panel(k).wait_send()
+        up_panel(B.sibling_target(k), ship, k)
+        pl.semaphore_wait(credit.at[k], 1)
+        B.ship(k)
+
+    for z in range(4):
+        if z < 3:
+            tile(wb, z + 1).start()
+        tile(wb, z).wait()
+
+        def part(start, size):
+            value = nt(gp[:, z * s.cols : (z + 1) * s.cols], wt[z % 2, pl.ds(start, size), :])
+            if z:
+                value = value + acc[:, pl.ds(start, size)]
+            acc[:, pl.ds(start, size)] = value
+
+        by_columns(s.width, part)
+        if z == 1:
+            C.turn(0)
+    tile(wa, 0, s.out_tile).start()
+    for k in range(2):
+        B.wait_panel(k)
+        up_panel(B.target(k), own_b, k, came)
+        B.start(k)
+        if k == 0:
+            C.turn(1)
+    C.land(0)
+    C.along(0)
+    loads[4].wait()
+
+    def norm(r):
+        given = cot[r, :].astype(f32)
+        back, gain, shift = norm_back(
+            res[r, : s.width], acc[r, : s.width], vec[5:6, : s.width]
+        )
+        total_r = given + back
+        res[r, : s.width] = total_r
+        low = to_low(total_r)
+        branch[r, : s.width] = low
+        sums[4:5, : s.width] += jnp.sum(low.astype(f32), axis=0, keepdims=True)
+        sums[5:6, : s.width] += gain
+        sums[6:7, : s.width] += shift
+        sums[7:8, : s.width] += jnp.sum(given, axis=0, keepdims=True)
+
+    branch[...] = jnp.zeros_like(branch)
+    by_rows(s.half, LANES, norm)
+    C.land(1)
+    C.along(1)
+    B.turn(0)
+
+    for z in range(4):
+        if z < 3:
+            tile(wa, z + 1, s.out_tile).start()
+        tile(wa, z, s.out_tile).wait()
+        source = z * s.out
+        base = source // LANES * LANES
+        size = s.cols - s.out_tile
+        moved = place_run(
+            branch[:, base : base + size].astype(f32), source - base, s.qkv - s.out_tile, s.out
+        )
+        oz[z] = to_low(moved)
+
+        def part(start, count):
+            value = nt(oz[z], wt[z % 2, pl.ds(start, count), :size])
+            if z:
+                value = value + acc[:, pl.ds(start, count)]
+            acc[:, pl.ds(start, count)] = value
+
+        by_columns(s.width, part)
+    B.turn(1)
+    branch_low = two
+    branch_low[...] = branch[:, : s.width]
+    lane = lax.broadcasted_iota(jnp.int32, (s.half, s.wide), 1)
+    branch[...] = to_low(jnp.where(lane < s.width, acc[...], 0.0))
+    saves = fetch_all(((res, gres_o), (branch_low, branch_o), (branch, gatt_o), (oz, oz_o)), save)
+    B.land(0)
+    B.along(0)
+    C.finish(False)
+    B.land(1)
+    B.along(1)
+    B.finish()
+    for copy in saves:
+        copy.wait()
+    seq_out.wait()
+    seq_out.drain()
+
+
+def last_kernel(s, *refs):
+    (wa, oz_i, dq_i, own_i, sib_i, normed_i, att_i, x_i, gres_i, vec, sums, tops) = refs[:12]
+    (qkv_o, gin_o, small_o, line_a) = refs[12:16]
+    (came_d, own_d, dq, wide, qz, oz, norm_t, att_t, normed, att, x, gres, wt, acc, gin, buf, got) = refs[16:33]
+    (ship, own_a, came_a, first_a, second_a, total, stage) = refs[33:40]
+    sems = refs[40:]
+    net = Net()
+    A = Scatter(net, s, own_a, ship, came_a, first_a, second_a, line_a, total, qkv_o, stage, sems[:12])
+    seq_in = FromSequences(net, gin, gin_o, sems[12:14])
+    load, tiles, ds, dr, gs, gr = sems[14:20]
+    loads = fetch_all(
+        ((dq_i, dq), (own_i, own_d), (normed_i, normed), (att_i, att), (oz_i, oz), (x_i, x), (gres_i, gres)),
+        load,
+    )
+    enter(net)
+    swap = pltpu.make_async_remote_copy(
+        sib_i, came_d, ds, dr, device_id=net.sib, device_id_type=MESH
+    )
+    swap.start()
+
+    def tile(j):
+        return pltpu.make_async_copy(
+            wa.at[:, pl.ds(j * s.cols, s.qkv_pad)], wt.at[j % 2], tiles.at[j % 2]
+        )
+
+    tile(0).start()
+    loads[2].wait()
+    norm_t[...] = normed[...].T
+    loads[3].wait()
+    att_t[...] = att[...].T
+    loads[0].wait()
+    loads[1].wait()
+    buf[...] = sums[...]
+    wide[:, : s.wide] = dq[...].astype(f32)
+    swap.wait()
+    for kind in range(2):
+        lanes = slice((kind + 1) * s.wide, (kind + 2) * s.wide)
+        value = to_low(own_d[kind].astype(f32) + came_d[kind].astype(f32)).astype(f32)
+        wide[:, lanes] = value
+    buf[2:3, :] = jnp.sum(wide[:, : s.wide], axis=0, keepdims=True)
+    buf[3:4, :] = jnp.sum(wide[:, 2 * s.wide :], axis=0, keepdims=True)
+    for z in range(4):
+        block = 0.0
+        for source, target, count in s.qkv_runs(z):
+            base = target // LANES * LANES
+            moved = place_run(
+                wide[:, base : base + s.qkv_pad], target - base, source, count
+            )
+            if moved.shape[1] < s.qkv_pad:
+                moved = jnp.concatenate(
+                    [moved, jnp.zeros((s.half, s.qkv_pad - moved.shape[1]), f32)], axis=1
+                )
+            block = block + moved
+        qz[z] = to_low(block)
+    loads[4].wait()
+
+    def panel(z, dst, k, came=None):
+        def put(start, size, value):
+            lanes = pl.ds(start, size)
+            if came is not None:
+                value = value + came[k, :, lanes].astype(f32)
+            dst[k, :, lanes] = to_low(value)
+
+        def part(start, size):
+            put(start, size, product(norm_t[...], qz[z, :, pl.ds(start, size)]))
+
+        by_columns(s.out_tile, part)
+        mixed = product(norm_t[...], qz[z, :, s.out_tile :]) + product(
+            att_t[: s.width, :], oz[z, :, : s.qkv_pad - s.out_tile]
+        )
+        put(s.out_tile, s.qkv_pad - s.out_tile, mixed)
+        rest = product(att_t[: s.width, :], oz[z, :, s.qkv_pad - s.out_tile :])
+        put(s.qkv_pad, s.cols - s.qkv_pad, rest)
+
+    for k in range(2):
+        panel(A.sibling_target(k), ship, k)
+        A.ship(k)
+    for z in range(2):
+        tile(z + 1).start()
+        tile(z).wait()
+        through(s, acc, qz, wt, z)
+    for k in range(2):
+        A.wait_panel(k)
+        panel(A.target(k), own_a, k, came_a)
+        A.start(k)
+    for z in range(2, 4):
+        if z < 3:
+            tile(z + 1).start()
+        tile(z).wait()
+        through(s, acc, qz, wt, z)
+    loads[5].wait()
+    loads[6].wait()
+
+    def norm(r):
+        back, gain, shift = norm_back(
+            x[r, :].astype(f32), acc[r, : s.width], vec[0:1, : s.width]
+        )
+        gin[r, :] = to_low(gres[r, : s.width] + back)
+        buf[0:1, : s.width] += gain
+        buf[1:2, : s.width] += shift
+
+    by_rows(s.half, LANES, norm)
+    seq_in.start()
+
+    def exchange(i, to):
+        return pltpu.make_async_remote_copy(
+            buf, got.at[i], gs.at[i], gr.at[i], device_id=to, device_id_type=MESH
+        )
+
+    def join(one, two):
+        row = lax.broadcasted_iota(jnp.int32, one.shape, 0)
+        return jnp.where(row == 12, jnp.maximum(one, two), one + two)
+
+    row = lax.broadcasted_iota(jnp.int32, buf.shape, 0)
+    buf[...] = jnp.where(row == 12, tops[0:1, :], buf[...])
+    partners = (net.sib, net.x_to, net.y_to)
+
+    def merge(i):
+        exchange(i, partners[i]).wait()
+        buf[...] = join(buf[...], got[i])
+
+    exchange(0, partners[0]).start()
+    A.turn(0)
+    merge(0)
+    exchange(1, partners[1]).start()
+    A.turn(1)
+    merge(1)
+    exchange(2, partners[2]).start()
+    A.land(0)
+    A.along(0)
+    merge(2)
+
+    def around(z):
+        return pltpu.make_async_remote_copy(
+            buf, got.at[3 + net.z], gs.at[3 + z], gr.at[3 + net.z], device_id=(net.d, z), device_id_type=MESH
+        )
+
+    for z in range(4):
+
+        @pl.when(z != net.z)
+        def _():
+            around(z).start()
+
+        @pl.when(z == net.z)
+        def _():
+            pltpu.make_async_copy(buf, got.at[3 + z], gr.at[3 + z]).start()
+
+    A.land(1)
+    A.along(1)
+    for z in range(4):
+        pltpu.make_async_copy(buf, got.at[3 + z], gr.at[3 + z]).wait()
+
+        @pl.when(z != net.z)
+        def _():
+            around(z).wait_send()
+
+    small_o[...] = join(join(got[3], got[4]), join(got[5], got[6]))
+    A.finish()
+    seq_in.wait()
+    seq_in.drain()
+
+
+def through(s, acc, qz, wt, z):
+    def part(start, size):
+        value = nt(qz[z], wt[z % 2, pl.ds(start, size), :])
+        if z:
+            value = value + acc[:, pl.ds(start, size)]
+        acc[:, pl.ds(start, size)] = value
+
+    by_columns(s.width, part)
+
+
+def middle_call(s, shape, wa, wb, wc, cot, res, two, slope, hid, out, vec):
+    dma = pltpu.SemaphoreType.DMA
+    rows, full = s.half, s.ctx * s.cols
+    anywhere = pl.BlockSpec(memory_space=pl.ANY)
+    local = pl.BlockSpec(memory_space=pltpu.VMEM)
+    low = lambda *dims: jax.ShapeDtypeStruct(dims, bf16)
+    high = lambda *dims: jax.ShapeDtypeStruct(dims, f32)
+    size = s.cols - s.out_tile
+    line = low(2, 2, s.rows, s.cols)
+    return pl.pallas_call(
+        partial(middle_kernel, s),
+        out_shape=[
+            high(s.rows, s.cols), high(s.rows, s.cols), high(rows, s.wide), low(rows, s.width),
+            low(rows, s.wide), low(4, rows, size), high(16, s.wide), low(*shape), line, line,
+        ],
+        in_specs=[anywhere] * 9 + [local],
+        out_specs=[anywhere] * 6 + [local] + [anywhere] * 3,
+        scratch_shapes=[
+            pltpu.VMEM((rows, s.width), bf16),
+            pltpu.VMEM((rows, s.wide), f32),
+            pltpu.VMEM((rows, s.width), bf16),
+            pltpu.VMEM((rows, full), bf16),
+            pltpu.VMEM((rows, full), bf16),
+            pltpu.VMEM((s.width, rows), bf16),
+            pltpu.VMEM((s.width, rows), bf16),
+            pltpu.VMEM((2, s.width, s.cols), bf16),
+            pltpu.VMEM((rows, s.wide), f32),
+            pltpu.VMEM((rows, s.wide), bf16),
+            pltpu.VMEM((4, rows, size), bf16),
+        ]
+        + scatter_scratch(s, 2)
+        + scatter_sems() * 2
+        + [dma((2,)), dma((2,)), dma((5,)), dma((2,)), dma((4,)), pltpu.SemaphoreType.REGULAR((2,))],
+        compiler_params=pltpu.CompilerParams(
+            collective_id=2, has_side_effects=True, vmem_limit_bytes=63 * 2**20
+        ),
+        name="middle",
+    )(wa, wb, wc, cot, res, two, slope, hid, out, vec)
+
+
+def last_call(s, shape, wa, oz, dq, d_own, d_sib, normed, att, x, gres, vec, sums, tops):
+    dma = pltpu.SemaphoreType.DMA
+    rows = s.half
+    anywhere = pl.BlockSpec(memory_space=pl.ANY)
+    local = pl.BlockSpec(memory_space=pltpu.VMEM)
+    low = lambda *dims: jax.ShapeDtypeStruct(dims, bf16)
+    high = lambda *dims: jax.ShapeDtypeStruct(dims, f32)
+    size = s.cols - s.out_tile
+    return pl.pallas_call(
+        partial(last_kernel, s),
+        out_shape=[
+            high(s.rows, s.cols), low(*shape), high(16, s.wide), low(2, 2, s.rows, s.cols),
+        ],
+        in_specs=[anywhere] * 9 + [local] * 3,
+        out_specs=[anywhere, anywhere, local, anywhere],
+        scratch_shapes=[
+            pltpu.VMEM((2, rows, s.wide), bf16),
+            pltpu.VMEM((2, rows, s.wide), bf16),
+            pltpu.VMEM((rows, s.wide), bf16),
+            pltpu.VMEM((rows, 3 * s.wide), f32),
+            pltpu.VMEM((4, rows, s.qkv_pad), bf16),
+            pltpu.VMEM((4, rows, size), bf16),
+            pltpu.VMEM((s.width, rows), bf16),
+            pltpu.VMEM((s.wide, rows), bf16),
+            pltpu.VMEM((rows, s.width), bf16),
+            pltpu.VMEM((rows, s.wide), bf16),
+            pltpu.VMEM((rows, s.width), bf16),
+            pltpu.VMEM((rows, s.wide), f32),
+            pltpu.VMEM((2, s.width, s.qkv_pad), bf16),
+            pltpu.VMEM((rows, s.wide), f32),
+            pltpu.VMEM((rows, s.width), bf16),
+            pltpu.VMEM((16, s.wide), f32),
+            pltpu.VMEM((7, 16, s.wide), f32),
+        ]
+        + scatter_scratch(s, 1)
+        + scatter_sems()
+        + [dma((2,)), dma((2,)), dma((7,)), dma((2,)), dma, dma, dma((7,)), dma((7,))],
+        compiler_params=pltpu.CompilerParams(
+            collective_id=3, has_side_effects=True, vmem_limit_bytes=63 * 2**20
+        ),
+        name="last",
+    )(wa, oz, dq, d_own, d_sib, normed, att, x, gres, vec, sums, tops)
 
 
 def slot_info(moves, segment_ids, padding, stretch_order):
@@ -1064,89 +1721,32 @@
     wide = s.wide
     kinfo, qinfo = slot_info(moves, segment_ids, padding, stretch_order)
     own_a, own_b, own_c, small = pack_blocks(moves, s, w_qkv, w_out, w_up, w_down, vectors, bias_up)
-    (wa, wb, wc, x_low, cot, vec, normed, queries, kv, attended, residual, normed_two, slope, hidden, lse, tops, output) = forward_call(
+    (wa, wb, wc, x, cot, vec, normed, queries, kv, attended, residual, two, slope, hidden, lse, tops, out) = forward_call(
         s, own_a, own_b, own_c, small, inputs, cotangent, kinfo, qinfo
     )
-    vec_rows = vec[:8, :width]
-    attended = attended[:, :width]
-    residual = residual[:, :width]
-
-    def unpad(values, size):
-        return values.reshape(values.shape[0], ctx, s.cols)[:, :, :size].reshape(values.shape[0], -1)
-
-    wide_qkv = unpad(wa, s.qkv)
-    wide_out = wa.reshape(width, ctx, s.cols)[:, :, s.qkv : s.qkv + s.out].reshape(width, -1)
-    wide_up = unpad(wb, s.up)
-    down_t = unpad(wc, s.up)
-    hidden = unpad(hidden, s.up)
-    slope = unpad(slope, s.up)
-    x_flat = x_low.astype(f32)
-    own, sib = kv[:, : s.half], kv[:, s.half :]
+    down_block, up_block, gres, _, gatt, oz, sums, output, _, _ = middle_call(
+        s, inputs.shape, wa, wb, wc, cot, residual, two, slope, hidden, out, vec
+    )
+    dq, d_own, d_sib = attend_backward(heads, kinfo, qinfo, queries, kv, gatt, lse)
+    block_top = jnp.max(tops, axis=2).reshape(1, -1)[:, :heads]
+    block_top = jnp.pad(block_top, ((0, 7), (0, wide - heads)))
+    qkv_block, grad_input, small_sums, _ = last_call(
+        s, inputs.shape, wa, oz, dq, d_own, d_sib, normed, attended, x, gres, vec, sums, block_top
+    )
+    rows_d = w_qkv.shape[0]
     cols_q, cols_d, cols_f = w_qkv.shape[1], w_out.shape[1], w_up.shape[1]
-    rows_d, ratio = w_qkv.shape[0], w_down.shape[0] // w_qkv.shape[0]
-    block_top = jnp.max(tops, axis=2).reshape(-1)[:heads]
-    global_top = lax.pmax(block_top, AXES)
-
-    def padded(values):
-        return jnp.pad(to_low(values), ((0, 0), (0, wide - width)))
-
-    grad_output = cot.astype(f32)
-    grad_bias_two = column_sum(cot)
-    sum_down = moves.scatter_dp(moves.weight_terms(hidden, cot))
-    grad_hidden = product(cot, down_t)
-    grad_pre = to_low(grad_hidden * slope.astype(f32))
-    grad_bias_up = column_sum(grad_pre)
-    sum_up = moves.weight_terms(normed_two, grad_pre)
-    sum_up = moves.scatter_dp(sum_up)
-    unused, norm_back_two = jax.vjp(layer_norm, residual, vec_rows[5], vec_rows[6])
-    back_two = norm_back_two(contract_cols(grad_pre, wide_up))
-    grad_residual = grad_output + back_two[0]
-    grad_branch = to_low(grad_residual)
-    sum_out = moves.weight_terms(attended, grad_branch)
-    sum_out = moves.scatter_dp(sum_out)
-    grad_attended = padded(contract_cols(grad_branch, wide_out))
-    dq, d_own, d_sib = attend_backward(
-        heads, kinfo, qinfo, queries, own, sib, grad_attended, lse
-    )
-    d_came = moves.swap_core(d_sib)
-    d_own = to_low(d_own.astype(f32) + d_came.astype(f32))
-    grad_proj = jnp.concatenate([dq[:, :width], d_own[0, :, :width], d_own[1, :, :width]], axis=1)
-    sum_qkv = moves.weight_terms(normed, grad_proj)
-    sum_qkv = moves.scatter_dp(sum_qkv)
-    unused, norm_back_one = jax.vjp(layer_norm, x_flat, vec_rows[0], vec_rows[1])
-    back_one = norm_back_one(contract_cols(grad_proj, wide_qkv))
-    grad_input = to_low(grad_residual + back_one[0])
-    grad_input = moves.from_sequences(grad_input).astype(f32)
-    grad_vectors = jnp.stack(
-        [
-            back_one[1],
-            back_one[2],
-            column_sum(dq[:, :width]),
-            column_sum(d_own[1, :, :width]),
-            column_sum(grad_branch),
-            back_two[1],
-            back_two[2],
-            grad_bias_two,
-        ]
-    )
-
-    def by_place(values):
-        return jnp.swapaxes(values.reshape(values.shape[0], ctx, -1), 0, 1)
-
-    blocks_down = sum_down.reshape(ratio, rows_d, ctx, cols_d)
-    blocks_down = jnp.transpose(blocks_down, (2, 1, 0, 3)).reshape(ctx, rows_d, -1)
-    later = jnp.concatenate([by_place(sum_up), blocks_down, by_place(sum_out)], axis=2)
-    later = moves.scatter_ctx(later)
-    grad_up = later[:, :cols_f]
-    grad_down = later[:, cols_f : 2 * cols_f].reshape(rows_d, ratio, cols_d)
-    grad_down = jnp.swapaxes(grad_down, 0, 1).reshape(ratio * rows_d, cols_d)
-    grad_out = later[:, 2 * cols_f :]
-    grad_qkv = moves.scatter_ctx(by_place(sum_qkv))
-
-    tiny = jnp.concatenate([grad_vectors, grad_bias_up.reshape(-1, width)], axis=0)
-    tiny = lax.psum(tiny, AXES)
-    grad_vectors = lax.dynamic_slice_in_dim(tiny[:8], place * cols_d, cols_d, 1)
-    grad_bias = lax.dynamic_slice_in_dim(tiny[8:].reshape(-1), place * cols_f, cols_f)
+    ff = w_down.shape[0]
+
+    def own_rows(block):
+        return jnp.where(core == 0, block[:rows_d], block[rows_d:])
+
+    qkv_block, up_block = own_rows(qkv_block), own_rows(up_block)
+    grad_qkv, grad_out = qkv_block[:, :cols_q], qkv_block[:, cols_q : cols_q + cols_d]
+    grad_up = up_block[:, :cols_f]
+    grad_down = jnp.where(core == 0, down_block[:, :ff], down_block[:, ff : 2 * ff]).T
+    grad_vectors = lax.dynamic_slice_in_dim(small_sums[:8, :width], place * cols_d, cols_d, 1)
+    grad_bias = lax.dynamic_index_in_dim(small_sums[8:12], place, 0, False)[:cols_f]
+    global_top = small_sums[12, :heads]
 
     factor = clip_limit / jnp.maximum(global_top, clip_limit)
     per_column = jnp.repeat(jnp.sqrt(factor), HD)
@@ -1157,7 +1757,7 @@
     clipped_bias = to_low(vectors[2].astype(f32) * bias_scale)
     return (
         output,
-        grad_input,
+        grad_input.astype(f32),
         grad_qkv,
         grad_out,
         grad_up,
@@ -1286,7 +1886,7 @@
     sum_out = moves.scatter_dp(sum_out)
     grad_attended = padded(contract_cols(grad_branch, wide_out))
     dq, d_own, d_sib = attend_backward(
-        heads, kinfo, qinfo, queries, own, sib, grad_attended, lse
+        heads, kinfo, qinfo, queries, jnp.concatenate([own, sib], axis=1), grad_attended, lse
     )
     d_came = moves.swap_core(d_sib)
     d_own = to_low(d_own.astype(f32) + d_came.astype(f32))

time: 898 us -> 561 us (0.62); the launches traced: 881 us -> 555 us
  Pallas kernels: 278 us -> 521 us
  local copies, waits for them, and re-layouts: 207 us -> 19.4 us
  waiting for transfers between devices: 112 us -> 0.01 us
  blocking collectives: 86.5 us -> 0 us
  matrix products: 74.4 us -> 0 us
  other arithmetic: 67.2 us -> 12.8 us
  starting transfers between devices: 54.2 us -> 0.57 us
    pallas_call x0 -> x2, Pallas kernels: none -> 275 us  [the longest x1 158 us: middle_call(): pl.pallas_call(partial(middle_kernel, s), out_shape=[high(s.rows, s.cols)...]
    ppermute x37 -> x2, waiting for transfers between devices: 112 us -> 0.01 us  [permute(): return lax.ppermute(values, AXES, pairs)]
    reshape x21 -> x1, local copies, waits for them, and re-layouts: 103 us -> 0.08 us  [fast_shards(): block_top = jnp.max(tops, axis=2).reshape(1, -1)[:, :heads]]
    dot_general x12 -> x0, matrix products: 74.4 us -> none  [the longest x8 37.2 us: contract_rows(): lax.dot_general(left, right, (((0,), (0,)), ((), ())), preferred_element_...]
    ppermute x37 -> x2, starting transfers between devices: 54.2 us -> 0.57 us  [permute(): return lax.ppermute(values, AXES, pairs)]
    pmax x1 -> x0, blocking collectives: 46 us -> none  [fast_shards(): global_top = lax.pmax(block_top, AXES)]
    psum x1 -> x0, blocking collectives: 40.5 us -> none  [fast_shards(): tiny = lax.psum(tiny, AXES)]
    pallas_call x1, Pallas kernels: 243 us -> 212 us  [forward_call(): pl.pallas_call(partial(forward_kernel, s), out_shape=out_shape, in_specs=...]
  transfers between devices with their start and end apart: 37 -> 2, of which waited for: 13 -> 0; matrix products, arithmetic and copies ran while one was open for 32% -> 1% of each run, Pallas kernels for 4% -> 0%
where the time goes in v3:
time: 561 us; the launch traced here: 555 us
  Pallas kernels  521 us (93%)
  local copies, waits for them, and re-layouts  19.4 us (3%)
  other arithmetic  12.8 us (2%)
    pallas_call x1, Pallas kernels, forward_call(): pl.pallas_call(partial(forward_kernel, s), out_shape=out_shape, in_specs=...  212 us
    pallas_call x1, Pallas kernels, middle_call(): pl.pallas_call(partial(middle_kernel, s), out_shape=[high(s.rows, s.cols)...  158 us
    pallas_call x1, Pallas kernels, last_call(): pl.pallas_call(partial(last_kernel, s), out_shape=[high(s.rows, s.cols),...  117 us
    pallas_call x1, Pallas kernels, attend_backward(): pl.pallas_call(partial(attend_backward_kernel, heads), grid=(pairs,), in_...  34.1 us
    unnamed x45, local copies, waits for them, and re-layouts  11.7 us
  transfers between devices with their start and end apart: 2, of which 0 were waited for; matrix products, arithmetic and copies ran while one was open for 1% of the time, Pallas kernels for 0%

profile of v3, /device:TPU:0, one launch (start us, length us, event | category | flops | bytes accessed | tf_op | source)
XLA Modules:
  0.0 554.9 jit_solution(14723959354417125494)
XLA Ops:
  0.6 0.0 copy-start.9
  0.7 1.1 fusion.29
  1.7 1.1 fusion.15
  2.9 0.0 copy-start.15
  2.9 0.0 copy-start.16
  2.9 0.0 copy-start.19
  2.9 0.0 copy-start.18
  2.9 0.0 copy-start.17
  3.0 0.0 copy-start.11
  3.0 0.0 copy-done.9
  3.0 1.0 fusion.7
  4.0 0.5 collective-permute-start
  4.4 0.1 collective-permute-start.1
  4.6 0.1 add.83
  4.7 0.1 broadcast_bitcast_fusion
  4.9 0.0 copy-done.11
  4.9 1.4 copy.40.refs_4_
  6.3 0.0 copy-done.12
  6.3 1.4 copy.41.refs_5_
  7.7 0.6 pad.36.refs_3_
  8.3 0.0 collective-permute-done.1
  8.3 0.6 gather_fusion
  8.9 0.1 select_bitcast_fusion.1
  9.1 0.0 copy-start.2
  9.1 1.0 copy.42.refs_6_.kinfo_ref
  10.2 0.0 collective-permute-done
  10.2 1.5 broadcast_select_fusion.1
  11.7 0.1 fusion.25
  11.8 0.1 fusion.27
  11.9 0.1 fusion.26
  12.0 0.1 fusion.28
  12.1 0.9 pad_maximum_fusion.1.refs_1_
  12.9 0.9 pad_maximum_fusion.refs_0_
  13.8 1.0 fusion.9.refs_2_
  14.8 211.7 %forward.1 = (bf16[1088,4608]{1,0:T(8,128)(2,1)}, bf16[1088,4608]{1,0:T(8,128)(2,1)}, bf16[1088,4608]{1,0:T(8,128)(2,1)}, bf16[512,1088]{1,0:T(8,128)(2,1)}, bf1...) custom-call(bf16[272,1152]{1,0:T(8,128)(2,1)} %pad_maximum_fusion.re, ...), custom_call_target="tpu_custom_call" | custom-call | tf_op jit(solution)/shard_map/forward/pallas_call | solution.py:965
  226.5 0.9 reduce_max.9
  227.4 0.1 reshape.56
  227.4 0.6 pad.37.refs_11_
  228.1 158.0 %middle.1 = (f32[272,1152]{1,0:T(8,128)}, f32[272,1152]{1,0:T(8,128)}, f32[512,1152]{1,0:T(8,128)}, bf16[512,1088]{1,0:T(8,128)(2,1)}, bf16[512,1152]{1,0:T(8,12...) custom-call(bf16[1088,4608]{1,0:T(8,128)(2,1)} %get-tuple-element.41, ...), custom_call_target="tpu_custom_call" | custom-call | tf_op jit(solution)/shard_map/middle/pallas_call | solution.py:1567
  386.1 0.0 copy-done
  386.1 0.0 copy-done.3
  386.2 1.3 copy-done.4
  387.4 1.3 copy-done.5
  388.7 34.1 %attend_backward.1 = (bf16[512,1152]{1,0:T(8,128)(2,1)S(1)}, bf16[2,512,1152]{2,1,0:T(8,128)(2,1)}, bf16[2,512,1152]{2,1,0:T(8,128)(2,1)}) custom-call(s32[1024,2]{1,0:T(8,128)S(1)} %copy-done, s32[1,512]{1,0:T(1,128)S(1)} %copy-done.3, bf16[512,1152]{1,0:T(8,128)(2,1)S(1)} %copy-done.4, bf16[2,1024,1152]{2,1,0:T(8,128)(2,1)} %get-tuple-element.54.own_ref.sib_ref, ...), custom_call_target="tpu_custom_call" | custom-call | flops 12079595520 | bytes 12976128 | tf_op jit(solution)/shard_map/attend_backward/pallas_call | solution.py:336
  422.8 1.0 copy-done.1
  423.8 116.7 %last.1 = (f32[272,1152]{1,0:T(8,128)}, bf16[2,256,1088]{2,1,0:T(8,128)(2,1)}, f32[16,1152]{1,0:T(8,128)}, bf16[2,2,272,1152]{3,2,1,0:T(8,128)(2,1)}) custom-call(bf16[1088,4608]{1,0:T(8,128)(2,1)} %get-tuple-element.41.refs_0_, bf16[4,512,384]{2,1,0:T(8,128)(2,1)} %get-tuple-element.52.refs_1_, bf16[512,1152]{1,0:T(8,128)(2,1)} %copy-done.1, ...), custom_call_target="tpu_custom_call" | custom-call | tf_op jit(solution)/shard_map/last/pallas_call | solution.py:1606
  540.6 1.4 slice_select_fusion.1
  542.0 0.8 slice.126
  542.8 0.8 slice.127
  543.6 0.5 divide_sqrt_fusion
  544.2 0.1 fusion.24
  544.3 1.2 copy-done.10
  545.4 1.7 copy.45
  547.1 0.1 broadcast_in_dim.29
  547.2 0.1 reshape.57
  547.3 0.1 concatenate.47
  547.4 0.1 dynamic_slice.37
  547.4 0.7 multiply_convert_fusion
  548.2 0.7 constant_dynamic-slice_fusion
  548.9 0.6 multiply_convert_fusion.1
  549.5 2.3 copy.44
  551.8 1.1 select_bitcast_fusion
  552.9 0.9 slice_select_fusion
  553.8 0.6 dynamic-slice_reduce_fusion
  (44 shorter events, 0.2 us)
Async XLA Ops:
  0.6 2.3 copy-start.9
  2.9 1.5 copy-start.15
  2.9 1.5 copy-start.16
  2.9 1.6 copy-start.19
  2.9 1.8 copy-start.18
  2.9 1.8 copy-start.17
  3.0 1.9 copy-start.11
  4.0 2.3 copy-start.12
  4.0 6.2 %collective-permute-start = (bf16[408,1152]{1,0:T(8,128)(2,1)}, bf16[408,1152]{1,0:T(8,128)(2,1)}, u32[]{:S(2)}, u32[]{:S(2)}) collective-permute-start(bf16[408,1152]{1,0:T(8,128)(2,1)} %fusion.7), channel_id=1, source_target_pairs={{0,4},{1,5},{2,6},{3,7},{4,0},{5,1},{6,2},{7,3},{8,12},{9,13},{10,... | collective-permute-start | bytes 2820104 | tf_op jit(solution)/shard_map/ppermute | solution.py:66
  4.4 3.9 collective-permute-start.1
  9.1 2.6 copy-start.2
  228.1 158.0 %copy-start = (s32[1024,2]{1,0:T(8,128)S(1)}, s32[1024,2]{1,0:T(8,128)}, u32[]{:S(2)}) copy-start(s32[1024,2]{1,0:T(8,128)} %copy.42.refs_6_.kinfo_ref) | copy-start | bytes 24580
  228.1 158.1 %copy-start.3 = (s32[1,512]{1,0:T(1,128)S(1)}, s32[1,512]{1,0:T(1,128)}, u32[]{:S(2)}) copy-start(s32[1,512]{1,0:T(1,128)} %copy-done.2) | copy-start | bytes 6148
  228.1 158.1 %copy-start.6 = (f32[9,2,512]{2,1,0:T(2,128)S(1)}, f32[9,2,512]{2,1,0:T(2,128)}, u32[]{:S(2)}) copy-start(f32[9,2,512]{2,1,0:T(2,128)} %get-tuple-element.56.lse_ref) | copy-start | bytes 110596
  386.1 1.3 copy-start.4
  387.4 1.3 copy-start.5
  422.8 1.0 copy-start.1
  540.6 3.1 copy-start.14
  540.6 3.6 copy-start.8
  544.2 1.3 copy-start.10
  545.4 2.0 copy-start.13
  548.2 3.6 copy-start.7

commit v4 on v3

--- a/solution.py
+++ b/solution.py
@@ -719,10 +719,10 @@
 
 def forward_kernel(s, *refs):
     (own_a, own_b, own_c, small, inp, cot, kinfo, qinfo) = refs[:8]
-    (wa, wb, wc, x_o, cot_o, vec, normed_o, q_o, kv_o, att_o, res_o, two_o, slope_o, hid_o) = refs[8:22]
+    (wa_o, wb_o, wc_o, x_o, cot_o, vec, normed_o, q_o, kv_o, att_o, res_o, two_o, slope_o, hid_o) = refs[8:22]
     (lse, top, out_o) = refs[22:25]
-    (x, normed, pre, q, kv, bias, att, res, two, slope, hid, wt, ct, out, smalls) = refs[25:40]
-    sems = refs[40:]
+    (x, normed, q, kv, bias, att, res, two, wa, wb, wc, out, smalls) = refs[25:38]
+    sems = refs[38:]
     net = Net()
     A, B, C = [
         Gather(net, s, w, own, swapped, sems[7 * g : 7 * g + 7])
@@ -732,7 +732,7 @@
     ]
     seq_x = ToSequences(net, inp, x, sems[21:23])
     seq_cot = ToSequences(net, cot, cot_o, sems[23:25])
-    small_s, small_r, kv_s, kv_r, load, save = sems[25:31]
+    small_s, small_r, kv_s, kv_r, save = sems[25:30]
     near, far = net.near, net.far
     saves = []
 
@@ -773,7 +773,6 @@
     diff = qinfo[0:1, :] - kinfo[:, 0:1]
     fine = (diff >= 0) & (diff <= kinfo[:, 1:2])
     bias[...] = jnp.where(fine, 0.0, masked_fill)
-    pre[...] = jnp.zeros_like(pre)
     at("vectors")
 
     for z in range(4):
@@ -802,34 +801,30 @@
     at("normed")
     A.ready()
 
-    def tile_a(z):
-        return pltpu.make_async_copy(
-            wa.at[:, pl.ds(z * s.cols, s.cols)], wt.at[z % 2], load.at[z % 2]
-        )
-
-    def tile_b(z):
-        return pltpu.make_async_copy(
-            wb.at[:, pl.ds(z * s.cols, s.cols)], wt.at[z % 2], load.at[z % 2]
-        )
-
-    tile_a(0).start()
+    wa_saved = len(saves)
+    keep(wa, wa_o)
+    q[...] = jnp.zeros_like(q)
+    kv[:, : s.half, :] = jnp.zeros((2, s.half, s.wide), bf16)
+    places = (q, kv.at[0, pl.ds(0, s.half)], kv.at[1, pl.ds(0, s.half)])
     for z in range(4):
-        if z < 3:
-            tile_a(z + 1).start()
-        tile_a(z).wait()
 
         def part(start, size):
-            res[:, pl.ds(start, size)] = product(normed[...], wt[z % 2, :, pl.ds(start, size)])
+            lanes = pl.ds(pl.multiple_of(z * s.cols + start, LANES), size)
+            res[:, pl.ds(start, size)] = product(normed[...], wa[:, lanes])
 
         by_columns(s.qkv_cols, part)
         for source, target, count in s.qkv_runs(z):
-            base = target // LANES * LANES
-            moved = place_run(res[:, : s.qkv_cols], source, target - base, count)
-            pre[:, base : base + moved.shape[1]] += moved
+            kind, first = target // s.wide, target % s.wide
+            base = first // LANES * LANES
+            moved = place_run(res[:, : s.qkv_cols], source, first - base, count)
+            lanes = slice(base, base + moved.shape[1])
+            if kind != 1:
+                lane = lax.broadcasted_iota(jnp.int32, (1, moved.shape[1]), 1)
+                fits = (lane >= first - base) & (lane < first - base + count)
+                moved = moved + jnp.where(fits, vec[2 + kind // 2 : 3 + kind // 2, lanes], 0.0)
+            place = places[kind]
+            place[:, lanes] = place[:, lanes] + to_low(moved)
         at("project", z)
-    tile_a(0).start()
-    kv[0, : s.half, :] = to_low(pre[:, s.wide : 2 * s.wide])
-    kv[1, : s.half, :] = to_low(pre[:, 2 * s.wide :] + vec[3:4, :])
     share = pltpu.make_async_remote_copy(
         kv.at[:, pl.ds(0, s.half)],
         kv.at[:, pl.ds(s.half, s.half)],
@@ -839,7 +834,6 @@
         device_id_type=MESH,
     )
     share.start()
-    q[...] = to_low(pre[:, : s.wide] + vec[2:3, :])
     at("share")
     share.wait()
     keep(q, q_o)
@@ -858,17 +852,15 @@
 
     res[...] = jnp.zeros_like(res)
     for z in range(4):
-        if z < 3:
-            tile_a(z + 1).start()
-        tile_a(z).wait()
-        block = product(att[:, : s.width], wt[z % 2, :, s.out_tile :])
+        lanes = slice(z * s.cols + s.out_tile, (z + 1) * s.cols)
+        block = product(att[:, : s.width], wa[:, lanes])
         target = z * s.out
         base = target // LANES * LANES
         moved = place_run(block, s.qkv - s.out_tile, target - base, s.out)
         res[:, base : base + moved.shape[1]] += moved
     at("second")
     B.ready()
-    tile_b(0).start()
+    keep(wb, wb_o)
 
     def second(r):
         total = res[r, : s.width] + x[r, :].astype(f32) + vec[4:5, : s.width]
@@ -879,18 +871,18 @@
     keep(res, res_o)
     keep(two, two_o)
 
+    A.drain()
+    saves[wa_saved].wait()
+    hid, slope = wa.at[pl.ds(0, s.half)], wa.at[pl.ds(s.half, s.half)]
     for z in range(4):
-        if z < 3:
-            tile_b(z + 1).start()
-        tile_b(z).wait()
 
         def part(start, size):
-            u = product(two[...], wt[z % 2, :, pl.ds(start, size)])
+            lanes = pl.ds(pl.multiple_of(z * s.cols + start, LANES), size)
+            u = product(two[...], wb[:, lanes])
             u = u + smalls[z, 8:9, pl.ds(start, size)].astype(f32)
             inner = math.sqrt(2 / math.pi) * (u + 0.044715 * u * u * u)
             t = jnp.tanh(inner)
             bend = math.sqrt(2 / math.pi) * (1 + 3 * 0.044715 * u * u)
-            lanes = pl.ds(pl.multiple_of(z * s.cols + start, LANES), size)
             hid[:, lanes] = to_low(0.5 * u * (1 + t))
             slope[:, lanes] = to_low(0.5 * (1 + t) + 0.5 * u * (1 - t * t) * bend)
 
@@ -901,24 +893,15 @@
     at("down")
     C.ready()
 
-    def tile_c(k):
-        count = min(3 * LANES, s.width - k * 3 * LANES)
-        return pltpu.make_async_copy(
-            wc.at[pl.ds(k * 3 * LANES, count)], ct.at[k % 2, pl.ds(0, count)], load.at[k % 2]
-        )
-
-    tile_c(0).start()
+    keep(wc, wc_o)
     for k in range(3):
-        if k < 2:
-            tile_c(k + 1).start()
-        tile_c(k).wait()
-        at, count = k * 3 * LANES, min(3 * LANES, s.width - k * 3 * LANES)
-        block = nt(hid[...], ct[k % 2, :count, :])
-        total = res[:, at : at + count] + block + vec[7:8, at : at + count]
-        out[:, at : at + count] = to_low(total)
+        first, count = k * 3 * LANES, min(3 * LANES, s.width - k * 3 * LANES)
+        block = nt(hid[...], wc[pl.ds(first, count), :])
+        total = res[:, first : first + count] + block + vec[7:8, first : first + count]
+        out[:, first : first + count] = to_low(total)
     keep(out, out_o)
     seq_cot.wait()
-    for group in (A, B, C):
+    for group in (B, C):
         group.drain()
     for z in range(4):
 
@@ -928,8 +911,9 @@
 
     seq_x.drain()
     seq_cot.drain()
-    for copy in saves:
-        copy.wait()
+    for i, copy in enumerate(saves):
+        if i != wa_saved:
+            copy.wait()
 
 
 def forward_call(s, own_a, own_b, own_c, small, inp, cot, kinfo, qinfo):
@@ -970,23 +954,21 @@
         scratch_shapes=[
             pltpu.VMEM((rows, s.width), bf16),
             pltpu.VMEM((rows, s.width), bf16),
-            pltpu.VMEM((rows, 3 * s.wide), f32),
             pltpu.VMEM((rows, s.wide), bf16),
             pltpu.VMEM((2, 2 * rows, s.wide), bf16),
             pltpu.VMEM((2 * rows, rows), f32),
             pltpu.VMEM((rows, s.wide), bf16),
             pltpu.VMEM((rows, s.wide), f32),
             pltpu.VMEM((rows, s.width), bf16),
-            pltpu.VMEM((rows, full), bf16),
-            pltpu.VMEM((rows, full), bf16),
-            pltpu.VMEM((2, s.width, s.cols), bf16),
-            pltpu.VMEM((2, 3 * LANES, full), bf16),
+            pltpu.VMEM((s.width, full), bf16),
+            pltpu.VMEM((s.width, full), bf16),
+            pltpu.VMEM((s.width, full), bf16),
             pltpu.VMEM((rows, s.width), bf16),
             pltpu.VMEM((4, 16, s.wide), bf16),
         ]
         + gather_sems() * 3
         + [dma((2,))] * 4
-        + [dma((4,)), dma((4,)), dma, dma, dma((2,)), dma((12,))],
+        + [dma((4,)), dma((4,)), dma, dma, dma((14,))],
         compiler_params=pltpu.CompilerParams(
             collective_id=1, has_side_effects=True, vmem_limit_bytes=61 * 2**20
         ),
@@ -995,11 +977,12 @@
 
 
 class Scatter:
-    def __init__(self, net, s, own, ship, came, first, second, line, total, out, stage, sems):
-        self.n, self.s = net, s
+    def __init__(self, net, s, own, ship, came, first, second, line, total, out, sums, sems):
+        self.n, self.s, self.sums = net, s, sums
         self.own, self.ship_ref, self.came = own, ship, came
         self.first_ref, self.second_ref, self.line = first, second, line
-        self.total, self.out, self.stage = total, out, stage
+        self.total, self.out = total, out
+        self.total_like = sums.at[0] if own is None else self.block(0, 0)
         (self.ps, self.pr, self.fs, self.fr, self.hs, self.hr, self.zs, self.zr, self.ld, self.es, self.er, self.eo) = sems
 
     def target(self, k):
@@ -1043,13 +1026,11 @@
             self.block(k, two), self.second_ref.at[k], self.hs.at[k], self.hr.at[k], to
         )
 
-    def step(self, k, up):
+    def along(self, k):
         n = self.n
-        t = self.target(k) // 2
-        to = (n.d, n.z + 1 if up else n.z - 1)
-        side = 0 if up else 1
+        src = self.block(k, n.p) if self.own is not None else self.sums.at[k]
         return self.remote(
-            self.block(k, n.p), self.line.at[t, side], self.zs.at[k], self.zr.at[t, side], to
+            src, self.line.at[n.z], self.zs.at[k], self.zr.at[n.z], (n.d, self.target(k))
         )
 
     def ship(self, k):
@@ -1085,80 +1066,59 @@
         self.piece(k).wait_recv()
         self.add(k, self.n.p, self.second_ref.at[k])
 
-    def fetch(self, k, side):
-        t = self.target(k) // 2
-        n = self.n
-        block = self.block(k, n.p)
-        self.remote(block, self.line.at[t, side], self.zs.at[k], self.zr.at[t, side], n.sib).wait_recv()
-        load = pltpu.make_async_copy(self.line.at[t, side], self.stage, self.ld)
-        load.start()
-        load.wait()
-
-    def along(self, k):
-        n, z, t = self.n, self.n.z, self.target(k)
-
-        @pl.when(t < z)
+    def send(self, k):
+        @pl.when(self.target(k) != self.n.z)
         def _():
-            @pl.when(z < 3)
-            def _():
-                self.fetch(k, 1)
-                self.add(k, n.p, self.stage)
-
-            self.step(k, False).start()
-
-        @pl.when(t > z)
+            self.along(k).start()
+
+    def mine(self):
+        return self.n.z % 2 == self.n.c
+
+    def collect(self, stage=None):
+        n, rows = self.n, self.s.rows
+
+        @pl.when(self.mine())
         def _():
-            @pl.when(z > 0)
-            def _():
-                self.fetch(k, 0)
-                self.add(k, n.p, self.stage)
-
-            self.step(k, True).start()
-
-        if k == 1:
-
-            @pl.when(t == z)
-            def _():
-                rows = self.s.rows
-
-                def begin(r):
-                    at = pl.ds(pl.multiple_of(n.p * rows + r.start, 16), r.size)
-                    self.total[r, :] = self.own[k, at, :].astype(f32)
-
-                by_rows(rows, 16, begin)
-
-                def more(r):
-                    self.total[r, :] += self.stage[r, :].astype(f32)
-
-                @pl.when(z > 0)
+            if self.own is None:
+                load = pltpu.make_async_copy(self.sums.at[1], stage, self.ld)
+                load.start()
+                load.wait()
+
+            def begin(r):
+                if self.own is None:
+                    value = stage[r, :]
+                else:
+                    value = self.own[1, pl.ds(pl.multiple_of(n.p * rows + r.start, 16), r.size), :]
+                self.total[r, :] = value.astype(f32)
+
+            by_rows(rows, 16, begin)
+            for z in range(4):
+
+                @pl.when(z != n.z)
                 def _():
-                    self.fetch(k, 0)
+                    self.remote(
+                        self.total_like, self.line.at[z], self.zs.at[0], self.zr.at[z], n.sib
+                    ).wait_recv()
+                    if stage is None:
+                        other = self.line.at[z]
+                    else:
+                        other = stage
+                        load = pltpu.make_async_copy(self.line.at[z], stage, self.ld)
+                        load.start()
+                        load.wait()
+
+                    def more(r):
+                        self.total[r, :] += other[r, :].astype(f32)
+
                     by_rows(rows, 16, more)
 
-                @pl.when(z < 3)
-                def _():
-                    self.fetch(k, 1)
-                    by_rows(rows, 16, more)
-
-                pltpu.make_async_copy(self.total, self.out, self.eo).start()
-                self.final().start()
+            pltpu.make_async_copy(self.total, self.out, self.eo).start()
+            self.final().start()
 
     def final(self):
         return self.remote(self.total, self.out, self.es, self.er, self.n.sib)
 
-    def finish(self, panels=True):
-        n = self.n
-        mine = n.z % 2 == n.c
-
-        @pl.when(mine)
-        def _():
-            pltpu.make_async_copy(self.total, self.out, self.eo).wait()
-            self.final().wait_send()
-
-        @pl.when(jnp.logical_not(mine))
-        def _():
-            self.final().wait_recv()
-
+    def drain(self, panels=True):
         for k in range(2):
             if panels:
                 self.panel(k).wait_send()
@@ -1166,16 +1126,28 @@
                 copy.wait_send()
             self.piece(k).wait_send()
 
-            @pl.when(self.target(k) != n.z)
+    def finish(self):
+        for k in range(2):
+
+            @pl.when(self.target(k) != self.n.z)
             def _():
-                self.step(k, True).wait_send()
+                self.along(k).wait_send()
+
+        @pl.when(self.mine())
+        def _():
+            pltpu.make_async_copy(self.total, self.out, self.eo).wait()
+            self.final().wait_send()
+
+        @pl.when(jnp.logical_not(self.mine()))
+        def _():
+            self.final().wait_recv()
 
 
 def scatter_sems():
     dma = pltpu.SemaphoreType.DMA
     return [
         dma((2,)), dma((2,)), dma((2, 2)), dma((2, 2)), dma((2,)), dma((2,)),
-        dma((2,)), dma((2, 2)), dma, dma, dma, dma,
+        dma((2,)), dma((4,)), dma, dma, dma, dma,
     ]
 
 
@@ -1212,15 +1184,15 @@
 
 def middle_kernel(s, *refs):
     (wa, wb, wc, cot_i, res_i, two_i, slope_i, hid_i, out_i, vec) = refs[:10]
-    (down_o, up_o, gres_o, branch_o, gatt_o, oz_o, sums, back_o, line_c, line_b) = refs[10:20]
-    (cot, res, two, gp, hid, cot_t, two_t, wt, acc, branch, oz) = refs[20:31]
-    (ship, own_c, came, first_c, second_c, own_b, first_b, second_b, total, stage) = refs[31:41]
-    sems = refs[41:]
+    (down_o, up_s, gres_o, gatt_o, oz_o, sums, back_o, line_c) = refs[10:18]
+    (cot, res, two, gp, hid, cot_t, two_t, wt, acc, branch, oz) = refs[18:29]
+    (ship, own_c, came, first_c, second_c, own_b, first_b, second_b, total, stage) = refs[29:39]
+    sems = refs[39:]
     net = Net()
-    C = Scatter(net, s, own_c, ship, came, first_c, second_c, line_c, total, down_o, stage, sems[:12])
-    B = Scatter(net, s, own_b, ship, came, first_b, second_b, line_b, total, up_o, stage, sems[12:24])
+    C = Scatter(net, s, own_c, ship, came, first_c, second_c, line_c, total, down_o, None, sems[:12])
+    B = Scatter(net, s, own_b, ship, came, first_b, second_b, None, None, None, None, sems[12:24])
     seq_out = FromSequences(net, out_i, back_o, sems[24:26])
-    load, tiles, save, credit = sems[26:30]
+    load, tiles, save, keep, credit = sems[26:31]
     loads = fetch_all(
         ((cot_i, cot), (hid_i, hid), (slope_i, gp), (two_i, two), (res_i, res)), load
     )
@@ -1323,7 +1295,7 @@
         if k == 0:
             C.turn(1)
     C.land(0)
-    C.along(0)
+    C.send(0)
     loads[4].wait()
 
     def norm(r):
@@ -1343,7 +1315,7 @@
     branch[...] = jnp.zeros_like(branch)
     by_rows(s.half, LANES, norm)
     C.land(1)
-    C.along(1)
+    C.send(1)
     B.turn(0)
 
     for z in range(4):
@@ -1366,31 +1338,33 @@
 
         by_columns(s.width, part)
     B.turn(1)
-    branch_low = two
-    branch_low[...] = branch[:, : s.width]
     lane = lax.broadcasted_iota(jnp.int32, (s.half, s.wide), 1)
     branch[...] = to_low(jnp.where(lane < s.width, acc[...], 0.0))
-    saves = fetch_all(((res, gres_o), (branch_low, branch_o), (branch, gatt_o), (oz, oz_o)), save)
-    B.land(0)
-    B.along(0)
-    C.finish(False)
-    B.land(1)
-    B.along(1)
-    B.finish()
-    for copy in saves:
+    saves = fetch_all(((res, gres_o), (branch, gatt_o), (oz, oz_o)), save)
+    C.collect(stage)
+    kept = []
+    for k in range(2):
+        B.land(k)
+        kept.append(pltpu.make_async_copy(B.block(k, net.p), up_s.at[k], keep.at[k]))
+        kept[k].start()
+    C.drain(False)
+    B.drain()
+    C.finish()
+    for copy in saves + kept:
         copy.wait()
     seq_out.wait()
     seq_out.drain()
 
 
 def last_kernel(s, *refs):
-    (wa, oz_i, dq_i, own_i, sib_i, normed_i, att_i, x_i, gres_i, vec, sums, tops) = refs[:12]
-    (qkv_o, gin_o, small_o, line_a) = refs[12:16]
-    (came_d, own_d, dq, wide, qz, oz, norm_t, att_t, normed, att, x, gres, wt, acc, gin, buf, got) = refs[16:33]
-    (ship, own_a, came_a, first_a, second_a, total, stage) = refs[33:40]
-    sems = refs[40:]
+    (wa, oz_i, dq_i, own_i, sib_i, normed_i, att_i, x_i, gres_i, up_s, vec, sums, tops) = refs[:13]
+    (qkv_o, up_o, gin_o, small_o) = refs[13:17]
+    (came_d, own_d, dq, wide, qz, oz, norm_t, att_t, normed, att, x, gres, wt, acc, gin, buf, got) = refs[17:34]
+    (ship, own_a, came_a, first_a, second_a, total, stage, line_a, line_b) = refs[34:43]
+    sems = refs[43:]
     net = Net()
-    A = Scatter(net, s, own_a, ship, came_a, first_a, second_a, line_a, total, qkv_o, stage, sems[:12])
+    A = Scatter(net, s, own_a, ship, came_a, first_a, second_a, line_a, total, qkv_o, None, sems[:12])
+    B = Scatter(net, s, None, None, None, None, None, line_b, total, up_o, up_s, sems[20:32])
     seq_in = FromSequences(net, gin, gin_o, sems[12:14])
     load, tiles, ds, dr, gs, gr = sems[14:20]
     loads = fetch_all(
@@ -1402,6 +1376,8 @@
         sib_i, came_d, ds, dr, device_id=net.sib, device_id_type=MESH
     )
     swap.start()
+    B.send(0)
+    B.send(1)
 
     def tile(j):
         return pltpu.make_async_copy(
@@ -1506,13 +1482,14 @@
 
     exchange(0, partners[0]).start()
     A.turn(0)
+    A.turn(1)
     merge(0)
     exchange(1, partners[1]).start()
-    A.turn(1)
+    B.collect(stage)
     merge(1)
     exchange(2, partners[2]).start()
     A.land(0)
-    A.along(0)
+    A.send(0)
     merge(2)
 
     def around(z):
@@ -1531,7 +1508,8 @@
             pltpu.make_async_copy(buf, got.at[3 + z], gr.at[3 + z]).start()
 
     A.land(1)
-    A.along(1)
+    A.send(1)
+    B.finish()
     for z in range(4):
         pltpu.make_async_copy(buf, got.at[3 + z], gr.at[3 + z]).wait()
 
@@ -1540,6 +1518,8 @@
             around(z).wait_send()
 
     small_o[...] = join(join(got[3], got[4]), join(got[5], got[6]))
+    A.collect()
+    A.drain()
     A.finish()
     seq_in.wait()
     seq_in.drain()
@@ -1563,15 +1543,15 @@
     low = lambda *dims: jax.ShapeDtypeStruct(dims, bf16)
     high = lambda *dims: jax.ShapeDtypeStruct(dims, f32)
     size = s.cols - s.out_tile
-    line = low(2, 2, s.rows, s.cols)
     return pl.pallas_call(
         partial(middle_kernel, s),
         out_shape=[
-            high(s.rows, s.cols), high(s.rows, s.cols), high(rows, s.wide), low(rows, s.width),
-            low(rows, s.wide), low(4, rows, size), high(16, s.wide), low(*shape), line, line,
+            high(s.rows, s.cols), low(2, s.rows, s.cols), high(rows, s.wide),
+            low(rows, s.wide), low(4, rows, size), high(16, s.wide), low(*shape),
+            low(4, s.rows, s.cols),
         ],
         in_specs=[anywhere] * 9 + [local],
-        out_specs=[anywhere] * 6 + [local] + [anywhere] * 3,
+        out_specs=[anywhere] * 5 + [local] + [anywhere] * 2,
         scratch_shapes=[
             pltpu.VMEM((rows, s.width), bf16),
             pltpu.VMEM((rows, s.wide), f32),
@@ -1587,7 +1567,7 @@
         ]
         + scatter_scratch(s, 2)
         + scatter_sems() * 2
-        + [dma((2,)), dma((2,)), dma((5,)), dma((2,)), dma((4,)), pltpu.SemaphoreType.REGULAR((2,))],
+        + [dma((2,)), dma((2,)), dma((5,)), dma((2,)), dma((3,)), dma((2,)), pltpu.SemaphoreType.REGULAR((2,))],
         compiler_params=pltpu.CompilerParams(
             collective_id=2, has_side_effects=True, vmem_limit_bytes=63 * 2**20
         ),
@@ -1595,7 +1575,7 @@
     )(wa, wb, wc, cot, res, two, slope, hid, out, vec)
 
 
-def last_call(s, shape, wa, oz, dq, d_own, d_sib, normed, att, x, gres, vec, sums, tops):
+def last_call(s, shape, wa, oz, dq, d_own, d_sib, normed, att, x, gres, up_sums, vec, sums, tops):
     dma = pltpu.SemaphoreType.DMA
     rows = s.half
     anywhere = pl.BlockSpec(memory_space=pl.ANY)
@@ -1606,10 +1586,10 @@
     return pl.pallas_call(
         partial(last_kernel, s),
         out_shape=[
-            high(s.rows, s.cols), low(*shape), high(16, s.wide), low(2, 2, s.rows, s.cols),
+            high(s.rows, s.cols), high(s.rows, s.cols), low(*shape), high(16, s.wide),
         ],
-        in_specs=[anywhere] * 9 + [local] * 3,
-        out_specs=[anywhere, anywhere, local, anywhere],
+        in_specs=[anywhere] * 10 + [local] * 3,
+        out_specs=[anywhere, anywhere, anywhere, local],
         scratch_shapes=[
             pltpu.VMEM((2, rows, s.wide), bf16),
             pltpu.VMEM((2, rows, s.wide), bf16),
@@ -1630,13 +1610,15 @@
             pltpu.VMEM((7, 16, s.wide), f32),
         ]
         + scatter_scratch(s, 1)
+        + [pltpu.VMEM((4, s.rows, s.cols), bf16)] * 2
         + scatter_sems()
-        + [dma((2,)), dma((2,)), dma((7,)), dma((2,)), dma, dma, dma((7,)), dma((7,))],
+        + [dma((2,)), dma((2,)), dma((7,)), dma((2,)), dma, dma, dma((7,)), dma((7,))]
+        + scatter_sems(),
         compiler_params=pltpu.CompilerParams(
             collective_id=3, has_side_effects=True, vmem_limit_bytes=63 * 2**20
         ),
         name="last",
-    )(wa, oz, dq, d_own, d_sib, normed, att, x, gres, vec, sums, tops)
+    )(wa, oz, dq, d_own, d_sib, normed, att, x, gres, up_sums, vec, sums, tops)
 
 
 def slot_info(moves, segment_ids, padding, stretch_order):
@@ -1724,14 +1706,14 @@
     (wa, wb, wc, x, cot, vec, normed, queries, kv, attended, residual, two, slope, hidden, lse, tops, out) = forward_call(
         s, own_a, own_b, own_c, small, inputs, cotangent, kinfo, qinfo
     )
-    down_block, up_block, gres, _, gatt, oz, sums, output, _, _ = middle_call(
+    down_block, up_sums, gres, gatt, oz, sums, output, _ = middle_call(
         s, inputs.shape, wa, wb, wc, cot, residual, two, slope, hidden, out, vec
     )
     dq, d_own, d_sib = attend_backward(heads, kinfo, qinfo, queries, kv, gatt, lse)
     block_top = jnp.max(tops, axis=2).reshape(1, -1)[:, :heads]
     block_top = jnp.pad(block_top, ((0, 7), (0, wide - heads)))
-    qkv_block, grad_input, small_sums, _ = last_call(
-        s, inputs.shape, wa, oz, dq, d_own, d_sib, normed, attended, x, gres, vec, sums, block_top
+    qkv_block, up_block, grad_input, small_sums = last_call(
+        s, inputs.shape, wa, oz, dq, d_own, d_sib, normed, attended, x, gres, up_sums, vec, sums, block_top
     )
     rows_d = w_qkv.shape[0]
     cols_q, cols_d, cols_f = w_qkv.shape[1], w_out.shape[1], w_up.shape[1]

time: 561 us -> 495 us (0.88)
  Pallas kernels: 521 us -> 455 us
    pallas_call x1, Pallas kernels: 212 us -> 178 us  [forward_call(): pl.pallas_call(partial(forward_kernel, s), out_shape=out_shape, in_specs=...]
    pallas_call x1, Pallas kernels: 158 us -> 132 us  [middle_call(): pl.pallas_call(partial(middle_kernel, s), out_shape=[high(s.rows, s.cols)...]
    pallas_call x1, Pallas kernels: 117 us -> 110 us  [last_call(): pl.pallas_call(partial(last_kernel, s), out_shape=[high(s.rows, s.cols),...]
where the time goes in v4:
time: 495 us; the launch traced here: 489 us
  Pallas kernels  455 us (92%)
  local copies, waits for them, and re-layouts  19.5 us (4%)
  other arithmetic  12.9 us (3%)
    pallas_call x1, Pallas kernels, forward_call(): pl.pallas_call(partial(forward_kernel, s), out_shape=out_shape, in_specs=...  178 us
    pallas_call x1, Pallas kernels, middle_call(): pl.pallas_call(partial(middle_kernel, s), out_shape=[high(s.rows, s.cols)...  132 us
    pallas_call x1, Pallas kernels, last_call(): pl.pallas_call(partial(last_kernel, s), out_shape=[high(s.rows, s.cols),...  110 us
    pallas_call x1, Pallas kernels, attend_backward(): pl.pallas_call(partial(attend_backward_kernel, heads), grid=(pairs,), in_...  34.2 us
    unnamed x45, local copies, waits for them, and re-layouts  11.7 us
  transfers between devices with their start and end apart: 2, of which 0 were waited for; matrix products, arithmetic and copies ran while one was open for 1% of the time, Pallas kernels for 0%

profile of v4, /device:TPU:0, one launch (start us, length us, event | category | flops | bytes accessed | tf_op | source)
XLA Modules:
  0.0 489.2 jit_solution(6939642052376788002)
XLA Ops:
  0.6 0.0 copy-start.9
  0.7 1.1 fusion.29
  1.7 1.1 fusion.15
  2.9 0.0 copy-start.15
  2.9 0.0 copy-start.16
  2.9 0.0 copy-start.19
  2.9 0.0 copy-start.18
  2.9 0.0 copy-start.17
  3.0 0.0 copy-start.11
  3.0 0.0 copy-done.9
  3.0 1.0 fusion.7
  4.0 0.5 collective-permute-start
  4.4 0.0 copy-done.15
  4.4 0.0 copy-done.16
  4.4 0.1 collective-permute-start.1
  4.6 0.0 copy-done.19
  4.6 0.1 add.83
  4.7 0.1 broadcast_bitcast_fusion
  4.8 0.0 copy-done.17
  4.9 1.4 copy.40.refs_4_
  6.3 1.4 copy.41.refs_5_
  7.7 0.6 pad.36.refs_3_
  8.3 0.0 collective-permute-done.1
  8.4 0.6 gather_fusion
  8.9 0.1 select_bitcast_fusion.1
  9.1 0.0 copy-start.2
  9.2 1.0 copy.42.refs_6_.kinfo_ref
  10.2 0.0 collective-permute-done
  10.2 1.6 broadcast_select_fusion.1
  11.8 0.1 fusion.25
  11.9 0.1 fusion.27
  11.9 0.1 fusion.26
  12.1 0.1 fusion.28
  12.1 0.9 pad_maximum_fusion.1.refs_1_
  13.0 0.9 pad_maximum_fusion.refs_0_
  13.9 1.0 fusion.9.refs_2_
  14.9 177.9 %forward.1 = (bf16[1088,4608]{1,0:T(8,128)(2,1)}, bf16[1088,4608]{1,0:T(8,128)(2,1)}, bf16[1088,4608]{1,0:T(8,128)(2,1)}, bf16[512,1088]{1,0:T(8,128)(2,1)}, bf1...) custom-call(bf16[272,1152]{1,0:T(8,128)(2,1)} %pad_maximum_fusion.re, ...), custom_call_target="tpu_custom_call" | custom-call | tf_op jit(solution)/shard_map/forward/pallas_call | solution.py:949
  192.8 0.9 reduce_max.9
  193.7 0.1 reshape.56
  193.8 0.6 pad.37.refs_12_
  194.4 132.4 %middle.1 = (f32[272,1152]{1,0:T(8,128)}, bf16[2,272,1152]{2,1,0:T(8,128)(2,1)}, f32[512,1152]{1,0:T(8,128)}, bf16[512,1152]{1,0:T(8,128)(2,1)}, bf16[4,512,384]...) custom-call(bf16[1088,4608]{1,0:T(8,128)(2,1)} %get-tuple-element.42.refs_0_,, ...), custom_call_target="tpu_custom_call" | custom-call | tf_op jit(solution)/shard_map/middle/pallas_call | solution.py:1546
  326.9 1.3 copy-done.4
  328.1 1.3 copy-done.5
  329.4 34.2 %attend_backward.1 = (bf16[512,1152]{1,0:T(8,128)(2,1)S(1)}, bf16[2,512,1152]{2,1,0:T(8,128)(2,1)}, bf16[2,512,1152]{2,1,0:T(8,128)(2,1)}) custom-call(s32[1024,2]{1,0:T(8,128)S(1)} %copy-done, s32[1,512]{1,0:T(1,128)S(1)} %copy-done.3, bf16[512,1152]{1,0:T(8,128)(2,1)S(1)} %copy-done.4, bf16[2,1024,1152]{2,1,0:T(8,128)(2,1)} %get-tuple-element.55.own_ref.sib_ref, ...), custom_call_target="tpu_custom_call" | custom-call | flops 12079595520 | bytes 12976128 | tf_op jit(solution)/shard_map/attend_backward/pallas_call | solution.py:336
  363.6 1.0 copy-done.1
  364.6 110.3 %last.1 = (f32[272,1152]{1,0:T(8,128)}, f32[272,1152]{1,0:T(8,128)}, bf16[2,256,1088]{2,1,0:T(8,128)(2,1)}, f32[16,1152]{1,0:T(8,128)}) custom-call(bf16[1088,4608]{1,0:T(8,128)(2,1)} %get-tuple-element.42.refs_0_, bf16[4,512,384]{2,1,0:T(8,128)(2,1)} %get-tuple-element.53.refs_1_, bf16[512,1152]{1,0:T(8,128)(2,1)} %copy-done.1, ...), custom_call_target="tpu_custom_call" | custom-call | tf_op jit(solution)/shard_map/last/pallas_call | solution.py:1586
  474.9 1.4 slice_select_fusion.1
  476.4 0.8 slice.126
  477.2 0.8 slice.127
  478.0 0.5 divide_sqrt_fusion
  478.5 0.1 fusion.24
  478.6 1.2 copy-done.10
  479.8 1.7 copy.45
  481.5 0.1 broadcast_in_dim.29
  481.5 0.1 reshape.57
  481.6 0.1 concatenate.47
  481.7 0.1 dynamic_slice.37
  481.8 0.7 multiply_convert_fusion
  482.5 0.7 constant_dynamic-slice_fusion
  483.2 0.6 multiply_convert_fusion.1
  483.8 2.3 copy.44
  486.2 1.1 select_bitcast_fusion
  487.3 0.9 slice_select_fusion
  488.2 0.6 dynamic-slice_reduce_fusion
  (44 shorter events, 0.2 us)
Async XLA Ops:
  0.6 2.3 copy-start.9
  2.9 1.5 copy-start.15
  2.9 1.5 copy-start.16
  2.9 1.6 copy-start.19
  2.9 1.8 copy-start.18
  2.9 1.8 copy-start.17
  3.0 1.9 copy-start.11
  4.0 2.3 copy-start.12
  4.0 6.2 %collective-permute-start = (bf16[408,1152]{1,0:T(8,128)(2,1)}, bf16[408,1152]{1,0:T(8,128)(2,1)}, u32[]{:S(2)}, u32[]{:S(2)}) collective-permute-start(bf16[408,1152]{1,0:T(8,128)(2,1)} %fusion.7), channel_id=1, source_target_pairs={{0,4},{1,5},{2,6},{3,7},{4,0},{5,1},{6,2},{7,3},{8,12},{9,13},{10,... | collective-permute-start | bytes 2820104 | tf_op jit(solution)/shard_map/ppermute | solution.py:66
  4.4 3.9 collective-permute-start.1
  9.1 2.7 copy-start.2
  194.4 132.5 %copy-start = (s32[1024,2]{1,0:T(8,128)S(1)}, s32[1024,2]{1,0:T(8,128)}, u32[]{:S(2)}) copy-start(s32[1024,2]{1,0:T(8,128)} %copy.42.refs_6_.kinfo_ref) | copy-start | bytes 24580
  194.4 132.5 %copy-start.3 = (s32[1,512]{1,0:T(1,128)S(1)}, s32[1,512]{1,0:T(1,128)}, u32[]{:S(2)}) copy-start(s32[1,512]{1,0:T(1,128)} %copy-done.2) | copy-start | bytes 6148
  194.4 132.5 %copy-start.6 = (f32[9,2,512]{2,1,0:T(2,128)S(1)}, f32[9,2,512]{2,1,0:T(2,128)}, u32[]{:S(2)}) copy-start(f32[9,2,512]{2,1,0:T(2,128)} %get-tuple-element.57.lse_ref) | copy-start | bytes 110596
  326.9 1.3 copy-start.4
  328.1 1.3 copy-start.5
  363.6 1.0 copy-start.1
  474.9 3.1 copy-start.14
  474.9 3.6 copy-start.8
  478.5 1.3 copy-start.10
  479.8 2.0 copy-start.13
  482.5 3.6 copy-start.7

commit v5 on v4

--- a/solution.py
+++ b/solution.py
@@ -643,7 +643,7 @@
     lax.fori_loop(0, total // step, one, 0)
 
 
-def by_columns(total, body, step=256):
+def by_columns(total, body, step=640):
     def one(i, carry):
         body(pl.multiple_of(i * step, LANES), step)
         return carry
@@ -1074,19 +1074,19 @@
     def mine(self):
         return self.n.z % 2 == self.n.c
 
-    def collect(self, stage=None):
+    def collect(self, stage=None, held=None):
         n, rows = self.n, self.s.rows
 
         @pl.when(self.mine())
         def _():
             if self.own is None:
-                load = pltpu.make_async_copy(self.sums.at[1], stage, self.ld)
+                load = pltpu.make_async_copy(self.sums.at[1], held, self.ld)
                 load.start()
                 load.wait()
 
             def begin(r):
                 if self.own is None:
-                    value = stage[r, :]
+                    value = held[r, :]
                 else:
                     value = self.own[1, pl.ds(pl.multiple_of(n.p * rows + r.start, 16), r.size), :]
                 self.total[r, :] = value.astype(f32)
@@ -1184,13 +1184,13 @@
 
 def middle_kernel(s, *refs):
     (wa, wb, wc, cot_i, res_i, two_i, slope_i, hid_i, out_i, vec) = refs[:10]
-    (down_o, up_s, gres_o, gatt_o, oz_o, sums, back_o, line_c) = refs[10:18]
-    (cot, res, two, gp, hid, cot_t, two_t, wt, acc, branch, oz) = refs[18:29]
-    (ship, own_c, came, first_c, second_c, own_b, first_b, second_b, total, stage) = refs[29:39]
-    sems = refs[39:]
+    (down_s, up_own, gres_o, gatt_o, oz_o, sums, back_o) = refs[10:17]
+    (cot, res, two, gp, hid, cot_t, two_t, wt, acc, branch, oz) = refs[17:28]
+    (ship, own_c, came, first_c, second_c, own_b) = refs[28:34]
+    sems = refs[34:]
     net = Net()
-    C = Scatter(net, s, own_c, ship, came, first_c, second_c, line_c, total, down_o, None, sems[:12])
-    B = Scatter(net, s, own_b, ship, came, first_b, second_b, None, None, None, None, sems[12:24])
+    C = Scatter(net, s, own_c, ship, came, first_c, second_c, None, None, None, None, sems[:12])
+    B = Scatter(net, s, own_b, ship, came, None, None, None, None, None, None, sems[12:24])
     seq_out = FromSequences(net, out_i, back_o, sems[24:26])
     load, tiles, save, keep, credit = sems[26:31]
     loads = fetch_all(
@@ -1291,11 +1291,10 @@
     for k in range(2):
         B.wait_panel(k)
         up_panel(B.target(k), own_b, k, came)
-        B.start(k)
         if k == 0:
             C.turn(1)
-    C.land(0)
-    C.send(0)
+    own_copy = pltpu.make_async_copy(own_b, up_own, save.at[3])
+    own_copy.start()
     loads[4].wait()
 
     def norm(r):
@@ -1314,9 +1313,11 @@
 
     branch[...] = jnp.zeros_like(branch)
     by_rows(s.half, LANES, norm)
-    C.land(1)
-    C.send(1)
-    B.turn(0)
+    kept = []
+    for k in range(2):
+        C.land(k)
+        kept.append(pltpu.make_async_copy(C.block(k, net.p), down_s.at[k], keep.at[k]))
+        kept[k].start()
 
     for z in range(4):
         if z < 3:
@@ -1337,45 +1338,157 @@
             acc[:, pl.ds(start, count)] = value
 
         by_columns(s.width, part)
-    B.turn(1)
     lane = lax.broadcasted_iota(jnp.int32, (s.half, s.wide), 1)
     branch[...] = to_low(jnp.where(lane < s.width, acc[...], 0.0))
     saves = fetch_all(((res, gres_o), (branch, gatt_o), (oz, oz_o)), save)
-    C.collect(stage)
-    kept = []
+    C.drain(False)
     for k in range(2):
-        B.land(k)
-        kept.append(pltpu.make_async_copy(B.block(k, net.p), up_s.at[k], keep.at[k]))
-        kept[k].start()
-    C.drain(False)
-    B.drain()
-    C.finish()
-    for copy in saves + kept:
+        B.panel(k).wait_send()
+    for copy in saves + kept + [own_copy]:
         copy.wait()
     seq_out.wait()
     seq_out.drain()
 
 
+def back_pair(s, i, q_ref, kv_ref, grad_ref, lse_ref, bias_ref, dq_ref, dkv_ref):
+    lanes = pl.ds(pl.multiple_of(i * LANES, LANES), LANES)
+    keys, values = kv_ref[0, :, lanes], kv_ref[1, :, lanes]
+    queries, grads = q_ref[:, lanes], grad_ref[:, lanes]
+    lane = lax.broadcasted_iota(jnp.int32, queries.shape, 1)
+    dqs, dk, dv = [], 0.0, 0.0
+    for side in range(2):
+        mine = (lane >= HD) if side else (lane < HD)
+        picked = jnp.where(mine, queries, jnp.zeros_like(queries)) * bf16(HD**-0.5)
+        grad = jnp.where(mine, grads, jnp.zeros_like(grads))
+        scores = nt(keys, picked) + bias_ref[...]
+        weights = jnp.exp(scores - lse_ref[i, side : side + 1, :])
+        dp = nt(values, grad)
+        delta = jnp.sum(weights * dp, axis=0, keepdims=True)
+        ds = (weights * (dp - delta)).astype(bf16)
+        dqs.append(tn(keys[:, side * HD : (side + 1) * HD], ds) * (HD**-0.5))
+        dk = dk + product(ds, picked)
+        dv = dv + product(weights.astype(bf16), grad)
+    dq_ref[:, lanes] = jnp.concatenate(dqs, axis=0).T.astype(bf16)
+    dkv_ref[0, :, lanes] = dk.astype(bf16)
+    dkv_ref[1, :, lanes] = dv.astype(bf16)
+
+
+def attention_kernel(s, *refs):
+    (kinfo, qinfo, lse, q_i, kv_i, grad_i, own_i, down_s) = refs[:8]
+    (dq_o, dkv_o, up_s, down_o) = refs[8:12]
+    (q, kv, grad, dq, dkv, came, bias, own_b, first_b, second_b, line, total, stage) = refs[12:25]
+    sems = refs[25:]
+    net = Net()
+    B = Scatter(net, s, own_b, None, None, first_b, second_b, None, None, None, None, sems[:12])
+    C = Scatter(net, s, None, None, None, None, None, line, total, down_o, down_s, sems[12:24])
+    load, save, ds, dr = sems[24:28]
+    loads = fetch_all(((own_i, own_b), (q_i, q), (kv_i, kv), (grad_i, grad)), load)
+    enter(net)
+    loads[0].wait()
+    B.start(0)
+    B.start(1)
+    C.send(0)
+    C.send(1)
+    fill_bias(kinfo, qinfo, bias)
+    for copy in loads[1:]:
+        copy.wait()
+
+    def pair(i, carry):
+        back_pair(s, i, q, kv, grad, lse, bias, dq, dkv)
+
+        @pl.when(i == 6)
+        def _():
+            B.turn(0)
+
+        @pl.when(i == 7)
+        def _():
+            B.turn(1)
+
+        return carry
+
+    lax.fori_loop(0, s.pairs, pair, 0)
+    rows = pl.ds(0, s.half)
+    swap = pltpu.make_async_remote_copy(
+        dkv.at[:, pl.ds(s.half, s.half)], came, ds, dr, device_id=net.sib, device_id_type=MESH
+    )
+    swap.start()
+    saves = [pltpu.make_async_copy(dq, dq_o, save.at[0])]
+    saves[0].start()
+    C.collect(held=stage)
+    swap.wait()
+
+    def join(r):
+        for kind in range(2):
+            dkv[kind, r, :] = to_low(dkv[kind, r, :].astype(f32) + came[kind, r, :].astype(f32))
+
+    by_rows(s.half, LANES, join)
+    saves.append(pltpu.make_async_copy(dkv.at[:, rows], dkv_o, save.at[1]))
+    saves[1].start()
+    for k in range(2):
+        B.land(k)
+        saves.append(pltpu.make_async_copy(B.block(k, net.p), up_s.at[k], save.at[2 + k]))
+        saves[2 + k].start()
+    B.drain(False)
+    C.finish()
+    for copy in saves:
+        copy.wait()
+
+
+def attention_call(s, kinfo, qinfo, lse, q, kv, grad, own, down_s):
+    dma = pltpu.SemaphoreType.DMA
+    rows = s.half
+    anywhere = pl.BlockSpec(memory_space=pl.ANY)
+    local = pl.BlockSpec(memory_space=pltpu.VMEM)
+    low = lambda *dims: jax.ShapeDtypeStruct(dims, bf16)
+    block = pltpu.VMEM((s.rows, s.cols), bf16)
+    return pl.pallas_call(
+        partial(attention_kernel, s),
+        out_shape=[
+            low(rows, s.wide), low(2, rows, s.wide), low(2, s.rows, s.cols),
+            jax.ShapeDtypeStruct((s.rows, s.cols), f32),
+        ],
+        in_specs=[local] * 3 + [anywhere] * 5,
+        out_specs=[anywhere] * 4,
+        scratch_shapes=[
+            pltpu.VMEM((rows, s.wide), bf16),
+            pltpu.VMEM((2, 2 * rows, s.wide), bf16),
+            pltpu.VMEM((rows, s.wide), bf16),
+            pltpu.VMEM((rows, s.wide), bf16),
+            pltpu.VMEM((2, 2 * rows, s.wide), bf16),
+            pltpu.VMEM((2, rows, s.wide), bf16),
+            pltpu.VMEM((2 * rows, rows), f32),
+            pltpu.VMEM((2, s.width, s.cols), bf16),
+            pltpu.VMEM((2, 2, s.rows, s.cols), bf16),
+            pltpu.VMEM((2, s.rows, s.cols), bf16),
+            pltpu.VMEM((4, s.rows, s.cols), bf16),
+            pltpu.VMEM((s.rows, s.cols), f32),
+            block,
+        ]
+        + scatter_sems() * 2
+        + [dma((4,)), dma((4,)), dma, dma],
+        compiler_params=pltpu.CompilerParams(
+            collective_id=4, has_side_effects=True, vmem_limit_bytes=60 * 2**20
+        ),
+        name="attention",
+    )(kinfo, qinfo, lse, q, kv, grad, own, down_s)
+
+
 def last_kernel(s, *refs):
-    (wa, oz_i, dq_i, own_i, sib_i, normed_i, att_i, x_i, gres_i, up_s, vec, sums, tops) = refs[:13]
-    (qkv_o, up_o, gin_o, small_o) = refs[13:17]
-    (came_d, own_d, dq, wide, qz, oz, norm_t, att_t, normed, att, x, gres, wt, acc, gin, buf, got) = refs[17:34]
-    (ship, own_a, came_a, first_a, second_a, total, stage, line_a, line_b) = refs[34:43]
-    sems = refs[43:]
+    (wa, oz_i, dq_i, own_i, normed_i, att_i, x_i, gres_i, up_s, vec, sums, tops) = refs[:12]
+    (qkv_o, up_o, gin_o, small_o) = refs[12:16]
+    (own_d, dq, wide, qz, oz, norm_t, att_t, normed, att, x, gres, wt, acc, gin, buf, got) = refs[16:32]
+    (ship, own_a, came_a, first_a, second_a, total, stage, line_a, line_b) = refs[32:41]
+    sems = refs[41:]
     net = Net()
     A = Scatter(net, s, own_a, ship, came_a, first_a, second_a, line_a, total, qkv_o, None, sems[:12])
-    B = Scatter(net, s, None, None, None, None, None, line_b, total, up_o, up_s, sems[20:32])
+    B = Scatter(net, s, None, None, None, None, None, line_b, total, up_o, up_s, sems[18:30])
     seq_in = FromSequences(net, gin, gin_o, sems[12:14])
-    load, tiles, ds, dr, gs, gr = sems[14:20]
+    load, tiles, gs, gr = sems[14:18]
     loads = fetch_all(
         ((dq_i, dq), (own_i, own_d), (normed_i, normed), (att_i, att), (oz_i, oz), (x_i, x), (gres_i, gres)),
         load,
     )
     enter(net)
-    swap = pltpu.make_async_remote_copy(
-        sib_i, came_d, ds, dr, device_id=net.sib, device_id_type=MESH
-    )
-    swap.start()
     B.send(0)
     B.send(1)
 
@@ -1393,11 +1506,8 @@
     loads[1].wait()
     buf[...] = sums[...]
     wide[:, : s.wide] = dq[...].astype(f32)
-    swap.wait()
     for kind in range(2):
-        lanes = slice((kind + 1) * s.wide, (kind + 2) * s.wide)
-        value = to_low(own_d[kind].astype(f32) + came_d[kind].astype(f32)).astype(f32)
-        wide[:, lanes] = value
+        wide[:, (kind + 1) * s.wide : (kind + 2) * s.wide] = own_d[kind].astype(f32)
     buf[2:3, :] = jnp.sum(wide[:, : s.wide], axis=0, keepdims=True)
     buf[3:4, :] = jnp.sum(wide[:, 2 * s.wide :], axis=0, keepdims=True)
     for z in range(4):
@@ -1436,11 +1546,10 @@
     for k in range(2):
         panel(A.sibling_target(k), ship, k)
         A.ship(k)
-    for z in range(2):
-        tile(z + 1).start()
-        tile(z).wait()
-        through(s, acc, qz, wt, z)
     for k in range(2):
+        tile(k + 1).start()
+        tile(k).wait()
+        through(s, acc, qz, wt, k)
         A.wait_panel(k)
         panel(A.target(k), own_a, k, came_a)
         A.start(k)
@@ -1485,7 +1594,7 @@
     A.turn(1)
     merge(0)
     exchange(1, partners[1]).start()
-    B.collect(stage)
+    B.collect(held=stage)
     merge(1)
     exchange(2, partners[2]).start()
     A.land(0)
@@ -1546,12 +1655,11 @@
     return pl.pallas_call(
         partial(middle_kernel, s),
         out_shape=[
-            high(s.rows, s.cols), low(2, s.rows, s.cols), high(rows, s.wide),
+            low(2, s.rows, s.cols), low(2, s.width, s.cols), high(rows, s.wide),
             low(rows, s.wide), low(4, rows, size), high(16, s.wide), low(*shape),
-            low(4, s.rows, s.cols),
         ],
         in_specs=[anywhere] * 9 + [local],
-        out_specs=[anywhere] * 5 + [local] + [anywhere] * 2,
+        out_specs=[anywhere] * 5 + [local, anywhere],
         scratch_shapes=[
             pltpu.VMEM((rows, s.width), bf16),
             pltpu.VMEM((rows, s.wide), f32),
@@ -1565,9 +1673,10 @@
             pltpu.VMEM((rows, s.wide), bf16),
             pltpu.VMEM((4, rows, size), bf16),
         ]
-        + scatter_scratch(s, 2)
+        + scatter_scratch(s, 1)[:-2]
+        + [pltpu.VMEM((2, s.width, s.cols), bf16)]
         + scatter_sems() * 2
-        + [dma((2,)), dma((2,)), dma((5,)), dma((2,)), dma((3,)), dma((2,)), pltpu.SemaphoreType.REGULAR((2,))],
+        + [dma((2,)), dma((2,)), dma((5,)), dma((2,)), dma((4,)), dma((2,)), pltpu.SemaphoreType.REGULAR((2,))],
         compiler_params=pltpu.CompilerParams(
             collective_id=2, has_side_effects=True, vmem_limit_bytes=63 * 2**20
         ),
@@ -1575,7 +1684,7 @@
     )(wa, wb, wc, cot, res, two, slope, hid, out, vec)
 
 
-def last_call(s, shape, wa, oz, dq, d_own, d_sib, normed, att, x, gres, up_sums, vec, sums, tops):
+def last_call(s, shape, wa, oz, dq, d_own, normed, att, x, gres, up_sums, vec, sums, tops):
     dma = pltpu.SemaphoreType.DMA
     rows = s.half
     anywhere = pl.BlockSpec(memory_space=pl.ANY)
@@ -1588,10 +1697,9 @@
         out_shape=[
             high(s.rows, s.cols), high(s.rows, s.cols), low(*shape), high(16, s.wide),
         ],
-        in_specs=[anywhere] * 10 + [local] * 3,
+        in_specs=[anywhere] * 9 + [local] * 3,
         out_specs=[anywhere, anywhere, anywhere, local],
         scratch_shapes=[
-            pltpu.VMEM((2, rows, s.wide), bf16),
             pltpu.VMEM((2, rows, s.wide), bf16),
             pltpu.VMEM((rows, s.wide), bf16),
             pltpu.VMEM((rows, 3 * s.wide), f32),
@@ -1612,13 +1720,13 @@
         + scatter_scratch(s, 1)
         + [pltpu.VMEM((4, s.rows, s.cols), bf16)] * 2
         + scatter_sems()
-        + [dma((2,)), dma((2,)), dma((7,)), dma((2,)), dma, dma, dma((7,)), dma((7,))]
+        + [dma((2,)), dma((2,)), dma((7,)), dma((2,)), dma((7,)), dma((7,))]
         + scatter_sems(),
         compiler_params=pltpu.CompilerParams(
             collective_id=3, has_side_effects=True, vmem_limit_bytes=63 * 2**20
         ),
         name="last",
-    )(wa, oz, dq, d_own, d_sib, normed, att, x, gres, up_sums, vec, sums, tops)
+    )(wa, oz, dq, d_own, normed, att, x, gres, up_sums, vec, sums, tops)
 
 
 def slot_info(moves, segment_ids, padding, stretch_order):
@@ -1706,14 +1814,16 @@
     (wa, wb, wc, x, cot, vec, normed, queries, kv, attended, residual, two, slope, hidden, lse, tops, out) = forward_call(
         s, own_a, own_b, own_c, small, inputs, cotangent, kinfo, qinfo
     )
-    down_block, up_sums, gres, gatt, oz, sums, output, _ = middle_call(
+    down_sums, up_own, gres, gatt, oz, sums, output = middle_call(
         s, inputs.shape, wa, wb, wc, cot, residual, two, slope, hidden, out, vec
     )
-    dq, d_own, d_sib = attend_backward(heads, kinfo, qinfo, queries, kv, gatt, lse)
+    dq, d_own, up_sums, down_block = attention_call(
+        s, kinfo, qinfo, lse, queries, kv, gatt, up_own, down_sums
+    )
     block_top = jnp.max(tops, axis=2).reshape(1, -1)[:, :heads]
     block_top = jnp.pad(block_top, ((0, 7), (0, wide - heads)))
     qkv_block, up_block, grad_input, small_sums = last_call(
-        s, inputs.shape, wa, oz, dq, d_own, d_sib, normed, attended, x, gres, up_sums, vec, sums, block_top
+        s, inputs.shape, wa, oz, dq, d_own, normed, attended, x, gres, up_sums, vec, sums, block_top
     )
     rows_d = w_qkv.shape[0]
     cols_q, cols_d, cols_f = w_qkv.shape[1], w_out.shape[1], w_up.shape[1]

time: 495 us -> 450 us (0.909); the launches traced: 489 us -> 450 us
  Pallas kernels: 455 us -> 420 us
    pallas_call x2, Pallas kernels: 167 us -> 130 us  [the longest x1 75.4 us: middle_call(): pl.pallas_call(partial(middle_kernel, s), out_shape=[low(2, s.rows, s.col...]
    pallas_call x1, Pallas kernels: 178 us -> 185 us  [forward_call(): pl.pallas_call(partial(forward_kernel, s), out_shape=out_shape, in_specs=...]
    pallas_call x1, Pallas kernels: 110 us -> 104 us  [last_call(): pl.pallas_call(partial(last_kernel, s), out_shape=[high(s.rows, s.cols),...]
    unnamed x45 -> x31, local copies, waits for them, and re-layouts: 11.7 us -> 8.05 us
where the time goes in v5:
time: 450 us
  Pallas kernels  420 us (93%)
  local copies, waits for them, and re-layouts  15.8 us (4%)
  other arithmetic  12.9 us (3%)
    pallas_call x1, Pallas kernels, forward_call(): pl.pallas_call(partial(forward_kernel, s), out_shape=out_shape, in_specs=...  185 us
    pallas_call x1, Pallas kernels, last_call(): pl.pallas_call(partial(last_kernel, s), out_shape=[high(s.rows, s.cols),...  104 us
    pallas_call x1, Pallas kernels, middle_call(): pl.pallas_call(partial(middle_kernel, s), out_shape=[low(2, s.rows, s.col...  75.4 us
    pallas_call x1, Pallas kernels, attention_call(): pl.pallas_call(partial(attention_kernel, s), out_shape=[low(rows, s.wide)...  55.1 us
  transfers between devices with their start and end apart: 2, of which 0 were waited for; matrix products, arithmetic and copies ran while one was open for 1% of the time, Pallas kernels for 0%

profile of v5, /device:TPU:0, one launch (start us, length us, event | category | flops | bytes accessed | tf_op | source)
XLA Modules:
  0.0 450.1 jit_solution(17484537239217207773)
XLA Ops:
  0.6 0.0 copy-start.2
  0.7 1.1 fusion.29
  1.7 1.1 fusion.15
  2.9 0.0 copy-start.8
  2.9 0.0 copy-start.9
  2.9 0.0 copy-start.12
  2.9 0.0 copy-start.11
  2.9 0.0 copy-start.10
  3.0 0.0 copy-start.3
  3.0 0.0 copy-done.2
  3.0 1.0 fusion.7
  4.0 0.5 collective-permute-start
  4.4 0.0 copy-done.8
  4.4 0.0 copy-done.9
  4.4 0.1 collective-permute-start.1
  4.6 0.0 copy-done.12
  4.6 0.1 add.83
  4.7 0.1 broadcast_bitcast_fusion
  4.7 0.0 copy-done.11
  4.8 0.0 copy-done.10
  4.9 1.4 copy.40.refs_4_
  6.3 1.4 copy.41.refs_5_
  7.7 0.6 pad.36.refs_3_
  8.3 0.0 collective-permute-done.1
  8.4 0.6 gather_fusion
  8.9 0.1 select_bitcast_fusion.1
  9.1 0.0 copy-start.7
  9.2 1.1 copy.42.refs_6_.refs_0_
  10.2 0.0 collective-permute-done
  10.2 1.6 broadcast_select_fusion.1
  11.8 0.1 fusion.25
  11.9 0.1 fusion.27
  12.0 0.1 fusion.26
  12.1 0.1 fusion.28
  12.1 0.9 pad_maximum_fusion.1.refs_1_
  13.0 0.9 pad_maximum_fusion.refs_0_
  13.9 1.0 fusion.9.refs_2_
  14.9 185.2 %forward.1 = (bf16[1088,4608]{1,0:T(8,128)(2,1)}, bf16[1088,4608]{1,0:T(8,128)(2,1)}, bf16[1088,4608]{1,0:T(8,128)(2,1)}, bf16[512,1088]{1,0:T(8,128)(2,1)}, bf1...) custom-call(bf16[272,1152]{1,0:T(8,128)(2,1)} %pad_maximum_fusion.re, ...), custom_call_target="tpu_custom_call" | custom-call | tf_op jit(solution)/shard_map/forward/pallas_call | solution.py:949
  200.1 0.9 reduce_max.9
  201.0 0.1 reshape.56
  201.0 0.6 pad.37.refs_11_
  201.7 75.4 %middle.1 = (bf16[2,272,1152]{2,1,0:T(8,128)(2,1)}, bf16[2,1088,1152]{2,1,0:T(8,128)(2,1)}, f32[512,1152]{1,0:T(8,128)}, bf16[512,1152]{1,0:T(8,128)(2,1)}, bf16...) custom-call(bf16[1088,4608]{1,0:T(8,128)(2,1)} %get-tuple-element.43.refs_0_, ...), custom_call_target="tpu_custom_call" | custom-call | tf_op jit(solution)/shard_map/middle/pallas_call | solution.py:1655
  277.1 55.1 %attention.1 = (bf16[512,1152]{1,0:T(8,128)(2,1)}, bf16[2,512,1152]{2,1,0:T(8,128)(2,1)}, bf16[2,272,1152]{2,1,0:T(8,128)(2,1)}, f32[272,1152]{1,0:T(8,128)}) custom-call(s32[1024,2]{1,0:T(8,128)} %copy.42.refs_6_.refs_0_, s32[1,512]{1,0:T(1,128)} %copy-done.7, f32[9,2,512]{2,1,0:T(2,128)} %get-tuple-element.55.refs_2_, ...), custom_call_target="tpu_custom_call" | custom-call | tf_op jit(solution)/shard_map/attention/pallas_call | solution.py:1444
  332.1 103.9 %last.1 = (f32[272,1152]{1,0:T(8,128)}, f32[272,1152]{1,0:T(8,128)}, bf16[2,256,1088]{2,1,0:T(8,128)(2,1)}, f32[16,1152]{1,0:T(8,128)}) custom-call(bf16[1088,4608]{1,0:T(8,128)(2,1)} %get-tuple-element.43.refs_0_, bf16[4,512,384]{2,1,0:T(8,128)(2,1)} %get-tuple-element.54.refs_1_, bf16[512,1152]{1,0:T(8,128)(2,1)} %get-tuple-element.61.refs_2_, ...), custom_call_target="tpu_custom_call" | custom-call | tf_op jit(solution)/shard_map/last/pallas_call | solution.py:1695
  436.1 1.4 slice_select_fusion.1
  437.5 0.8 slice.126
  438.4 0.8 slice.127
  439.2 0.5 divide_sqrt_fusion
  439.7 0.1 fusion.24
  439.8 0.0 copy-start.5
  439.8 2.8 copy.45
  442.6 0.1 broadcast_in_dim.29
  442.6 0.1 reshape.57
  442.7 0.1 concatenate.47
  442.8 0.1 dynamic_slice.37
  442.9 0.0 copy-done.5
  442.9 0.7 multiply_convert_fusion
  443.6 0.7 constant_dynamic-slice_fusion
  444.3 0.6 multiply_convert_fusion.1
  444.9 0.0 copy-done
  444.9 1.1 select_bitcast_fusion
  446.0 2.3 copy.44
  448.4 0.9 slice_select_fusion
  449.3 0.6 dynamic-slice_reduce_fusion
  (30 shorter events, 0.2 us)
Async XLA Ops:
  0.6 2.3 copy-start.2
  2.9 1.5 copy-start.8
  2.9 1.5 copy-start.9
  2.9 1.6 copy-start.12
  2.9 1.8 copy-start.11
  2.9 1.8 copy-start.10
  3.0 1.9 copy-start.3
  4.0 2.3 copy-start.4
  4.0 6.2 %collective-permute-start = (bf16[408,1152]{1,0:T(8,128)(2,1)}, bf16[408,1152]{1,0:T(8,128)(2,1)}, u32[]{:S(2)}, u32[]{:S(2)}) collective-permute-start(bf16[408,1152]{1,0:T(8,128)(2,1)} %fusion.7), channel_id=1, source_target_pairs={{0,4},{1,5},{2,6},{3,7},{4,0},{5,1},{6,2},{7,3},{8,12},{9,13},{10,... | collective-permute-start | bytes 2820104 | tf_op jit(solution)/shard_map/ppermute | solution.py:66
  4.4 3.9 collective-permute-start.1
  9.1 2.7 copy-start.7
  436.1 3.1 copy-start.6
  436.1 3.6 copy-start.1
  439.8 3.1 copy-start.5
  439.8 5.1 %copy-start = (f32[272,1152]{1,0:T(8,128)S(1)}, f32[272,1152]{1,0:T(8,128)}, u32[]{:S(2)}) copy-start(f32[272,1152]{1,0:T(8,128)} %get-tuple-element.73) | copy-start | bytes 3760132

commit v6 on v5

--- a/solution.py
+++ b/solution.py
@@ -992,12 +992,14 @@
         n = self.n
         return 1 - n.c + 2 * (n.z // 2 if k else 1 - n.z // 2)
 
-    def route(self, k):
+    def route(self, h):
         n = self.n
-        early = self.target(k) < 2
-        one = jnp.where(early, n.py, n.px)
-        two = jnp.where(early, n.px, n.py)
-        return (one, (2 * one + n.c, n.z)), (two, (2 * two + n.c, n.z))
+        both = ((n.px, n.x_to), (n.py, n.y_to))
+        return both[h], both[1 - h]
+
+    def lanes(self, h):
+        cut = (self.s.cols // 2 + LANES - 1) // LANES * LANES
+        return pl.ds(0, cut) if h == 0 else pl.ds(cut, self.s.cols - cut)
 
     def block(self, k, p):
         rows = self.s.rows
@@ -1013,17 +1015,29 @@
             self.ship_ref.at[k], self.came.at[k], self.ps.at[k], self.pr.at[k], self.n.sib
         )
 
-    def pieces(self, k):
-        (one, to), _ = self.route(k)
+    def part(self, k, p, h):
+        rows = self.s.rows
+        return self.own.at[k, pl.ds(pl.multiple_of(p * rows, 16), rows), self.lanes(h)]
+
+    def pieces(self, k, h):
+        (one, to), _ = self.route(h)
         for i, p in enumerate((one, self.n.pd)):
             yield self.remote(
-                self.block(k, p), self.first_ref.at[k, i], self.fs.at[k, i], self.fr.at[k, i], to
+                self.part(k, p, h),
+                self.first_ref.at[k, i, :, self.lanes(h)],
+                self.fs.at[k, h, i],
+                self.fr.at[k, h, i],
+                to,
             )
 
-    def piece(self, k):
-        _, (two, to) = self.route(k)
+    def piece(self, k, h):
+        _, (two, to) = self.route(h)
         return self.remote(
-            self.block(k, two), self.second_ref.at[k], self.hs.at[k], self.hr.at[k], to
+            self.part(k, two, h),
+            self.second_ref.at[k, :, self.lanes(h)],
+            self.hs.at[k, h],
+            self.hr.at[k, h],
+            to,
         )
 
     def along(self, k):
@@ -1040,31 +1054,35 @@
         self.panel(k).wait_recv()
 
     def start(self, k):
-        for copy in self.pieces(k):
-            copy.start()
-
-    def add(self, k, p, other):
-        rows = self.s.rows
+        for h in range(2):
+            for copy in self.pieces(k, h):
+                copy.start()
+
+    def add(self, k, p, h, other):
+        rows, lanes = self.s.rows, self.lanes(h)
 
         def some(r):
             at = pl.ds(pl.multiple_of(p * rows + r.start, 16), r.size)
-            self.own[k, at, :] = to_low(
-                self.own[k, at, :].astype(f32) + other[r, :].astype(f32)
+            self.own[k, at, lanes] = to_low(
+                self.own[k, at, lanes].astype(f32) + other[r, lanes].astype(f32)
             )
 
         by_rows(rows, 16, some)
 
     def turn(self, k):
-        for copy in self.pieces(k):
-            copy.wait_recv()
-        _, (two, _) = self.route(k)
-        self.add(k, two, self.first_ref.at[k, 1])
-        self.piece(k).start()
-        self.add(k, self.n.p, self.first_ref.at[k, 0])
+        for h in range(2):
+            for copy in self.pieces(k, h):
+                copy.wait_recv()
+            _, (two, _) = self.route(h)
+            self.add(k, two, h, self.first_ref.at[k, 1])
+            self.piece(k, h).start()
+        for h in range(2):
+            self.add(k, self.n.p, h, self.first_ref.at[k, 0])
 
     def land(self, k):
-        self.piece(k).wait_recv()
-        self.add(k, self.n.p, self.second_ref.at[k])
+        for h in range(2):
+            self.piece(k, h).wait_recv()
+            self.add(k, self.n.p, h, self.second_ref.at[k])
 
     def send(self, k):
         @pl.when(self.target(k) != self.n.z)
@@ -1122,9 +1140,10 @@
         for k in range(2):
             if panels:
                 self.panel(k).wait_send()
-            for copy in self.pieces(k):
-                copy.wait_send()
-            self.piece(k).wait_send()
+            for h in range(2):
+                for copy in self.pieces(k, h):
+                    copy.wait_send()
+                self.piece(k, h).wait_send()
 
     def finish(self):
         for k in range(2):
@@ -1146,7 +1165,7 @@
 def scatter_sems():
     dma = pltpu.SemaphoreType.DMA
     return [
-        dma((2,)), dma((2,)), dma((2, 2)), dma((2, 2)), dma((2,)), dma((2,)),
+        dma((2,)), dma((2,)), dma((2, 2, 2)), dma((2, 2, 2)), dma((2, 2)), dma((2, 2)),
         dma((2,)), dma((4,)), dma, dma, dma, dma,
     ]
 

time: 450 us -> 438 us (0.973)
  Pallas kernels: 420 us -> 407 us
    pallas_call x1, Pallas kernels: 55.1 us -> 47.3 us  [attention_call(): pl.pallas_call(partial(attention_kernel, s), out_shape=[low(rows, s.wide)...]
where the time goes in v6:
time: 438 us; the launch traced here: 437 us
  Pallas kernels  407 us (93%)
  local copies, waits for them, and re-layouts  15.8 us (4%)
  other arithmetic  12.9 us (3%)
    pallas_call x1, Pallas kernels, forward_call(): pl.pallas_call(partial(forward_kernel, s), out_shape=out_shape, in_specs=...  185 us
    pallas_call x1, Pallas kernels, last_call(): pl.pallas_call(partial(last_kernel, s), out_shape=[high(s.rows, s.cols),...  102 us
    pallas_call x1, Pallas kernels, middle_call(): pl.pallas_call(partial(middle_kernel, s), out_shape=[low(2, s.rows, s.col...  72.4 us
    pallas_call x1, Pallas kernels, attention_call(): pl.pallas_call(partial(attention_kernel, s), out_shape=[low(rows, s.wide)...  47.3 us
  transfers between devices with their start and end apart: 2, of which 0 were waited for; matrix products, arithmetic and copies ran while one was open for 1% of the time, Pallas kernels for 0%

profile of v6, /device:TPU:0, one launch (start us, length us, event | category | flops | bytes accessed | tf_op | source)
XLA Modules:
  0.0 437.4 jit_solution(6728742675279442711)
XLA Ops:
  0.6 0.0 copy-start.2
  0.7 1.1 fusion.29
  1.7 1.1 fusion.15
  2.9 0.0 copy-start.8
  2.9 0.0 copy-start.9
  2.9 0.0 copy-start.12
  2.9 0.0 copy-start.11
  2.9 0.0 copy-start.10
  3.0 0.0 copy-start.3
  3.0 0.0 copy-done.2
  3.0 1.0 fusion.7
  4.0 0.5 collective-permute-start
  4.4 0.0 copy-done.8
  4.4 0.0 copy-done.9
  4.4 0.1 collective-permute-start.1
  4.6 0.0 copy-done.12
  4.6 0.1 add.83
  4.7 0.1 broadcast_bitcast_fusion
  4.7 0.0 copy-done.11
  4.8 0.0 copy-done.10
  4.9 1.4 copy.40.refs_4_
  6.3 1.4 copy.41.refs_5_
  7.7 0.6 pad.36.refs_3_
  8.3 0.0 collective-permute-done.1
  8.4 0.6 gather_fusion
  8.9 0.1 select_bitcast_fusion.1
  9.1 0.0 copy-start.7
  9.2 1.1 copy.42.refs_6_.refs_0_
  10.2 0.0 collective-permute-done
  10.2 1.6 broadcast_select_fusion.1
  11.8 0.1 fusion.25
  11.9 0.1 fusion.27
  12.0 0.1 fusion.26
  12.1 0.1 fusion.28
  12.1 0.9 pad_maximum_fusion.1.refs_1_
  13.0 0.9 pad_maximum_fusion.refs_0_
  13.9 1.0 fusion.9.refs_2_
  14.9 185.2 %forward.1 = (bf16[1088,4608]{1,0:T(8,128)(2,1)}, bf16[1088,4608]{1,0:T(8,128)(2,1)}, bf16[1088,4608]{1,0:T(8,128)(2,1)}, bf16[512,1088]{1,0:T(8,128)(2,1)}, bf1...) custom-call(bf16[272,1152]{1,0:T(8,128)(2,1)} %pad_maximum_fusion.re, ...), custom_call_target="tpu_custom_call" | custom-call | tf_op jit(solution)/shard_map/forward/pallas_call | solution.py:949
  200.1 0.9 reduce_max.9
  201.0 0.1 reshape.56
  201.0 0.6 pad.37.refs_11_
  201.7 72.4 %middle.1 = (bf16[2,272,1152]{2,1,0:T(8,128)(2,1)}, bf16[2,1088,1152]{2,1,0:T(8,128)(2,1)}, f32[512,1152]{1,0:T(8,128)}, bf16[512,1152]{1,0:T(8,128)(2,1)}, bf16...) custom-call(bf16[1088,4608]{1,0:T(8,128)(2,1)} %get-tuple-element.43.refs_0_, ...), custom_call_target="tpu_custom_call" | custom-call | tf_op jit(solution)/shard_map/middle/pallas_call | solution.py:1674
  274.1 47.3 %attention.1 = (bf16[512,1152]{1,0:T(8,128)(2,1)}, bf16[2,512,1152]{2,1,0:T(8,128)(2,1)}, bf16[2,272,1152]{2,1,0:T(8,128)(2,1)}, f32[272,1152]{1,0:T(8,128)}) custom-call(s32[1024,2]{1,0:T(8,128)} %copy.42.refs_6_.refs_0_, s32[1,512]{1,0:T(1,128)} %copy-done.7, f32[9,2,512]{2,1,0:T(2,128)} %get-tuple-element.55.refs_2_, ...), custom_call_target="tpu_custom_call" | custom-call | tf_op jit(solution)/shard_map/attention/pallas_call | solution.py:1463
  321.4 101.9 %last.1 = (f32[272,1152]{1,0:T(8,128)}, f32[272,1152]{1,0:T(8,128)}, bf16[2,256,1088]{2,1,0:T(8,128)(2,1)}, f32[16,1152]{1,0:T(8,128)}) custom-call(bf16[1088,4608]{1,0:T(8,128)(2,1)} %get-tuple-element.43.refs_0_, bf16[4,512,384]{2,1,0:T(8,128)(2,1)} %get-tuple-element.54.refs_1_, bf16[512,1152]{1,0:T(8,128)(2,1)} %get-tuple-element.61.refs_2_, ...), custom_call_target="tpu_custom_call" | custom-call | tf_op jit(solution)/shard_map/last/pallas_call | solution.py:1714
  423.4 1.4 slice_select_fusion.1
  424.8 0.8 slice.126
  425.6 0.8 slice.127
  426.4 0.5 divide_sqrt_fusion
  426.9 0.0 copy-done.1
  427.0 0.1 fusion.24
  427.0 0.0 copy-start.5
  427.1 0.0 copy-start
  427.1 2.8 copy.45
  429.8 0.1 broadcast_in_dim.29
  429.9 0.1 reshape.57
  430.0 0.1 concatenate.47
  430.1 0.1 dynamic_slice.37
  430.1 0.7 multiply_convert_fusion
  430.9 0.7 constant_dynamic-slice_fusion
  431.5 0.6 multiply_convert_fusion.1
  432.2 1.1 select_bitcast_fusion
  433.3 2.3 copy.44
  435.6 0.9 slice_select_fusion
  436.5 0.6 dynamic-slice_reduce_fusion
  (30 shorter events, 0.2 us)
Async XLA Ops:
  0.6 2.3 copy-start.2
  2.9 1.5 copy-start.8
  2.9 1.5 copy-start.9
  2.9 1.6 copy-start.12
  2.9 1.8 copy-start.11
  2.9 1.8 copy-start.10
  3.0 1.9 copy-start.3
  4.0 2.3 copy-start.4
  4.0 6.2 %collective-permute-start = (bf16[408,1152]{1,0:T(8,128)(2,1)}, bf16[408,1152]{1,0:T(8,128)(2,1)}, u32[]{:S(2)}, u32[]{:S(2)}) collective-permute-start(bf16[408,1152]{1,0:T(8,128)(2,1)} %fusion.7), channel_id=1, source_target_pairs={{0,4},{1,5},{2,6},{3,7},{4,0},{5,1},{6,2},{7,3},{8,12},{9,13},{10,... | collective-permute-start | bytes 2820104 | tf_op jit(solution)/shard_map/ppermute | solution.py:66
  4.4 3.9 collective-permute-start.1
  9.1 2.7 copy-start.7
  423.3 3.1 copy-start.6
  423.4 3.6 copy-start.1
  427.0 3.1 copy-start.5
  427.1 5.1 %copy-start = (f32[272,1152]{1,0:T(8,128)S(1)}, f32[272,1152]{1,0:T(8,128)}, u32[]{:S(2)}) copy-start(f32[272,1152]{1,0:T(8,128)} %get-tuple-element.73) | copy-start | bytes 3760132

commit v7 on v6

--- a/solution.py
+++ b/solution.py
@@ -1130,11 +1130,20 @@
 
                     by_rows(rows, 16, more)
 
-            pltpu.make_async_copy(self.total, self.out, self.eo).start()
+            self.kept().start()
             self.final().start()
 
+    def share(self, core):
+        rows = self.out.shape[0]
+        if rows == self.s.rows:
+            return self.total
+        return self.total.at[pl.ds(pl.multiple_of(core * rows, 8), rows)]
+
+    def kept(self):
+        return pltpu.make_async_copy(self.share(self.n.c), self.out, self.eo)
+
     def final(self):
-        return self.remote(self.total, self.out, self.es, self.er, self.n.sib)
+        return self.remote(self.share(1 - self.n.c), self.out, self.es, self.er, self.n.sib)
 
     def drain(self, panels=True):
         for k in range(2):
@@ -1154,7 +1163,7 @@
 
         @pl.when(self.mine())
         def _():
-            pltpu.make_async_copy(self.total, self.out, self.eo).wait()
+            self.kept().wait()
             self.final().wait_send()
 
         @pl.when(jnp.logical_not(self.mine()))
@@ -1714,7 +1723,7 @@
     return pl.pallas_call(
         partial(last_kernel, s),
         out_shape=[
-            high(s.rows, s.cols), high(s.rows, s.cols), low(*shape), high(16, s.wide),
+            high(s.rows // 2, s.cols), high(s.rows // 2, s.cols), low(*shape), high(16, s.wide),
         ],
         in_specs=[anywhere] * 9 + [local] * 3,
         out_specs=[anywhere, anywhere, anywhere, local],
@@ -1844,14 +1853,9 @@
     qkv_block, up_block, grad_input, small_sums = last_call(
         s, inputs.shape, wa, oz, dq, d_own, normed, attended, x, gres, up_sums, vec, sums, block_top
     )
-    rows_d = w_qkv.shape[0]
     cols_q, cols_d, cols_f = w_qkv.shape[1], w_out.shape[1], w_up.shape[1]
     ff = w_down.shape[0]
 
-    def own_rows(block):
-        return jnp.where(core == 0, block[:rows_d], block[rows_d:])
-
-    qkv_block, up_block = own_rows(qkv_block), own_rows(up_block)
     grad_qkv, grad_out = qkv_block[:, :cols_q], qkv_block[:, cols_q : cols_q + cols_d]
     grad_up = up_block[:, :cols_f]
     grad_down = jnp.where(core == 0, down_block[:, :ff], down_block[:, ff : 2 * ff]).T

time: 438 us -> 435 us (level)
  no operation moved by 1% of the time
where the time goes in v7:
time: 435 us
  Pallas kernels  406 us (93%)
  local copies, waits for them, and re-layouts  16.6 us (4%)
  other arithmetic  10.5 us (2%)
    pallas_call x1, Pallas kernels, forward_call(): pl.pallas_call(partial(forward_kernel, s), out_shape=out_shape, in_specs=...  185 us
    pallas_call x1, Pallas kernels, last_call(): pl.pallas_call(partial(last_kernel, s), out_shape=[high(s.rows // 2, s.co...  101 us
    pallas_call x1, Pallas kernels, middle_call(): pl.pallas_call(partial(middle_kernel, s), out_shape=[low(2, s.rows, s.col...  72.3 us
    pallas_call x1, Pallas kernels, attention_call(): pl.pallas_call(partial(attention_kernel, s), out_shape=[low(rows, s.wide)...  47.3 us
  transfers between devices with their start and end apart: 2, of which 0 were waited for; matrix products, arithmetic and copies ran while one was open for 1% of the time, Pallas kernels for 0%

profile of v7, /device:TPU:0, one launch (start us, length us, event | category | flops | bytes accessed | tf_op | source)
XLA Modules:
  0.0 434.7 jit_solution(4937747420710076923)
XLA Ops:
  0.6 0.0 copy-start.1
  0.7 1.1 fusion.28
  1.7 1.1 fusion.15
  2.9 0.0 copy-start.10
  2.9 0.0 copy-start.11
  2.9 0.0 copy-start.14
  2.9 0.0 copy-start.13
  2.9 0.0 copy-start.12
  2.9 0.0 copy-start.4
  3.0 0.0 copy-done.1
  3.0 1.0 fusion.7
  4.0 0.5 collective-permute-start
  4.4 0.0 copy-done.10
  4.4 0.0 copy-done.11
  4.4 0.1 collective-permute-start.1
  4.6 0.0 copy-done.14
  4.6 0.1 add.83
  4.7 0.1 broadcast_bitcast_fusion
  4.7 0.0 copy-done.13
  4.8 0.0 copy-done.12
  4.9 0.0 copy-done.4
  4.9 1.4 copy.40.refs_4_
  6.3 0.0 copy-done.5
  6.3 1.4 copy.41.refs_5_
  7.7 0.6 pad.36.refs_3_
  8.3 0.0 collective-permute-done.1
  8.3 0.6 gather_fusion
  8.9 0.1 select_bitcast_fusion.1
  9.1 0.0 copy-start.9
  9.2 1.0 copy.42.refs_6_.refs_0_
  10.2 0.0 collective-permute-done
  10.2 1.5 broadcast_select_fusion.1
  11.7 0.0 copy-done.9
  11.7 0.1 fusion.24
  11.9 0.1 fusion.26
  11.9 0.1 fusion.25
  12.1 0.1 fusion.27
  12.1 0.9 pad_maximum_fusion.1.refs_1_
  13.0 0.9 pad_maximum_fusion.refs_0_
  13.9 1.0 fusion.9.refs_2_
  14.9 185.2 %forward.1 = (bf16[1088,4608]{1,0:T(8,128)(2,1)}, bf16[1088,4608]{1,0:T(8,128)(2,1)}, bf16[1088,4608]{1,0:T(8,128)(2,1)}, bf16[512,1088]{1,0:T(8,128)(2,1)}, bf1...) custom-call(bf16[272,1152]{1,0:T(8,128)(2,1)} %pad_maximum_fusion.re, ...), custom_call_target="tpu_custom_call" | custom-call | tf_op jit(solution)/shard_map/forward/pallas_call | solution.py:949
  200.0 0.9 reduce_max.9
  200.9 0.1 reshape.56
  201.0 0.6 pad.37.refs_11_
  201.6 72.3 %middle.1 = (bf16[2,272,1152]{2,1,0:T(8,128)(2,1)}, bf16[2,1088,1152]{2,1,0:T(8,128)(2,1)}, f32[512,1152]{1,0:T(8,128)}, bf16[512,1152]{1,0:T(8,128)(2,1)}, bf16...) custom-call(bf16[1088,4608]{1,0:T(8,128)(2,1)} %get-tuple-element.43.refs_0_, ...), custom_call_target="tpu_custom_call" | custom-call | tf_op jit(solution)/shard_map/middle/pallas_call | solution.py:1683
  273.9 47.3 %attention.1 = (bf16[512,1152]{1,0:T(8,128)(2,1)}, bf16[2,512,1152]{2,1,0:T(8,128)(2,1)}, bf16[2,272,1152]{2,1,0:T(8,128)(2,1)}, f32[272,1152]{1,0:T(8,128)}) custom-call(s32[1024,2]{1,0:T(8,128)} %copy.42.refs_6_.refs_0_, s32[1,512]{1,0:T(1,128)} %copy-done.9, f32[9,2,512]{2,1,0:T(2,128)} %get-tuple-element.55.refs_2_, ...), custom_call_target="tpu_custom_call" | custom-call | tf_op jit(solution)/shard_map/attention/pallas_call | solution.py:1472
  321.2 101.0 %last.1 = (f32[136,1152]{1,0:T(8,128)}, f32[136,1152]{1,0:T(8,128)}, bf16[2,256,1088]{2,1,0:T(8,128)(2,1)}, f32[16,1152]{1,0:T(8,128)}) custom-call(bf16[1088,4608]{1,0:T(8,128)(2,1)} %get-tuple-element.43.refs_0_, bf16[4,512,384]{2,1,0:T(8,128)(2,1)} %get-tuple-element.54.refs_1_, bf16[512,1152]{1,0:T(8,128)(2,1)} %get-tuple-element.61.refs_2_, ...), custom_call_target="tpu_custom_call" | custom-call | tf_op jit(solution)/shard_map/last/pallas_call | solution.py:1723
  422.2 1.9 slice.85
  424.2 1.7 slice.86
  425.9 0.0 copy-done.8
  425.9 0.5 divide_sqrt_fusion
  426.4 0.0 copy-start.6
  426.5 1.7 copy.45
  428.2 0.1 broadcast_in_dim.29
  428.2 0.1 reshape.57
  428.3 0.1 concatenate.47
  428.4 0.1 dynamic_slice.37
  428.5 0.7 multiply_convert_fusion
  429.2 0.7 constant_dynamic-slice_fusion
  429.9 0.6 multiply_convert_fusion.1
  430.5 1.1 select_bitcast_fusion
  431.6 1.4 copy.44
  433.0 0.6 dynamic-slice_reduce_fusion
  433.6 0.8 copy.49
  (32 shorter events, 0.2 us)
Async XLA Ops:
  0.6 2.3 copy-start.1
  2.9 1.5 copy-start.10
  2.9 1.5 copy-start.11
  2.9 1.6 copy-start.14
  2.9 1.8 copy-start.13
  2.9 1.8 copy-start.12
  2.9 1.9 copy-start.4
  4.0 2.3 copy-start.5
  4.0 6.2 %collective-permute-start = (bf16[408,1152]{1,0:T(8,128)(2,1)}, bf16[408,1152]{1,0:T(8,128)(2,1)}, u32[]{:S(2)}, u32[]{:S(2)}) collective-permute-start(bf16[408,1152]{1,0:T(8,128)(2,1)} %fusion.7), channel_id=1, source_target_pairs={{0,4},{1,5},{2,6},{3,7},{4,0},{5,1},{6,2},{7,3},{8,12},{9,13},{10,... | collective-permute-start | bytes 2820104 | tf_op jit(solution)/shard_map/ppermute | solution.py:66
  4.4 3.9 collective-permute-start.1
  9.1 2.7 copy-start.9
  422.2 3.7 copy-start.8
  422.2 4.2 copy-start.3
  426.4 2.0 copy-start.6
  426.5 4.1 copy-start
  428.5 3.2 copy-start.2
  431.6 2.0 copy-start.7
